TPU v7x, 32 devices: a whole 2x2x4 slice. The times are simulated.
32 devices in a mesh: grp: 8 (over z, y), blk: 4 (over x, core).
Axes of the slice: x: 2, y: 2, z: 4, core: 2. Of those that a mesh axis runs over, the one named last changes fastest.
Arguments:
- images: bfloat16 [16, 1024, 1152], P('grp', 'blk'), may hold values from -6 to 6
- cotangent: bfloat16 [16, 1024, 1152], P('grp', 'blk'), may hold values from -6 to 6
- timestep: int32 [16], P('grp'), may hold values from 0 to 999
- input_weight: bfloat16 [1152, 3456], P('blk'), may hold values from -0.1875 to 0.1875
- input_bias: float32 [2304], replicated, may hold values from -3 to 3
- output_weight: bfloat16 [1152, 1152], P('blk'), may hold values from -0.75 to 0.75
- output_bias: float32 [1152], replicated, may hold values from -3 to 3
- expand_weight: bfloat16 [1152, 4608], P('blk'), may hold values from -0.1875 to 0.1875
- expand_bias: float32 [4608], replicated, may hold values from -3 to 3
- shrink_weight: bfloat16 [4608, 1152], P('blk'), may hold values from -0.09375 to 0.09375
- shrink_bias: float32 [1152], replicated, may hold values from -3 to 3
- modulate_weight: bfloat16 [1152, 6912], P('blk'), may hold values from -0.1875 to 0.1875
- modulate_bias: float32 [6912], replicated, may hold values from -4 to 4
- position_table: float32 [3969, 16], replicated, may hold values from -4 to 4
Outputs:
- result: bfloat16 [16, 1024, 1152], P('grp', 'blk')
- grad_images: bfloat16 [16, 1024, 1152], P('grp', 'blk')
- grad_input_weight: float32 [1152, 3456], P('blk')
- grad_input_bias: float32 [2304], P('blk')
- grad_output_weight: float32 [1152, 1152], P('blk')
- grad_output_bias: float32 [1152], P('blk')
- grad_expand_weight: float32 [1152, 4608], P('blk')
- grad_expand_bias: float32 [4608], P('blk')
- grad_shrink_weight: float32 [4608, 1152], P('blk')
- grad_shrink_bias: float32 [1152], P('blk')
- grad_modulate_weight: float32 [1152, 6912], P('blk')
- grad_modulate_bias: float32 [6912], P('blk')
- grad_position_table: float32 [3969, 16], replicated
All inputs are finite; a program needn't handle non-finite values.
Results may differ from a plain program's by a relative error of at most 0.023.
Values may be sent and summed in bfloat16 or wider, within the bound.
No kernel may reach another device: no remote copies, remote signals or barrier semaphores. Data moves between devices by JAX's collectives and lax.ppermute only.
A program may use at most 384 MiB of HBM per device.

v0:
```python
import math

import jax
import jax.numpy as jnp
from jax import lax
from jax.sharding import PartitionSpec as P

GRID = 32


HIGHEST = lax.Precision.HIGHEST


def embedding(step_values, width):
    half_width = width // 2
    frequency = jnp.exp(-math.log(10000.0) * jnp.arange(half_width, dtype=jnp.float32) / half_width)
    angles = step_values.astype(jnp.float32)[:, None] * frequency[None, :]
    return jnp.concatenate([jnp.cos(angles), jnp.sin(angles)], axis=-1)


def norm_rows(values):
    centered = values - jnp.mean(values, axis=-1, keepdims=True)
    variance = jnp.mean(centered * centered, axis=-1, keepdims=True)
    inverse = lax.rsqrt(variance + 1e-06)
    return (centered * inverse, inverse)


def norm_back(grad_normed, normed, inverse):
    first_mean = jnp.mean(grad_normed, axis=-1, keepdims=True)
    second_mean = jnp.mean(grad_normed * normed, axis=-1, keepdims=True)
    return inverse * (grad_normed - first_mean - normed * second_mean)


def column_table(grid_side):
    across = jnp.arange(grid_side, dtype=jnp.int32)
    offsets = jnp.arange(2 * grid_side - 1, dtype=jnp.int32)
    return (
        across[:, None, None] - across[None, :, None] + grid_side - 1 == offsets[None, None, :]
    ).astype(jnp.float32)


def row_table(query_lines, key_lines, query_first, grid_side):
    offsets = jnp.arange(2 * grid_side - 1, dtype=jnp.int32)
    query_at = query_first + jnp.arange(query_lines, dtype=jnp.int32)
    key_at = jnp.arange(key_lines, dtype=jnp.int32)
    return (
        query_at[:, None, None] - key_at[None, :, None] + grid_side - 1 == offsets[None, None, :]
    ).astype(jnp.float32)


def position_bias(table_part, query_start, query_count, key_count, grid_side):
    heads_here = table_part.shape[1]
    span = 2 * grid_side - 1
    grid_table = table_part.reshape(span, span, heads_here)
    rows_pick = row_table(
        query_count // grid_side, key_count // grid_side, query_start // grid_side, grid_side
    )
    by_rows = jnp.einsum("ije,edh->hijd", rows_pick, grid_table, precision=HIGHEST)
    expanded_bias = jnp.einsum(
        "hijd,xyd->hixjy", by_rows, column_table(grid_side), precision=HIGHEST
    )
    return expanded_bias.reshape(heads_here, query_count, key_count)


def position_grad(grad_scores, query_start, grid_side):
    image_count, heads_here, query_count, key_count = grad_scores.shape
    span = 2 * grid_side - 1
    blocked = grad_scores.reshape(
        image_count,
        heads_here,
        query_count // grid_side,
        grid_side,
        key_count // grid_side,
        grid_side,
    )
    by_cols = jnp.einsum(
        "ahixjy,xyd->ahijd",
        blocked,
        column_table(grid_side).astype(jnp.bfloat16),
        preferred_element_type=jnp.float32,
    )
    rows_pick = row_table(
        query_count // grid_side, key_count // grid_side, query_start // grid_side, grid_side
    )
    summed = jnp.einsum("ahijd,ije->hed", by_cols, rows_pick, precision=HIGHEST)
    return summed.reshape(heads_here, span * span).T


def score_block(query_use, key_use, table_part, query_start, grid_side):
    head_dim = query_use.shape[3]
    scores = jnp.einsum(
        "aqhd,akhd->ahqk", query_use, key_use, preferred_element_type=jnp.float32
    ) * head_dim ** (-0.5)
    return (
        scores
        + position_bias(table_part, query_start, query_use.shape[1], key_use.shape[1], grid_side)[
            None
        ]
    )


def attend(query_use, key_use, value_use, table_part, query_start, grid_side):
    scores = score_block(query_use, key_use, table_part, query_start, grid_side)
    largest = jnp.max(scores, axis=-1, keepdims=True)
    exponent = jnp.exp(scores - largest)
    denominator = jnp.sum(exponent, axis=-1, keepdims=True)
    softmax_weights = (exponent / denominator).astype(jnp.bfloat16)
    attended = jnp.einsum(
        "ahqk,akhd->aqhd", softmax_weights, value_use, preferred_element_type=jnp.float32
    )
    return (attended.astype(jnp.bfloat16), largest + jnp.log(denominator))


def attend_back(
    query_use, key_use, value_use, grad_attended, log_total, table_part, query_start, grid_side
):
    head_dim = query_use.shape[3]
    scores = score_block(query_use, key_use, table_part, query_start, grid_side)
    softmax_weights = jnp.exp(scores - log_total)
    grad_values = jnp.einsum(
        "ahqk,aqhd->akhd",
        softmax_weights.astype(jnp.bfloat16),
        grad_attended,
        preferred_element_type=jnp.float32,
    )
    grad_weights = jnp.einsum(
        "aqhd,akhd->ahqk", grad_attended, value_use, preferred_element_type=jnp.float32
    )
    row_dots = jnp.sum(grad_weights * softmax_weights, axis=-1, keepdims=True)
    grad_scores = (softmax_weights * (grad_weights - row_dots)).astype(jnp.bfloat16)
    grad_queries = jnp.einsum(
        "ahqk,akhd->aqhd", grad_scores, key_use, preferred_element_type=jnp.float32
    ) * head_dim ** (-0.5)
    grad_keys = jnp.einsum(
        "ahqk,aqhd->akhd", grad_scores, query_use, preferred_element_type=jnp.float32
    ) * head_dim ** (-0.5)
    return (
        grad_queries,
        grad_keys,
        grad_values,
        position_grad(grad_scores, query_start, grid_side),
    )


def shards(
    images,
    cotangent,
    timestep,
    input_weight,
    input_bias,
    output_weight,
    output_bias,
    expand_weight,
    expand_bias,
    shrink_weight,
    shrink_bias,
    modulate_weight,
    modulate_bias,
    position_table,
):
    image_count, token_count, model_width = images.shape
    heads_all = position_table.shape[1]
    head_dim = model_width // heads_all
    grid_side = GRID
    cycle_place = lax.axis_index("blk")
    own_rows = modulate_weight.shape[0]
    full_input, full_output, full_expand, full_shrink = (
        lax.all_gather(input_weight, "blk", axis=0, tiled=True),
        lax.all_gather(output_weight, "blk", axis=0, tiled=True),
        lax.all_gather(expand_weight, "blk", axis=0, tiled=True),
        lax.all_gather(shrink_weight, "blk", axis=0, tiled=True),
    )
    condition = jax.nn.silu(embedding(timestep, model_width)).astype(jnp.bfloat16)
    condition_own = lax.dynamic_slice_in_dim(condition, cycle_place * own_rows, own_rows, 1)
    modulation_part = jnp.dot(condition_own, modulate_weight, preferred_element_type=jnp.float32)
    modulation = lax.psum(modulation_part, "blk") + modulate_bias
    shift_one, scale_one, gate_one, shift_two, scale_two, gate_two = [
        member[:, None, :] for member in jnp.split(modulation, 6, axis=-1)
    ]
    tokens = images.astype(jnp.float32)
    normed_one, inverse_one = norm_rows(tokens)
    hidden_one = (normed_one * (1.0 + scale_one) + shift_one).astype(jnp.bfloat16)
    projected = jnp.einsum(
        "atd,de->ate", hidden_one, full_input, preferred_element_type=jnp.float32
    )
    query_flat = (projected[..., :model_width] + input_bias[:model_width]).astype(jnp.bfloat16)
    key_flat = projected[..., model_width : 2 * model_width].astype(jnp.bfloat16)
    value_flat = (projected[..., 2 * model_width :] + input_bias[model_width:]).astype(jnp.bfloat16)
    key_all, value_all = (
        lax.all_gather(key_flat, "blk", axis=1, tiled=True),
        lax.all_gather(value_flat, "blk", axis=1, tiled=True),
    )
    query_start = cycle_place * token_count
    query_use = query_flat.reshape(image_count, token_count, heads_all, head_dim)
    key_use = key_all.reshape(image_count, -1, heads_all, head_dim)
    value_use = value_all.reshape(image_count, -1, heads_all, head_dim)
    attended, log_total = attend(
        query_use, key_use, value_use, position_table, query_start, grid_side
    )
    mixed_flat = attended.reshape(image_count, token_count, model_width)
    branch_one = (
        jnp.einsum("atd,de->ate", mixed_flat, full_output, preferred_element_type=jnp.float32)
        + output_bias
    )
    middle = tokens + gate_one * branch_one
    normed_two, inverse_two = norm_rows(middle)
    hidden_two = (normed_two * (1.0 + scale_two) + shift_two).astype(jnp.bfloat16)
    expanded = (
        jnp.einsum("atd,df->atf", hidden_two, full_expand, preferred_element_type=jnp.float32)
        + expand_bias
    )
    activated, gelu_back = jax.vjp(
        lambda inner_value: jax.nn.gelu(inner_value, approximate=True), expanded
    )
    activated_low = activated.astype(jnp.bfloat16)
    branch_two = (
        jnp.einsum("atf,fd->atd", activated_low, full_shrink, preferred_element_type=jnp.float32)
        + shrink_bias
    )
    result = (middle + gate_two * branch_two).astype(jnp.bfloat16)
    grad_out = cotangent.astype(jnp.float32)
    grad_branch_two = (gate_two * grad_out).astype(jnp.bfloat16)
    grad_gate_two = jnp.sum(grad_out * branch_two, axis=1)
    shrink_grad = jnp.einsum(
        "atf,atd->fd", activated_low, grad_branch_two, preferred_element_type=jnp.float32
    )
    shrink_bias_grad = jnp.sum(grad_branch_two.astype(jnp.float32), axis=(0, 1))
    grad_activated = jnp.einsum(
        "atd,fd->atf", grad_branch_two, full_shrink, preferred_element_type=jnp.float32
    )
    grad_expanded = gelu_back(grad_activated)[0].astype(jnp.bfloat16)
    expand_grad = jnp.einsum(
        "atd,atf->df", hidden_two, grad_expanded, preferred_element_type=jnp.float32
    )
    expand_bias_grad = jnp.sum(grad_expanded.astype(jnp.float32), axis=(0, 1))
    grad_hidden_two = jnp.einsum(
        "atf,df->atd", grad_expanded, full_expand, preferred_element_type=jnp.float32
    )
    grad_scale_two = jnp.sum(grad_hidden_two * normed_two, axis=1)
    grad_shift_two = jnp.sum(grad_hidden_two, axis=1)
    grad_middle = grad_out + norm_back(grad_hidden_two * (1.0 + scale_two), normed_two, inverse_two)
    grad_branch_one = (gate_one * grad_middle).astype(jnp.bfloat16)
    grad_gate_one = jnp.sum(grad_middle * branch_one, axis=1)
    output_grad = jnp.einsum(
        "atd,ate->de", mixed_flat, grad_branch_one, preferred_element_type=jnp.float32
    )
    output_bias_grad = jnp.sum(grad_branch_one.astype(jnp.float32), axis=(0, 1))
    grad_mixed = jnp.einsum(
        "ate,de->atd", grad_branch_one, full_output, preferred_element_type=jnp.float32
    ).astype(jnp.bfloat16)
    grad_queries, grad_keys, grad_values, table_grad = attend_back(
        query_use,
        key_use,
        value_use,
        grad_mixed.reshape(image_count, token_count, heads_all, head_dim),
        log_total,
        position_table,
        query_start,
        grid_side,
    )
    grad_query = grad_queries.reshape(image_count, token_count, model_width).astype(jnp.bfloat16)
    key_sum, value_sum = (
        lax.psum_scatter(
            grad_keys.reshape(image_count, -1, model_width), "blk", scatter_dimension=1, tiled=True
        ),
        lax.psum_scatter(
            grad_values.reshape(image_count, -1, model_width),
            "blk",
            scatter_dimension=1,
            tiled=True,
        ),
    )
    grad_key = key_sum.astype(jnp.bfloat16)
    grad_value = value_sum.astype(jnp.bfloat16)
    grad_projected = jnp.concatenate([grad_query, grad_key, grad_value], axis=-1)
    input_grad = jnp.einsum(
        "atd,ate->de", hidden_one, grad_projected, preferred_element_type=jnp.float32
    )
    input_bias_grad = jnp.concatenate(
        [
            jnp.sum(grad_query.astype(jnp.float32), axis=(0, 1)),
            jnp.sum(grad_value.astype(jnp.float32), axis=(0, 1)),
        ]
    )
    grad_hidden_one = jnp.einsum(
        "ate,de->atd", grad_projected, full_input, preferred_element_type=jnp.float32
    )
    grad_scale_one = jnp.sum(grad_hidden_one * normed_one, axis=1)
    grad_shift_one = jnp.sum(grad_hidden_one, axis=1)
    grad_images = (
        grad_middle + norm_back(grad_hidden_one * (1.0 + scale_one), normed_one, inverse_one)
    ).astype(jnp.bfloat16)
    grad_modulation = jnp.concatenate(
        [
            grad_shift_one,
            grad_scale_one,
            grad_gate_one,
            grad_shift_two,
            grad_scale_two,
            grad_gate_two,
        ],
        axis=-1,
    )
    gathered_grads, gathered_conditions = (
        lax.all_gather(
            grad_modulation.astype(jnp.bfloat16), ("grp", "blk"), axis=0, tiled=True
        ).astype(grad_modulation.dtype),
        lax.all_gather(
            condition.astype(jnp.float32).astype(jnp.bfloat16), ("grp", "blk"), axis=0, tiled=True
        ).astype(jnp.float32),
    )
    conditions_own = lax.dynamic_slice_in_dim(
        gathered_conditions, cycle_place * own_rows, own_rows, 1
    )
    modulate_grad = jnp.dot(conditions_own.T, gathered_grads, precision=HIGHEST)
    bias_width = gathered_grads.shape[1] // lax.axis_size("blk")
    modulate_bias_grad = lax.dynamic_slice_in_dim(
        jnp.sum(gathered_grads, axis=0), cycle_place * bias_width, bias_width, 0
    )
    (
        share_input,
        share_input_bias,
        share_output,
        share_output_bias,
        share_expand,
        share_expand_bias,
        share_shrink,
        share_shrink_bias,
    ) = (
        lax.psum_scatter(
            input_grad.astype(jnp.bfloat16), "blk", scatter_dimension=0, tiled=True
        ).astype(jnp.float32),
        lax.psum_scatter(
            input_bias_grad.astype(jnp.bfloat16), "blk", scatter_dimension=0, tiled=True
        ).astype(jnp.float32),
        lax.psum_scatter(
            output_grad.astype(jnp.bfloat16), "blk", scatter_dimension=0, tiled=True
        ).astype(jnp.float32),
        lax.psum_scatter(
            output_bias_grad.astype(jnp.bfloat16), "blk", scatter_dimension=0, tiled=True
        ).astype(jnp.float32),
        lax.psum_scatter(
            expand_grad.astype(jnp.bfloat16), "blk", scatter_dimension=0, tiled=True
        ).astype(jnp.float32),
        lax.psum_scatter(
            expand_bias_grad.astype(jnp.bfloat16), "blk", scatter_dimension=0, tiled=True
        ).astype(jnp.float32),
        lax.psum_scatter(
            shrink_grad.astype(jnp.bfloat16), "blk", scatter_dimension=0, tiled=True
        ).astype(jnp.float32),
        lax.psum_scatter(
            shrink_bias_grad.astype(jnp.bfloat16), "blk", scatter_dimension=0, tiled=True
        ).astype(jnp.float32),
    )
    (
        total_input,
        total_input_bias,
        total_output,
        total_output_bias,
        total_expand,
        total_expand_bias,
        total_shrink,
        total_shrink_bias,
    ) = (
        lax.psum(share_input.astype(jnp.bfloat16), "grp").astype(jnp.float32),
        lax.psum(share_input_bias.astype(jnp.bfloat16), "grp").astype(jnp.float32),
        lax.psum(share_output.astype(jnp.bfloat16), "grp").astype(jnp.float32),
        lax.psum(share_output_bias.astype(jnp.bfloat16), "grp").astype(jnp.float32),
        lax.psum(share_expand.astype(jnp.bfloat16), "grp").astype(jnp.float32),
        lax.psum(share_expand_bias.astype(jnp.bfloat16), "grp").astype(jnp.float32),
        lax.psum(share_shrink.astype(jnp.bfloat16), "grp").astype(jnp.float32),
        lax.psum(share_shrink_bias.astype(jnp.bfloat16), "grp").astype(jnp.float32),
    )
    table_total = lax.psum(table_grad, ("grp", "blk"))
    return (
        result,
        grad_images,
        total_input,
        total_input_bias,
        total_output,
        total_output_bias,
        total_expand,
        total_expand_bias,
        total_shrink,
        total_shrink_bias,
        modulate_grad,
        modulate_bias_grad,
        table_total,
    )


def solution(mesh):
    return jax.shard_map(
        shards,
        mesh=mesh,
        in_specs=(
            P("grp", "blk", None),
            P("grp", "blk", None),
            P("grp"),
            P("blk", None),
            P(),
            P("blk", None),
            P(),
            P("blk", None),
            P(),
            P("blk", None),
            P(),
            P("blk", None),
            P(),
            P(),
        ),
        out_specs=(
            P("grp", "blk", None),
            P("grp", "blk", None),
            P("blk", None),
            P("blk"),
            P("blk", None),
            P("blk"),
            P("blk", None),
            P("blk"),
            P("blk", None),
            P("blk"),
            P("blk", None),
            P("blk"),
            P(),
        ),
        check_vma=False,
    )
```

profile of v0, /device:TPU:16, one launch (start us, length us, event | category | flops | bytes accessed | tf_op | source)
XLA Modules:
  0.0 1308.5 jit_solution(1878097401501681069)
XLA Ops:
  26.4 40.3 %all-gather.9.cloned.1.call-done = bf16[1152,3456]{1,0:T(8,128)(2,1)} async-done(((bf16[288,3456]{1,0:T(8,128)(2,1)}), bf16[1152,3456]{1,0:T(8,128)(2,1)}) %all-gather.9.cloned.1.call-update) | async-done | bytes 7962640 | tf_op jit(solution)/shard_map/all_gather | solution.py:168
  86.2 31.4 %convolution_bitcast_fusion = f32[16,8,32,32,32]{3,4,1,0,2:T(8,128)} fusion(f32[8,32,63,16]{2,1,0,3:T(8,128)S(1)} %fusion.62, s32[32,32]{1,0:T(8,128)S(1)} %subtract_add_fusion), kind=kOutput, calls=%fused_computation.8 | convolution fusion | flops 3170958336 | bytes 17813504 | tf_op jit(solution)/shard_map/hijd,xyd->hixjy/dot_general | solution.py:59
  117.5 61.7 %copy.57 = f32[16,8,32,32,32]{4,3,2,1,0:T(8,128)} copy(f32[16,8,32,32,32]{3,4,1,0,2:T(8,128)} %convolution_bitcast_fusion) | data formatting | bytes 33554432 | tf_op jit(solution)/shard_map/hijd,xyd->hixjy/transpose | solution.py:59
  179.3 51.8 %add.237 = f32[16,256,1024]{2,1,0:T(8,128)} reshape(f32[16,8,32,32,32]{4,3,2,1,0:T(8,128)} %copy.57) | data formatting | bytes 33554432 | tf_op jit(solution)/shard_map/add | solution.py:95
  245.3 19.8 %fusion.89 = (f32[2,16,256]{2,1,0:T(8,128)S(1)}, f32[2,16,256,1024]{3,2,1,0:T(8,128)}) fusion(f32[16,256,1024]{2,1,0:T(8,128)} %add.237, bf16[2,256,16,72]{1,3,2,0:T(8,128)(2,1)S(1)} %bitcast.137, bf16[2,1024,16,72]{1,3,2,0:T(8,128)(2,1)} %bitcast.129), kind=kOutput, calls=%fused_computation.147 | convolution fusion | flops 1233117184 | bytes 56262656 | tf_op jit(solution)/shard_map/aqhd,akhd->ahqk/dot_general | solution.py:91
  265.1 16.2 %fusion = f32[2,16,256]{2,1,0:T(8,128)S(1)} fusion(f32[2,16,256,1024]{3,2,1,0:T(8,128)} %get-tuple-element.58, f32[2,16,256]{2,1,0:T(8,128)S(1)} %get-tuple-element.57), kind=kLoop, calls=%fused_computation.6 | loop fusion | flops 16769024 | bytes 33619968 | tf_op jit(solution)/shard_map/reduce_sum | solution.py:106
  281.3 16.6 %fusion.56 = bf16[2,16,72,256]{3,2,1,0:T(8,128)(2,1)} fusion(bf16[2,1024,16,72]{1,3,2,0:T(8,128)(2,1)} %bitcast.133, f32[2,16,256,1024]{3,2,1,0:T(8,128)} %get-tuple-element.58, f32[2,16,256]{2,1,0:T(8,128)S(1)} %fusion, f32[2,16,256]{2,1,0:T(8,128)S(1)} %get-tuple-element.57), kind=kOutput, calls=%fused_computation.91 | convolution fusion | flops 1233715200 | bytes 39518208 | tf_op jit(solution)/shard_map/ahqk,akhd->aqhd/dot_general | solution.py:108
  328.0 16.4 %fusion.91 = (bf16[4608]{0:T(1024)(128)(2,1)}, bf16[2,256,4608]{2,1,0:T(8,128)(2,1)S(1)}) fusion(f32[2,256,4608]{2,1,0:T(8,128)} %fusion.15, f32[4608]{0:T(1024)} %param.22, bf16[4608,1152]{1,0:T(8,128)(2,1)} %all-gather.19.cloned.1.call-done, bf16[2,256,1152]{2,1,0:T(8,128)(2,1)S(1)} %copy-done.20, f32[2,1152]{1,0:T(2,128)} %get-tuple-element.47), kind=kOutput, calls=%fused_computation.149 | convolution fusion | flops 5489487360 | bytes 25989120 | tf_op jit(solution)/shard_map/atd,fd->atf/dot_general | solution.py:228
  357.5 15.0 %fusion.52 = (bf16[2,1152]{1,0:T(2,128)(2,1)}, bf16[2,256,1152]{2,1,0:T(8,128)(2,1)}, bf16[2,1152]{1,0:T(2,128)(2,1)}, f32[2,256,1152]{2,1,0:T(8,128)S(1)}) fusion(bf16[2,256,1152]{2,1,0:T(8,128)(2,1)S(1)} %copy-done.20, f32[2,256,1152]{2,1,0:T(8,128)S(1)} %get-tuple-element.40, f32[2,1152]{1,0:T(2,128)S(1)} %copy-done.40, ...), kind=kOutput, calls=%fused_computation.72 | convolution fusion | flops 5469433856 | bytes 31909376 | tf_op jit(solution)/shard_map/atf,fd->atd/dot_general | solution.py:217
  378.2 24.3 %multiply_reduce_fusion = (f32[2,16,256]{2,1,0:T(8,128)S(1)}, f32[2,16,256,1024]{3,2,1,0:T(8,128)}) fusion(f32[2,16,256,1024]{3,2,1,0:T(8,128)} %get-tuple-element.58, f32[2,16,256]{2,1,0:T(8,128)S(1)} %copy-done.15, bf16[2,256,16,72]{1,3,2,0:T(8,128)(2,1)S(1)} %bitcast.135, bf16[2,1024,16,72]{1,3,2,0:T(8,128)(2,1)} %bitcast.134), kind=kOutput, calls=%fused_computation.1 | convolution fusion | flops 1233117184 | bytes 73072640 | tf_op jit(solution)/shard_map/aqhd,akhd->ahqk/dot_general | solution.py:126
  402.4 27.8 %multiply_convert_fusion = bf16[2,16,256,1024]{3,2,1,0:T(8,128)(2,1)} fusion(f32[2,16,256,1024]{3,2,1,0:T(8,128)} %get-tuple-element.62, f32[2,16,256,1024]{3,2,1,0:T(8,128)} %get-tuple-element.58, f32[2,16,256]{2,1,0:T(8,128)S(1)} %get-tuple-element.61, f32[2,16,256]{2,1,0:T(8,128)S(1)} %copy-done.15), kind=kLoop, calls=%fused_computation | loop fusion | flops 33554432 | bytes 83951616 | tf_op jit(solution)/shard_map/convert_element_type | solution.py:130
  452.4 20.4 %fusion.4 = f32[2,16,72,1024]{3,2,1,0:T(8,128)} fusion(bf16[2,256,16,72]{1,3,2,0:T(8,128)(2,1)S(1)} %bitcast.136, f32[2,16,256,1024]{3,2,1,0:T(8,128)} %get-tuple-element.58, f32[2,16,256]{2,1,0:T(8,128)S(1)} %copy-done.15), kind=kOutput, calls=%fused_computation.14 | convolution fusion | flops 1224736768 | bytes 44204032 | tf_op jit(solution)/shard_map/ahqk,aqhd->akhd/dot_general | solution.py:120
  532.8 79.2 %reduce-scatter.9.cloned.1.call-done = f32[2,256,1152]{2,1,0:T(8,128)} async-done(((f32[2,1024,1152]{2,1,0:T(8,128)}), f32[2,256,1152]{2,1,0:T(8,128)}) %reduce-scatter.9.cloned.1.call-update) | async-done | bytes 2359312 | tf_op jit(solution)/shard_map/reduce_scatter | solution.py:266
  622.4 27.6 %reduce-scatter.13.cloned.1.call-done = bf16[288,1152]{1,0:T(8,128)(2,1)} async-done(((bf16[1152,1152]{1,0:T(8,128)(2,1)}), bf16[288,1152]{1,0:T(8,128)(2,1)}) %reduce-scatter.13.cloned.1.call-update) | async-done | bytes 663568 | tf_op jit(solution)/shard_map/reduce_scatter | solution.py:336
  650.0 88.8 %reduce-scatter.15.cloned.1.call-done = bf16[288,4608]{1,0:T(8,128)(2,1)} async-done(((bf16[1152,4608]{1,0:T(8,128)(2,1)}), bf16[288,4608]{1,0:T(8,128)(2,1)}) %reduce-scatter.15.cloned.1.call-update) | async-done | bytes 2654224 | tf_op jit(solution)/shard_map/reduce_scatter | solution.py:342
  738.8 89.0 %reduce-scatter.17.cloned.1.call-done = bf16[1152,1152]{1,0:T(8,128)(2,1)} async-done(((bf16[4608,1152]{1,0:T(8,128)(2,1)}), bf16[1152,1152]{1,0:T(8,128)(2,1)}) %reduce-scatter.17.cloned.1.call-update) | async-done | bytes 2654224 | tf_op jit(solution)/shard_map/reduce_scatter | solution.py:348
  827.8 72.5 %reduce-scatter.11.cloned.1.call-done = bf16[288,3456]{1,0:T(8,128)(2,1)} async-done(((bf16[1152,3456]{1,0:T(8,128)(2,1)}), bf16[288,3456]{1,0:T(8,128)(2,1)}) %reduce-scatter.11.cloned.1.call-update) | async-done | bytes 1990672 | tf_op jit(solution)/shard_map/reduce_scatter | solution.py:330
  901.1 34.0 %all-gather = bf16[32,2,1152]{2,1,0:T(2,128)(2,1)S(1)} all-gather(bf16[1,2,1152]{2,1,0:T(2,128)(2,1)S(1)} %fusion.112), channel_id=1, replica_groups=mesh['grp'=8,'blk'=4] {'grp','blk'}, dimensions={0}, use_global_device_ids=true | all-gather | bytes 152064 | tf_op jit(solution)/shard_map/all_gather | solution.py:308
  939.3 77.2 %reshape.190 = bf16[2,16,8,32,32,32]{5,4,3,2,1,0:T(8,128)(2,1)} reshape(bf16[2,16,256,1024]{3,2,1,0:T(8,128)(2,1)} %multiply_convert_fusion) | data formatting | bytes 33554432 | tf_op jit(solution)/shard_map/reshape | solution.py:68
  1016.4 25.2 %bitcast_reduce_fusion = f32[16,8,32,63]{3,2,1,0:T(8,128)S(1)} fusion(bf16[2,16,8,32,32,32]{5,4,3,2,1,0:T(8,128)(2,1)} %reshape.190, s32[32,32]{1,0:T(8,128)S(1)} %copy-done.29), kind=kOutput, calls=%fused_computation.43 | convolution fusion | flops 1057416192 | bytes 17813504 | tf_op jit(solution)/shard_map/ahixjy,xyd->ahijd/dot_general | solution.py:76
  1054.5 38.0 %all-gather.1 = bf16[32,2,6912]{2,1,0:T(2,128)(2,1)S(1)} all-gather(bf16[1,2,6912]{2,1,0:T(2,128)(2,1)S(1)} %bitcast.143), channel_id=1, replica_groups=mesh['grp'=8,'blk'=4] {'grp','blk'}, dimensions={0}, use_global_device_ids=true | all-gather | bytes 912384 | tf_op jit(solution)/shard_map/all_gather | solution.py:305
  1107.2 26.3 %all-reduce.4 = (bf16[576]{0:T(1024)(128)(2,1)S(1)}, bf16[288]{0:T(512)(128)(2,1)S(1)}, bf16[1152]{0:T(1024)(128)(2,1)S(1)}, bf16[288]{0:T(512)(128)(2,1)S(1)}) all-reduce(bf16[576]{0:T(1024)(128)(2,1)S(1)} %dynamic-slice.1, bf16[288]{0:T(512)(128)(2,1)S(1)} %dynamic-slice.3, ...), channel_id=1, replica_groups=mesh['grp'=8,'blk'=4] {'grp'}, use_global_device_ids=true, to_apply=%region_19.20 | all-reduce | flops 2304 | bytes 9216 | tf_op jit(solution)/shard_map/psum | solution.py:366
  1143.1 25.4 %all-reduce.12.cloned.1.call-done = (bf16[288,3456]{1,0:T(8,128)(2,1)}, bf16[288,1152]{1,0:T(8,128)(2,1)}, bf16[288,4608]{1,0:T(8,128)(2,1)}, bf16[1152,1152]{1,0:T(8,128)(2,1)}) async-done(((bf16[288,3456]{1,0:T(8,128)(2,1)}, bf16[288,1152]{1,0:T(8,128)(2,1)}, bf16[288,4608]{1,0:T(8,128)(2,1)}, bf16[1152,1152]{1,0:T(8,128)(2,1)}), (bf16[288,3456]{1,0:T(8,128)(2,1)}, bf16[288,1152]{1,0:T(8,128)(2,1)}, ...) | async-done | bytes 7962640 | tf_op jit(solution)/shard_map/psum | solution.py:365
  1179.5 120.7 %all-reduce.10.cloned.1.call-done = f32[3969,16]{0,1:T(8,128)} async-done(((f32[3969,16]{0,1:T(8,128)}), f32[3969,16]{0,1:T(8,128)}) %all-reduce.10.cloned.1.call-update) | async-done | bytes 254032 | tf_op jit(solution)/shard_map/psum | solution.py:374
  (248 shorter events, 246.1 us)
Async XLA Ops:
  7.2 59.5 %all-gather.9.cloned.1.call-start = ((), (), s32[]{:S(2)}) async-start(), calls=%async_computation.6 | async-start | bytes 9953280 | tf_op jit(solution)/shard_map/all_gather | solution.py:168
  7.9 223.7 %all-gather.13.cloned.1.call-start = ((), (), s32[]{:S(2)}) async-start(), calls=%async_computation.8 | async-start | bytes 5898240 | tf_op jit(solution)/shard_map/all_gather | solution.py:190
  25.2 49.2 %copy-start.44 = (f32[2,256]{1,0:T(2,128)}, f32[2,256]{1,0:T(2,128)S(1)}, u32[]{:S(2)}) copy-start(f32[2,256]{1,0:T(2,128)S(1)} %broadcast_multiply_fusion.6) | copy-start | bytes 6148
  25.7 48.8 %copy-start.53 = (f32[2,256]{1,0:T(2,128)}, f32[2,256]{1,0:T(2,128)S(1)}, u32[]{:S(2)}) copy-start(f32[2,256]{1,0:T(2,128)S(1)} %add_rsqrt_fusion.1) | copy-start | bytes 6148
  26.4 48.1 %copy-start.48 = (f32[2,1152]{1,0:T(2,128)}, f32[2,1152]{1,0:T(2,128)S(1)}, u32[]{:S(2)}) copy-start(f32[2,1152]{1,0:T(2,128)S(1)} %get-tuple-element.50) | copy-start | bytes 27652
  78.6 160.1 %all-gather.11.cloned.1.call-start = ((), (), s32[]{:S(2)}) async-start(), calls=%async_computation.7 | async-start | bytes 5898240 | tf_op jit(solution)/shard_map/all_gather | solution.py:191
  82.5 215.5 %all-gather.15.cloned.1.call-start = ((), (), s32[]{:S(2)}) async-start(), calls=%async_computation.9 | async-start | bytes 3317760 | tf_op jit(solution)/shard_map/all_gather | solution.py:169
  83.1 222.5 %all-gather.17.cloned.1.call-start = ((), (), s32[]{:S(2)}) async-start(), calls=%async_computation.10 | async-start | bytes 13271040 | tf_op jit(solution)/shard_map/all_gather | solution.py:170
  83.6 244.4 %all-gather.19.cloned.1.call-start = ((), (), s32[]{:S(2)}) async-start(), calls=%async_computation.11 | async-start | bytes 13271040 | tf_op jit(solution)/shard_map/all_gather | solution.py:171
  84.2 446.7 %reduce-scatter.7.cloned.1.call-start = ((), (), s32[]{:S(2)}) async-start(), calls=%async_computation.12 | async-start | bytes 11796480 | tf_op jit(solution)/shard_map/reduce_scatter | solution.py:263
  303.7 53.8 %copy-start.5 = (f32[2,256,1152]{2,1,0:T(8,128)}, f32[2,256,1152]{2,1,0:T(8,128)S(1)}, u32[]{:S(2)}) copy-start(f32[2,256,1152]{2,1,0:T(8,128)S(1)} %get-tuple-element.40) | copy-start | bytes 7077892
  452.3 159.7 %reduce-scatter.9.cloned.1.call-start = ((), (), s32[]{:S(2)}) async-start(), calls=%async_computation.13 | async-start | bytes 11796480 | tf_op jit(solution)/shard_map/reduce_scatter | solution.py:266
  482.6 167.5 %reduce-scatter.13.cloned.1.call-start = ((), (), s32[]{:S(2)}) async-start(), calls=%async_computation.15 | async-start | bytes 3317760 | tf_op jit(solution)/shard_map/reduce_scatter | solution.py:336
  487.4 251.5 %reduce-scatter.15.cloned.1.call-start = ((), (), s32[]{:S(2)}) async-start(), calls=%async_computation.16 | async-start | bytes 13271040 | tf_op jit(solution)/shard_map/reduce_scatter | solution.py:342
  500.0 327.8 %reduce-scatter.17.cloned.1.call-start = ((), (), s32[]{:S(2)}) async-start(), calls=%async_computation.17 | async-start | bytes 13271040 | tf_op jit(solution)/shard_map/reduce_scatter | solution.py:348
  514.4 385.9 %reduce-scatter.11.cloned.1.call-start = ((), (), s32[]{:S(2)}) async-start(), calls=%async_computation.14 | async-start | bytes 9953280 | tf_op jit(solution)/shard_map/reduce_scatter | solution.py:330
  532.7 82.3 %copy-start.2 = (bf16[2,256,1152]{2,1,0:T(8,128)(2,1)S(1)}, bf16[2,256,1152]{2,1,0:T(8,128)(2,1)}, u32[]{:S(2)}) copy-start(bf16[2,256,1152]{2,1,0:T(8,128)(2,1)} %param.14) | copy-start | bytes 3538948
  532.7 82.3 %copy-start.39 = (f32[2,1152]{1,0:T(2,128)S(1)}, f32[2,1152]{1,0:T(2,128)}, u32[]{:S(2)}) copy-start(f32[2,1152]{1,0:T(2,128)} %copy-done.38) | copy-start | bytes 27652
  532.7 82.3 %copy-start.45 = (f32[2,256]{1,0:T(2,128)S(1)}, f32[2,256]{1,0:T(2,128)}, u32[]{:S(2)}) copy-start(f32[2,256]{1,0:T(2,128)} %copy-done.44) | copy-start | bytes 6148
  532.7 82.3 %copy-start.49 = (f32[2,1152]{1,0:T(2,128)S(1)}, f32[2,1152]{1,0:T(2,128)}, u32[]{:S(2)}) copy-start(f32[2,1152]{1,0:T(2,128)} %copy-done.48) | copy-start | bytes 27652
  532.7 82.3 %copy-start.54 = (f32[2,256]{1,0:T(2,128)S(1)}, f32[2,256]{1,0:T(2,128)}, u32[]{:S(2)}) copy-start(f32[2,256]{1,0:T(2,128)} %copy-done.53) | copy-start | bytes 6148
  622.3 546.1 %all-reduce.12.cloned.1.call-start = ((), (), s32[]{:S(2)}) async-start(), calls=%async_computation.19 | async-start | bytes 15925248 | tf_op jit(solution)/shard_map/psum | solution.py:365
  900.3 399.8 %all-reduce.10.cloned.1.call-start = ((), (), s32[]{:S(2)}) async-start(), calls=%async_computation.18 | async-start | bytes 524288 | tf_op jit(solution)/shard_map/psum | solution.py:374
  939.3 77.2 %copy-start.29 = (s32[32,32]{1,0:T(8,128)S(1)}, s32[32,32]{1,0:T(8,128)}, u32[]{:S(2)}) copy-start(s32[32,32]{1,0:T(8,128)} %copy-done.28) | copy-start | bytes 12292
  (56 other events, 607.7 us)
Sparse Core Ops, SparseCore 0:
  9.6 57.0 all-gather.8
  78.7 37.6 all-gather.12
  118.5 37.4 all-gather.10
  157.5 25.7 all-gather.14
  184.6 70.9 all-gather.16
  257.0 70.9 all-gather.18
  452.5 78.4 reduce-scatter.6
  533.5 78.4 reduce-scatter.8
  615.1 34.8 reduce-scatter.12
  652.7 86.1 reduce-scatter.14
  741.6 86.1 reduce-scatter.16
  831.0 69.2 reduce-scatter.10
  905.4 263.0 all-reduce.11
  1175.3 124.7 all-reduce.9
where the time goes:
time: 1320 us; the launch traced here: 1310 us
  waiting for transfers between devices  560 us (42%)
  matrix products  287 us (22%)
  local copies, waits for them, and re-layouts  245 us (19%)
  blocking collectives  125 us (9%)
  other arithmetic  73.7 us (6%)
  between operations  16.9 us (1%)
    psum x1, waiting for transfers between devices, shards(): table_total = lax.psum(table_grad, ('grp', 'blk'))  121 us
    reduce_scatter x1, waiting for transfers between devices, shards(): lax.psum_scatter(shrink_grad.astype(jnp.bfloat16), 'blk', scatter_dimensi...  89 us
    reduce_scatter x1, waiting for transfers between devices, shards(): lax.psum_scatter(expand_grad.astype(jnp.bfloat16), 'blk', scatter_dimensi...  88.8 us
    reduce_scatter x1, waiting for transfers between devices, shards(): lax.psum_scatter(grad_values.reshape(image_count, -1, model_width), 'blk'...  79.2 us
    reshape x1, local copies, waits for them, and re-layouts, position_grad(): grad_scores.reshape(image_count, heads_here, query_count // grid_side, gr...  77.2 us
    reduce_scatter x1, waiting for transfers between devices, shards(): lax.psum_scatter(input_grad.astype(jnp.bfloat16), 'blk', scatter_dimensio...  72.5 us
    transpose x1, local copies, waits for them, and re-layouts, position_bias(): jnp.einsum('hijd,xyd->hixjy', by_rows, column_table(grid_side), precision...  61.7 us
    add x1, local copies, waits for them, and re-layouts, score_block(): scores + position_bias(table_part, query_start, query_use.shape[1], key_u...  51.8 us
  transfers between devices with their start and end apart: 14, of which 10 were waited for; matrix products, arithmetic and copies ran while one was open for 35% of the time, Pallas kernels for 0%

commit v1 on v0

v1 whole, which is shorter than its diff:
```python
import functools
import math

import jax
import jax.numpy as jnp
from jax import lax
from jax.experimental import pallas as pl
from jax.experimental.pallas import tpu as pltpu
from jax.sharding import PartitionSpec as P

GRID = 32
F32 = jnp.float32
LOW = jnp.bfloat16
HIGHEST = lax.Precision.HIGHEST
TILE = 256
LANES = 128
MIB = 2**20


def dot(left, right, left_dim, right_dim):
    return lax.dot_general(
        left, right, (((left_dim,), (right_dim,)), ((), ())), preferred_element_type=F32
    )


def call(kernel, grid, in_specs, out_specs, out_shape, scratch=(), mib=56):
    return pl.pallas_call(
        kernel,
        grid=grid,
        in_specs=in_specs,
        out_specs=out_specs,
        out_shape=out_shape,
        scratch_shapes=list(scratch),
        compiler_params=pltpu.CompilerParams(vmem_limit_bytes=mib * MIB),
    )


def shape(dims, kind=F32):
    return jax.ShapeDtypeStruct(dims, kind)


def whole(dims):
    return pl.BlockSpec(dims, lambda *_: (0,) * len(dims))


def norm_rows(values):
    centered = values - jnp.mean(values, axis=-1, keepdims=True)
    variance = jnp.mean(centered * centered, axis=-1, keepdims=True)
    inverse = lax.rsqrt(variance + 1e-06)
    return centered * inverse, inverse


def norm_back(grad_normed, normed, inverse):
    first = jnp.mean(grad_normed, axis=-1, keepdims=True)
    second = jnp.mean(grad_normed * normed, axis=-1, keepdims=True)
    return inverse * (grad_normed - first - normed * second)


def project_kernel(parts, head_dim, x_ref, mod_ref, w_ref, b_ref, h_ref, o_ref):
    normed, _ = norm_rows(x_ref[...].astype(F32))
    hidden = (normed * (1.0 + mod_ref[1:2]) + mod_ref[0:1]).astype(LOW)
    h_ref[...] = hidden
    low = (dot(hidden, w_ref[...], 1, 0) + b_ref[...]).astype(LOW)
    for part in range(parts):
        o_ref[part] = low[:, part * head_dim : (part + 1) * head_dim]


def project(tokens, mod, weight, bias, head_dim):
    count, width = tokens.shape
    columns = weight.shape[1]
    parts = columns // head_dim
    return call(
        functools.partial(project_kernel, parts, head_dim),
        (count // TILE,),
        [
            pl.BlockSpec((TILE, width), lambda i: (i, 0)),
            whole(mod.shape),
            whole(weight.shape),
            whole((1, columns)),
        ],
        [
            pl.BlockSpec((TILE, width), lambda i: (i, 0)),
            pl.BlockSpec((parts, TILE, head_dim), lambda i: (0, i, 0)),
        ],
        [shape((count, width), LOW), shape((parts, count, head_dim), LOW)],
    )(tokens, mod, weight, bias)


def bias_tile(table_ref, head, tile, keys):
    pieces = []
    per = TILE // LANES
    last = keys // LANES - 1
    for piece in range(per):
        start = (last - (tile * per + piece)) * LANES
        pieces.append(table_ref[head, start : start + keys, :])
    return jnp.concatenate(pieces, axis=1)


def attend_kernel(q_ref, k_ref, v_ref, table_ref, o_ref, lse_ref):
    heads, count, head_dim = q_ref.shape
    scale = head_dim ** (-0.5)
    for tile in range(count // TILE):
        outs, logs = [], []
        for head in range(heads):
            span = slice(tile * TILE, (tile + 1) * TILE)
            scores = dot(k_ref[head], q_ref[head, span, :], 1, 1) * scale
            scores = scores + bias_tile(table_ref, head, tile, k_ref.shape[1])
            largest = jnp.max(scores, axis=0, keepdims=True)
            exponent = jnp.exp(scores - largest)
            total = jnp.sum(exponent, axis=0, keepdims=True)
            out = dot(v_ref[head], exponent.astype(LOW), 0, 0)
            outs.append(out / total)
            logs.append(largest + jnp.log(total))
        o_ref[:, span] = jnp.concatenate(outs, axis=0).astype(LOW)
        lse_ref[0, :, span] = jnp.concatenate(logs, axis=0)


def attend(parts, table, heads, pair):
    _, count, head_dim = parts.shape
    groups = heads // pair

    def head_block(first):
        return pl.BlockSpec(
            (pair, count, head_dim), lambda i, first=first: (first * groups + i, 0, 0)
        )

    return call(
        attend_kernel,
        (groups,),
        [
            head_block(0),
            head_block(1),
            head_block(2),
            pl.BlockSpec((pair,) + table.shape[1:], lambda i: (i, 0, 0)),
        ],
        [
            pl.BlockSpec((pair * head_dim, count), lambda i: (i, 0)),
            pl.BlockSpec((1, pair, count), lambda i: (i, 0, 0)),
        ],
        [shape((heads * head_dim, count), LOW), shape((groups, pair, count))],
    )(parts, parts, parts, table)


def attend_back_kernel(
    q_ref, k_ref, v_ref, go_ref, o_ref, lse_ref, table_ref, gq_ref, gk_ref, gv_ref, gt_ref
):
    heads, count, head_dim = q_ref.shape
    keys = k_ref.shape[1]
    scale = head_dim ** (-0.5)
    per = TILE // LANES
    last = keys // LANES - 1
    gt_ref[...] = jnp.zeros_like(gt_ref)
    for head in range(heads):
        key = k_ref[head]
        value = v_ref[head]
        grad_key = jnp.zeros((keys, head_dim), F32)
        grad_value = jnp.zeros((keys, head_dim), F32)
        for tile in range(count // TILE):
            span = slice(tile * TILE, (tile + 1) * TILE)
            query = q_ref[head, span, :]
            grad_out = go_ref[head, span, :]
            scores = dot(key, query, 1, 1) * scale + bias_tile(table_ref, head, tile, keys)
            probs = jnp.exp(scores - lse_ref[0, head : head + 1, span])
            grad_probs = dot(value, grad_out, 1, 1)
            out = o_ref[head * head_dim : (head + 1) * head_dim, span].astype(F32)
            row_dot = jnp.sum(out * grad_out.astype(F32).T, axis=0, keepdims=True)
            grad_scores = probs * (grad_probs - row_dot)
            for piece in range(per):
                start = (last - (tile * per + piece)) * LANES
                gt_ref[head, start : start + keys, :] += grad_scores[
                    :, piece * LANES : (piece + 1) * LANES
                ]
            low = grad_scores.astype(LOW)
            grad_value = grad_value + dot(probs.astype(LOW), grad_out, 1, 0)
            grad_key = grad_key + dot(low, query, 1, 0)
            gq_ref[head, span, :] = (dot(key, low, 0, 0) * scale).T.astype(LOW)
        gk_ref[head] = (grad_key * scale).astype(LOW)
        gv_ref[head] = grad_value.astype(LOW)


def attend_back(parts, grad_out, attended, log_total, table, heads, pair):
    _, count, head_dim = parts.shape
    groups = heads // pair

    def head_block(first):
        return pl.BlockSpec(
            (pair, count, head_dim), lambda i, first=first: (first * groups + i, 0, 0)
        )

    table_block = pl.BlockSpec((pair,) + table.shape[1:], lambda i: (i, 0, 0))
    return call(
        attend_back_kernel,
        (groups,),
        [
            head_block(0),
            head_block(1),
            head_block(2),
            head_block(0),
            pl.BlockSpec((pair * head_dim, count), lambda i: (i, 0)),
            pl.BlockSpec((1, pair, count), lambda i: (i, 0, 0)),
            table_block,
        ],
        [head_block(0)] * 3 + [table_block],
        [shape((heads, count, head_dim), LOW)] * 3 + [shape(table.shape)],
    )(parts, parts, parts, grad_out, attended, log_total, table)


def middle_kernel(
    att_ref, w_ref, ob_ref, x_ref, cot_ref, mod_ref, br_ref, mid_ref, h_ref, gb_ref, sum_ref
):
    branch = dot(att_ref[...], w_ref[...], 0, 0) + ob_ref[...]
    middle = x_ref[...].astype(F32) + mod_ref[2:3] * branch
    normed, _ = norm_rows(middle)
    br_ref[...] = branch.astype(LOW)
    mid_ref[...] = middle
    h_ref[...] = (normed * (1.0 + mod_ref[4:5]) + mod_ref[3:4]).astype(LOW)
    grad = (mod_ref[5:6] * cot_ref[...].astype(F32)).astype(LOW)
    gb_ref[...] = grad

    @pl.when(pl.program_id(0) == 0)
    def _():
        sum_ref[...] = jnp.zeros_like(sum_ref)

    sum_ref[...] += jnp.sum(grad.astype(F32), axis=0, keepdims=True)


def middle_part(attended, weight, bias, tokens, cotangent, mod):
    count, width = tokens.shape
    rows = pl.BlockSpec((TILE, width), lambda i: (i, 0))
    return call(
        middle_kernel,
        (count // TILE,),
        [
            pl.BlockSpec((attended.shape[0], TILE), lambda i: (0, i)),
            whole(weight.shape),
            whole((1, width)),
            rows,
            rows,
            whole(mod.shape),
        ],
        [rows, rows, rows, rows, whole((1, width))],
        [
            shape((count, width), LOW),
            shape((count, width)),
            shape((count, width), LOW),
            shape((count, width), LOW),
            shape((1, width)),
        ],
    )(attended, weight, bias, tokens, cotangent, mod)


def feed_kernel(
    h_ref, g_ref, we_ref, ws_ref, be_ref, act_ref, ge_ref, sum_ref, b2_ref, gh_ref, b2_acc, gh_acc
):
    step = pl.program_id(0)
    hidden, grad, expand, shrink = h_ref[...], g_ref[...], we_ref[...], ws_ref[...]
    inner = dot(hidden, expand, 1, 0) + be_ref[...]
    slope = math.sqrt(2.0 / math.pi)
    square = inner * inner
    bent = jnp.tanh(slope * (inner + 0.044715 * inner * square))
    act = (0.5 * inner * (1.0 + bent)).astype(LOW)
    act_ref[...] = act
    back = 0.5 * (1.0 + bent) + 0.5 * inner * (1.0 - bent * bent) * (
        slope * (1.0 + 3 * 0.044715 * square)
    )
    grad_inner = (dot(grad, shrink, 1, 1) * back).astype(LOW)
    ge_ref[...] = grad_inner
    sum_ref[...] = jnp.sum(grad_inner.astype(F32), axis=0, keepdims=True)

    @pl.when(step == 0)
    def _():
        b2_acc[...] = dot(act, shrink, 1, 0)
        gh_acc[...] = dot(grad_inner, expand, 1, 1)

    @pl.when(step > 0)
    def _():
        b2_acc[...] += dot(act, shrink, 1, 0)
        gh_acc[...] += dot(grad_inner, expand, 1, 1)

    @pl.when(step == pl.num_programs(0) - 1)
    def _():
        b2_ref[...] = b2_acc[...].astype(LOW)
        gh_ref[...] = gh_acc[...].astype(LOW)


def feed(hidden, grad, expand, shrink, bias, chunk):
    count, width = hidden.shape
    inner = expand.shape[1]
    return call(
        feed_kernel,
        (inner // chunk,),
        [
            whole(hidden.shape),
            whole(grad.shape),
            pl.BlockSpec((width, chunk), lambda i: (0, i)),
            pl.BlockSpec((chunk, width), lambda i: (i, 0)),
            pl.BlockSpec((1, chunk), lambda i: (0, i)),
        ],
        [
            pl.BlockSpec((count, chunk), lambda i: (0, i)),
            pl.BlockSpec((count, chunk), lambda i: (0, i)),
            pl.BlockSpec((1, chunk), lambda i: (0, i)),
            whole((count, width)),
            whole((count, width)),
        ],
        [
            shape((count, inner), LOW),
            shape((count, inner), LOW),
            shape((1, inner)),
            shape((count, width), LOW),
            shape((count, width), LOW),
        ],
        [pltpu.VMEM((count, width), F32)] * 2,
    )(hidden, grad, expand, shrink, bias)


def branch_back_kernel(
    head_dim,
    own_ref,
    got_ref,
    mid_ref,
    cot_ref,
    br_ref,
    w_ref,
    mod_ref,
    gm_ref,
    gb_ref,
    ga_ref,
    sum_ref,
):
    grad_hidden = own_ref[...].astype(F32) + got_ref[...].astype(F32)
    normed, inverse = norm_rows(mid_ref[...])
    grad_middle = cot_ref[...].astype(F32) + norm_back(
        grad_hidden * (1.0 + mod_ref[4:5]), normed, inverse
    )
    gm_ref[...] = grad_middle
    grad_branch = (mod_ref[2:3] * grad_middle).astype(LOW)
    gb_ref[...] = grad_branch
    grad_att = dot(grad_branch, w_ref[...], 1, 1).astype(LOW)
    for part in range(ga_ref.shape[0]):
        ga_ref[part] = grad_att[:, part * head_dim : (part + 1) * head_dim]

    @pl.when(pl.program_id(0) == 0)
    def _():
        sum_ref[...] = jnp.zeros_like(sum_ref)

    sum_ref[0:1] += jnp.sum(grad_hidden, axis=0, keepdims=True)
    sum_ref[1:2] += jnp.sum(grad_hidden * normed, axis=0, keepdims=True)
    sum_ref[2:3] += jnp.sum(grad_middle * br_ref[...].astype(F32), axis=0, keepdims=True)
    sum_ref[3:4] += jnp.sum(grad_branch.astype(F32), axis=0, keepdims=True)


def branch_back(own, got, middle, cotangent, branch, weight, mod, head_dim):
    count, width = own.shape
    rows = pl.BlockSpec((TILE, width), lambda i: (i, 0))
    parts = weight.shape[0] // head_dim
    return call(
        functools.partial(branch_back_kernel, head_dim),
        (count // TILE,),
        [rows, rows, rows, rows, rows, whole(weight.shape), whole(mod.shape)],
        [
            rows,
            rows,
            pl.BlockSpec((parts, TILE, head_dim), lambda i: (0, i, 0)),
            whole((8, width)),
        ],
        [
            shape((count, width)),
            shape((count, width), LOW),
            shape((parts, count, head_dim), LOW),
            shape((8, width)),
        ],
    )(own, got, middle, cotangent, branch, weight, mod)


def project_back_kernel(gq_ref, gk_ref, gv_ref, w_ref, x_ref, g_ref, gh_ref, sum_ref, bias_ref):
    pieces = [ref[part] for ref in (gq_ref, gk_ref, gv_ref) for part in range(ref.shape[0])]
    joined = jnp.concatenate(pieces, axis=1)
    g_ref[...] = joined
    grad_hidden = dot(joined, w_ref[...], 1, 1)
    gh_ref[...] = grad_hidden.astype(LOW)
    normed, _ = norm_rows(x_ref[...].astype(F32))

    @pl.when(pl.program_id(0) == 0)
    def _():
        sum_ref[...] = jnp.zeros_like(sum_ref)
        bias_ref[...] = jnp.zeros_like(bias_ref)

    sum_ref[0:1] += jnp.sum(grad_hidden, axis=0, keepdims=True)
    sum_ref[1:2] += jnp.sum(grad_hidden * normed, axis=0, keepdims=True)
    bias_ref[...] += jnp.sum(joined.astype(F32), axis=0, keepdims=True)


def project_back(grad_query, grad_key, grad_value, weight, tokens):
    count, width = tokens.shape
    columns = weight.shape[1]
    heads, _, head_dim = grad_query.shape
    rows = pl.BlockSpec((TILE, width), lambda i: (i, 0))
    part = pl.BlockSpec((heads, TILE, head_dim), lambda i: (0, i, 0))
    return call(
        project_back_kernel,
        (count // TILE,),
        [part, part, part, whole(weight.shape), rows],
        [
            pl.BlockSpec((TILE, columns), lambda i: (i, 0)),
            rows,
            whole((8, width)),
            whole((1, columns)),
        ],
        [
            shape((count, columns), LOW),
            shape((count, width), LOW),
            shape((8, width)),
            shape((1, columns)),
        ],
    )(grad_query, grad_key, grad_value, weight, tokens)


def input_back_kernel(own_ref, got_ref, x_ref, gm_ref, mod_ref, o_ref):
    grad_hidden = own_ref[...].astype(F32) + got_ref[...].astype(F32)
    normed, inverse = norm_rows(x_ref[...].astype(F32))
    grad = gm_ref[...] + norm_back(grad_hidden * (1.0 + mod_ref[1:2]), normed, inverse)
    o_ref[...] = grad.astype(LOW)


def input_back(own, got, tokens, grad_middle, mod):
    count, width = own.shape
    rows = pl.BlockSpec((TILE, width), lambda i: (i, 0))
    return call(
        input_back_kernel,
        (count // TILE,),
        [rows, rows, rows, rows, whole(mod.shape)],
        rows,
        shape((count, width), LOW),
    )(own, got, tokens, grad_middle, mod)


def swap_core(value):
    return lax.ppermute(value, "blk", [(i, i ^ 1) for i in range(4)])


def swap_chip(value):
    return lax.ppermute(value, "blk", [(i, i ^ 2) for i in range(4)])


def swap_group(value, bit):
    return lax.ppermute(value, "grp", [(i, i ^ bit) for i in range(lax.axis_size("grp"))])


def ordered(mine, other, place, axis=0):
    first = jnp.where(place == 0, mine, other)
    second = jnp.where(place == 0, other, mine)
    return jnp.concatenate([first, second], axis=axis)


def split_at(value, place, axis):
    half = value.shape[axis] // 2
    keep = lax.dynamic_slice_in_dim(value, place * half, half, axis)
    send = lax.dynamic_slice_in_dim(value, (1 - place) * half, half, axis)
    return keep, send


def add_low(one, two):
    return (one.astype(F32) + two.astype(F32)).astype(LOW)


def group_bits():
    count = lax.axis_size("grp")
    return [1 << i for i in range(count.bit_length() - 1)]


def bit_of(bit):
    return (lax.axis_index("grp") // bit) % 2


def scatter_groups(value, axis):
    for bit in group_bits():
        keep, send = split_at(value, bit_of(bit), axis)
        value = add_low(keep, swap_group(send, bit))
    return value


def gather_groups(value, axis):
    for bit in reversed(group_bits()):
        value = ordered(value, swap_group(value, bit), bit_of(bit), axis)
    return value


def table_picks(grid_side):
    span = 2 * grid_side - 1
    per = LANES // grid_side
    piece = jnp.arange(per, dtype=jnp.int32)
    offset = jnp.arange(span, dtype=jnp.int32)
    across = jnp.arange(grid_side, dtype=jnp.int32)
    same_piece = piece[:, None] == piece[None, :]
    same_offset = (
        across[None, None, :] - across[None, :, None] + grid_side - 1 == offset[:, None, None]
    )
    picks = same_piece[:, None, None, :, None] & same_offset[None, :, :, None, :]
    return picks.reshape(per * span, grid_side * LANES).astype(F32)


def table_rows(grid_side):
    return 2 * grid_side - LANES // grid_side


def spread_table(table, grid_side):
    span = 2 * grid_side - 1
    per = LANES // grid_side
    heads = table.shape[1]
    grid_table = table.T.reshape(heads, span, span)
    count = table_rows(grid_side)
    flipped = grid_table[:, ::-1]
    shifted = [
        flipped[:, per - 1 - piece : per - 1 - piece + count] for piece in range(per)
    ]
    stacked = jnp.stack(shifted, axis=2).reshape(heads * count, per * span)
    spread = jnp.dot(stacked, table_picks(grid_side), precision=HIGHEST)
    return spread.reshape(heads, count * grid_side, LANES)


def gather_table(grads, grid_side):
    span = 2 * grid_side - 1
    per = LANES // grid_side
    heads = grads.shape[0]
    count = table_rows(grid_side)
    flat = grads.reshape(heads * count, grid_side * LANES)
    picked = lax.dot_general(
        flat, table_picks(grid_side), (((1,), (1,)), ((), ())), precision=HIGHEST
    ).reshape(heads, count, per, span)
    total = sum(
        jnp.pad(
            picked[:, :, piece],
            ((0, 0), (per - 1 - piece, span - count - (per - 1 - piece)), (0, 0)),
        )
        for piece in range(per)
    )
    return total[:, ::-1].reshape(heads, span * span)


def embedding(step_values, width):
    half_width = width // 2
    frequency = jnp.exp(-math.log(10000.0) * jnp.arange(half_width, dtype=F32) / half_width)
    angles = step_values.astype(F32)[:, None] * frequency[None, :]
    return jnp.concatenate([jnp.cos(angles), jnp.sin(angles)], axis=-1)


def pick(value, place, axis=0):
    return lax.dynamic_index_in_dim(value, place, axis, keepdims=False)


def shards(
    images,
    cotangent,
    timestep,
    input_weight,
    input_bias,
    output_weight,
    output_bias,
    expand_weight,
    expand_bias,
    shrink_weight,
    shrink_bias,
    modulate_weight,
    modulate_bias,
    position_table,
):
    _, block_tokens, width = images.shape
    heads_all = position_table.shape[1]
    head_dim = width // heads_all
    heads = heads_all // 2
    feed_width = expand_weight.shape[1]
    own_rows = modulate_weight.shape[0]
    block = lax.axis_index("blk")
    chip, core = block // 2, block % 2

    condition = jax.nn.silu(embedding(timestep, width)).astype(LOW)
    condition_own = lax.dynamic_slice_in_dim(condition, block * own_rows, own_rows, 1)
    partial = jnp.dot(condition_own, modulate_weight, preferred_element_type=F32)
    partial = partial.reshape(2, -1, LANES)
    summed = pick(partial, core) + swap_core(pick(partial, 1 - core))
    summed = summed + swap_chip(summed)
    mod = (summed.reshape(-1) + modulate_bias).reshape(6, width)

    def gather_columns(weight, pieces):
        cut = weight.reshape(own_rows, pieces, 2, -1)
        mine = pick(cut, chip, 2).reshape(own_rows, -1)
        other = swap_chip(pick(cut, 1 - chip, 2).reshape(own_rows, -1))
        both = ordered(mine[None], other[None], chip)
        return ordered(both[:, None], swap_core(both)[:, None], core, 1).reshape(width, -1)

    def own_image(value):
        mine = pick(value, core)
        half = ordered(mine, swap_core(pick(value, 1 - core)), core)
        return half, ordered(half, swap_chip(half), chip)

    weight_in = gather_columns(input_weight, 3)
    tokens_half, tokens = own_image(images)
    cot_half, cot = own_image(cotangent)
    weight_out_pair = ordered(output_weight[None], swap_chip(output_weight)[None], chip)
    weight_out = ordered(
        weight_out_pair[:, None], swap_core(weight_out_pair)[:, None], core, 1
    ).reshape(width, width)
    weight_expand = gather_columns(expand_weight, 1)
    weight_shrink = ordered(shrink_weight, swap_core(shrink_weight), core)

    def own_half(vector):
        return lax.dynamic_slice_in_dim(vector, chip * (vector.shape[0] // 2), vector.shape[0] // 2, 0)

    bias_in = jnp.concatenate(
        [
            own_half(input_bias[:width]),
            jnp.zeros((width // 2,), F32),
            own_half(input_bias[width:]),
        ]
    )[None]
    table = spread_table(
        lax.dynamic_slice_in_dim(position_table, chip * heads, heads, 1), GRID
    )

    hidden_one, parts = project(tokens, mod, weight_in, bias_in, head_dim)
    attended, log_total = attend(parts, table, heads, 2)
    attended_all = ordered(attended, swap_chip(attended), chip)
    branch_one, middle, hidden_two, grad_branch_two, shrink_bias_grad = middle_part(
        attended_all, weight_out, output_bias[None], tokens, cot, mod
    )
    activated, grad_expanded, expand_bias_grad, branch_two, grad_hidden_two = feed(
        hidden_two, grad_branch_two, weight_expand, weight_shrink, own_half(expand_bias)[None], 384
    )
    half_count = tokens_half.shape[0]

    def half_of(value, place):
        return lax.dynamic_slice_in_dim(value, place * half_count, half_count, 0)

    grad_hidden_two_got = swap_chip(grad_hidden_two)
    branch_two_got = swap_chip(half_of(branch_two, 1 - chip))
    grad_middle, grad_branch_one, grad_attended, sums_two = branch_back(
        grad_hidden_two,
        grad_hidden_two_got,
        middle,
        cot,
        branch_one,
        lax.dynamic_slice_in_dim(weight_out, chip * (width // 2), width // 2, 0),
        mod,
        head_dim,
    )
    shrink_grad = dot(activated, grad_branch_two, 0, 0).astype(LOW)
    expand_grad = dot(hidden_two, grad_expanded, 0, 0).astype(LOW)
    output_grad = dot(attended, grad_branch_one, 1, 0).astype(LOW)
    grad_query, grad_key, grad_value, table_grad = attend_back(
        parts, grad_attended, attended, log_total, table, heads, 2
    )
    grad_projected, grad_hidden_one, sums_one, projected_bias_grad = project_back(
        grad_query, grad_key, grad_value, weight_in, tokens
    )
    grad_hidden_one_got = swap_chip(half_of(grad_hidden_one, 1 - chip))
    input_grad = dot(hidden_one, grad_projected, 0, 0).astype(LOW)
    grad_tokens = input_back(
        half_of(grad_hidden_one, chip),
        grad_hidden_one_got,
        tokens_half,
        half_of(grad_middle, chip),
        mod,
    )

    branch_two_half = (
        half_of(branch_two, chip).astype(F32) + branch_two_got.astype(F32) + shrink_bias
    )
    result_half = (half_of(middle, chip) + mod[5:6] * branch_two_half).astype(LOW)
    grad_gate_two = jnp.sum(cot_half.astype(F32) * branch_two_half, axis=0)

    def to_blocks(value):
        cut = value.reshape(2, block_tokens, width)
        mine = pick(cut, core)
        other = swap_core(pick(cut, 1 - core))
        return ordered(mine[None], other[None], core)

    result = to_blocks(result_half)
    grad_images = to_blocks(grad_tokens)

    def reduce_rows(grad):
        keep, send = split_at(grad, core, 0)
        return gather_groups(scatter_groups(add_low(keep, swap_core(send)), 0), 0).astype(F32)

    def reduce_columns(grad, pieces):
        keep, send = split_at(grad.reshape(2, 2, own_rows, -1), core, 1)
        cut = add_low(keep, swap_core(send)).reshape(2, own_rows, -1)
        cut = scatter_groups(cut, 1)
        mine = pick(cut, chip)
        other = swap_chip(pick(cut, 1 - chip))
        rows = mine.shape[0]
        mine, other = mine.reshape(rows, pieces, 1, -1), other.reshape(rows, pieces, 1, -1)
        joined = ordered(mine, other, chip, 2).reshape(rows, -1)
        return gather_groups(joined, 0).astype(F32)

    total_shrink = reduce_rows(shrink_grad)
    total_expand = reduce_columns(expand_grad, 1)
    total_output = reduce_rows(output_grad)
    total_input = reduce_columns(input_grad, 3)

    half_width = width // 2
    table_vector = gather_table(table_grad, GRID)
    split_vector = jnp.concatenate(
        [
            table_vector.reshape(-1),
            projected_bias_grad[0, :half_width],
            projected_bias_grad[0, 2 * half_width :],
            expand_bias_grad[0],
        ]
    )
    both_vector = jnp.concatenate([sums_two[3], shrink_bias_grad[0]])
    split_rows = -(-split_vector.shape[0] // LANES)
    split_vector_padded = jnp.pad(split_vector, (0, split_rows * LANES - split_vector.shape[0]))
    small = jnp.concatenate([split_vector_padded, both_vector]).reshape(-1, LANES)
    small = small + swap_core(small)
    for bit in group_bits():
        small = small + swap_group(small, bit)
    small_own = small[:split_rows]
    small_two = ordered(small_own[None], swap_chip(small_own)[None], chip).reshape(2, -1)
    table_size = table_vector.size
    table_total = small_two[:, :table_size].reshape(heads_all, -1).T
    at = table_size
    bias_query = small_two[:, at : at + half_width]
    bias_value = small_two[:, at + half_width : at + 2 * half_width]
    at = at + 2 * half_width
    bias_expand = small_two[:, at : at + feed_width // 2].reshape(-1)
    bias_input = jnp.stack([bias_query, bias_value]).reshape(-1)
    both = small[split_rows:].reshape(2, width)

    def own_part(vector):
        size = vector.shape[0] // 4
        return lax.dynamic_slice_in_dim(vector, block * size, size, 0)

    split_sums = jnp.stack([sums_one[0], sums_one[1], grad_gate_two]).reshape(-1, LANES)
    split_sums = (split_sums + swap_chip(split_sums)).reshape(3, width)
    image_row = jnp.concatenate(
        [
            split_sums[0],
            split_sums[1],
            sums_two[2],
            sums_two[0],
            sums_two[1],
            split_sums[2],
            pick(condition, core).astype(F32),
        ]
    ).astype(LOW)
    rows = image_row.reshape(1, -1, LANES)
    rows = ordered(rows, swap_core(rows), core)
    for bit in group_bits():
        rows = ordered(rows, swap_group(rows, bit), bit_of(bit))
    rows = rows.reshape(rows.shape[0], -1)
    grads_all, conditions = rows[:, : 6 * width], rows[:, 6 * width :]
    conditions_own = lax.dynamic_slice_in_dim(conditions, block * own_rows, own_rows, 1)
    modulate_grad = dot(conditions_own, grads_all, 0, 0)
    modulate_bias_grad = own_part(jnp.sum(grads_all.astype(F32), axis=0))

    return (
        result,
        grad_images,
        total_input,
        own_part(bias_input),
        total_output,
        own_part(both[0]),
        total_expand,
        own_part(bias_expand),
        total_shrink,
        own_part(both[1]),
        modulate_grad,
        modulate_bias_grad,
        table_total,
    )


def solution(mesh):
    return jax.shard_map(
        shards,
        mesh=mesh,
        in_specs=(
            P("grp", "blk", None),
            P("grp", "blk", None),
            P("grp"),
            P("blk", None),
            P(),
            P("blk", None),
            P(),
            P("blk", None),
            P(),
            P("blk", None),
            P(),
            P("blk", None),
            P(),
            P(),
        ),
        out_specs=(
            P("grp", "blk", None),
            P("grp", "blk", None),
            P("blk", None),
            P("blk"),
            P("blk", None),
            P("blk"),
            P("blk", None),
            P("blk"),
            P("blk", None),
            P("blk"),
            P("blk", None),
            P("blk"),
            P(),
        ),
        check_vma=False,
    )
```

time: 1320 us -> 853 us (0.65)
  matrix products: 287 us -> 51 us
  waiting for transfers between devices: 560 us -> 377 us
  Pallas kernels: 0 us -> 145 us
  blocking collectives: 125 us -> 0 us
  local copies, waits for them, and re-layouts: 245 us -> 132 us
  starting transfers between devices: 0.56 us -> 58.2 us
  between operations: 16.9 us -> 2.74 us
    ppermute x0 -> x59, waiting for transfers between devices: none -> 377 us  [the longest x30 244 us: swap_group(): lax.ppermute(value, 'grp', [(i, i ^ bit) for i in range(lax.axis_size('gr...]
    reduce_scatter x6 -> x0, waiting for transfers between devices: 362 us -> none  [the longest x1 89 us: shards(): lax.psum_scatter(shrink_grad.astype(jnp.bfloat16), 'blk', scatter_dimensi...]
    dot_general x24 -> x8, matrix products: 287 us -> 51 us  [the longest x5 33.2 us: dot(): lax.dot_general(left, right, (((left_dim,), (right_dim,)), ((), ())), pre...]
    psum x2 -> x0, waiting for transfers between devices: 146 us -> none  [the longest x1 121 us: shards(): table_total = lax.psum(table_grad, ('grp', 'blk'))]
    pallas_call x0 -> x8, Pallas kernels: none -> 145 us  [the longest x1 40.6 us: feed(): call(feed_kernel, (inner // chunk,), [whole(hidden.shape), whole(grad.sha...]
    reshape x5 -> x15, local copies, waits for them, and re-layouts: 98.2 us -> 24.1 us  [the longest x1 9.66 us: spread_table(): return spread.reshape(heads, count * grid_side, LANES)]
    all_gather x2 -> x0, blocking collectives: 72 us -> none  [the longest x1 38 us: shards(): lax.all_gather(grad_modulation.astype(jnp.bfloat16), ('grp', 'blk'), axis...]
    transpose x1, local copies, waits for them, and re-layouts: 61.7 us -> 0.02 us  [spread_table(): grid_table = table.T.reshape(heads, span, span)]
  transfers between devices with their start and end apart: 14 -> 59, of which waited for: 10 -> 32; matrix products, arithmetic and copies ran while one was open for 35% -> 28% of each run, Pallas kernels for 0% -> 11%
where the time goes in v1:
time: 853 us; the launch traced here: 842 us
  waiting for transfers between devices  377 us (44%)
  Pallas kernels  145 us (17%)
  local copies, waits for them, and re-layouts  132 us (15%)
  other arithmetic  75.6 us (9%)
  starting transfers between devices  58.2 us (7%)
  matrix products  51 us (6%)
    ppermute x30, waiting for transfers between devices, swap_group(): lax.ppermute(value, 'grp', [(i, i ^ bit) for i in range(lax.axis_size('gr...  244 us
    ppermute x14, waiting for transfers between devices, swap_chip(): return lax.ppermute(value, 'blk', [(i, i ^ 2) for i in range(4)])  130 us
    ppermute x30, starting transfers between devices, swap_group(): lax.ppermute(value, 'grp', [(i, i ^ bit) for i in range(lax.axis_size('gr...  44.1 us
    pallas_call x1, Pallas kernels, feed(): call(feed_kernel, (inner // chunk,), [whole(hidden.shape), whole(grad.sha...  40.6 us
    dot_general x5, matrix products, dot(): lax.dot_general(left, right, (((left_dim,), (right_dim,)), ((), ())), pre...  33.2 us
    pallas_call x1, Pallas kernels, attend_back(): call(attend_back_kernel, (groups,), [head_block(0), head_block(1), head_b...  26.5 us
    pallas_call x1, Pallas kernels, attend(): call(attend_kernel, (groups,), [head_block(0), head_block(1), head_block(...  26.3 us
    select_n x32, other arithmetic, ordered(): first = jnp.where(place == 0, mine, other)  24.6 us
  transfers between devices with their start and end apart: 59, of which 32 were waited for; matrix products, arithmetic and copies ran while one was open for 28% of the time, Pallas kernels for 11%

profile of v1, /device:TPU:16, one launch (start us, length us, event | category | flops | bytes accessed | tf_op | source)
XLA Modules:
  0.0 841.6 jit_solution(4276283149047252271)
XLA Ops:
  68.0 9.7 %reshape.380.table_ref = f32[8,1920,128]{2,1,0:T(8,128)} reshape(f32[480,4096]{1,0:T(8,128)} %fusion.21) | data formatting | bytes 15728640 | tf_op jit(solution)/shard_map/reshape | solution.py:519
  98.7 11.6 %collective-permute-done.11 = bf16[288,2304]{1,0:T(8,128)(2,1)} collective-permute-done((bf16[288,2304]{1,0:T(8,128)(2,1)}, bf16[288,2304]{1,0:T(8,128)(2,1)}, u32[]{:S(2)}, u32[]{:S(2)}) %collective-permute-start.11) | collective-permute-done | bytes 1327136 | tf_op jit(solution)/shard_map/ppermute | solution.py:443
  114.4 21.1 %collective-permute-done.10 = bf16[512,1152]{1,0:T(8,128)(2,1)} collective-permute-done((bf16[512,1152]{1,0:T(8,128)(2,1)}, bf16[512,1152]{1,0:T(8,128)(2,1)}, u32[]{:S(2)}, u32[]{:S(2)}) %collective-permute-start.10) | collective-permute-done | bytes 1179680 | tf_op jit(solution)/shard_map/ppermute | solution.py:443
  137.2 22.2 %collective-permute-done.1 = bf16[512,1152]{1,0:T(8,128)(2,1)} collective-permute-done((bf16[512,1152]{1,0:T(8,128)(2,1)}, bf16[512,1152]{1,0:T(8,128)(2,1)}, u32[]{:S(2)}, u32[]{:S(2)}) %collective-permute-start.1) | collective-permute-done | bytes 1179680 | tf_op jit(solution)/shard_map/ppermute | solution.py:443
  191.6 11.3 %shard_map.237 = (bf16[1024,1152]{1,0:T(8,128)(2,1)}, bf16[24,1024,72]{2,1,0:T(8,128)(2,1)}) custom-call(bf16[1024,1152]{1,0:T(8,128)(2,1)} %get-tuple-element.165.x_ref, f32[6,1152]{1,0:T(8,128)} %reshape.374.mod_ref, bf16[1152,1728]{1,0:T(8,128)(2,1)} %bitcast.182, f32[1,1728]{1,0:T(1,128)} %broadcast_in_dim.13.b_ref), custom_call_target="tpu_custom_call" | custom-call | tf_op jit(solution)/shard_map/pallas_call | solution.py:72
  202.9 26.3 %shard_map.238 = (bf16[576,1024]{1,0:T(8,128)(2,1)}, f32[4,2,1024]{2,1,0:T(2,128)}) custom-call(bf16[24,1024,72]{2,1,0:T(8,128)(2,1)} %get-tuple-element.39.q_ref.k_ref.v_ref, bf16[24,1024,72]{2,1,0:T(8,128)(2,1)} %get-tuple-element.39.q_ref.k_ref.v_ref, bf16[24,1024,72]{2,1,0:T(8,128)(2,1)} %get-tuple-element.39.q_ref.k_ref.v_ref, ...), custom_call_target="tpu_custom_call" | custom-call | tf_op jit(solution)/shard_map/pallas_call | solution.py:127
  235.1 21.0 %collective-permute-done.6 = bf16[576,1024]{1,0:T(8,128)(2,1)S(1)} collective-permute-done((bf16[576,1024]{1,0:T(8,128)(2,1)}, bf16[576,1024]{1,0:T(8,128)(2,1)S(1)}, u32[]{:S(2)}, u32[]{:S(2)}) %collective-permute-start.6) | collective-permute-done | bytes 1179680 | tf_op jit(solution)/shard_map/ppermute | solution.py:443
  257.8 11.5 %shard_map.239 = (bf16[1024,1152]{1,0:T(8,128)(2,1)}, f32[1024,1152]{1,0:T(8,128)}, bf16[1024,1152]{1,0:T(8,128)(2,1)}, bf16[1024,1152]{1,0:T(8,128)(2,1)}, f32[1,1152]{1,0:T(1,128)}) custom-call(bf16[1152,1024]{1,0:T(8,128)(2,1)} %pad_maximum_fusion.7.att_ref, bf16[1152,1152]{1,0:T(8,128)(2,1)} %bitcast.186, f32[1,1152]{1,0:T(1,128)} %broadcast_in_dim.14.ob_ref, ...), custom_call_target="tpu_custom_call" | custom-call | tf_op jit(solution)/shard_map/pallas_call | solution.py:230
  270.0 40.6 %shard_map.240 = (bf16[1024,2304]{1,0:T(8,128)(2,1)}, bf16[1024,2304]{1,0:T(8,128)(2,1)}, f32[1,2304]{1,0:T(1,128)}, bf16[1024,1152]{1,0:T(8,128)(2,1)}, bf16[1024,1152]{1,0:T(8,128)(2,1)}) custom-call(bf16[1024,1152]{1,0:T(8,128)(2,1)} %get-tuple-element.42.h_ref, bf16[1024,1152]{1,0:T(8,128)(2,1)} %get-tuple-element.43.g_ref, ...), custom_call_target="tpu_custom_call" | custom-call | tf_op jit(solution)/shard_map/pallas_call | solution.py:289
  327.7 14.2 %collective-permute-done.14 = bf16[512,1152]{1,0:T(8,128)(2,1)S(1)} collective-permute-done((bf16[512,1152]{1,0:T(8,128)(2,1)S(1)}, bf16[512,1152]{1,0:T(8,128)(2,1)S(1)}, u32[]{:S(2)}, u32[]{:S(2)}) %collective-permute-start.14) | collective-permute-done | bytes 1179680 | tf_op jit(solution)/shard_map/ppermute | solution.py:443
  354.7 34.5 %collective-permute-done.16.got_ref = bf16[1024,1152]{1,0:T(8,128)(2,1)S(1)} collective-permute-done((bf16[1024,1152]{1,0:T(8,128)(2,1)S(1)}, bf16[1024,1152]{1,0:T(8,128)(2,1)S(1)}, u32[]{:S(2)}, u32[]{:S(2)}) %collective-permute-start.16) | collective-permute-done | bytes 2359328 | tf_op jit(solution)/shard_map/ppermute | solution.py:443
  390.7 12.1 %shard_map.241 = (f32[1024,1152]{1,0:T(8,128)}, bf16[1024,1152]{1,0:T(8,128)(2,1)}, bf16[8,1024,72]{2,1,0:T(8,128)(2,1)}, f32[8,1152]{1,0:T(8,128)}) custom-call(bf16[1024,1152]{1,0:T(8,128)(2,1)} %get-tuple-element.45.own_ref, bf16[1024,1152]{1,0:T(8,128)(2,1)} %copy-done.27, f32[1024,1152]{1,0:T(8,128)} %get-tuple-element.41.mid_ref, ...), custom_call_target="tpu_custom_call" | custom-call | tf_op jit(solution)/shard_map/pallas_call | solution.py:357
  406.3 26.5 %shard_map.242 = (bf16[8,1024,72]{2,1,0:T(8,128)(2,1)}, bf16[8,1024,72]{2,1,0:T(8,128)(2,1)}, bf16[8,1024,72]{2,1,0:T(8,128)(2,1)}, f32[8,1920,128]{2,1,0:T(8,128)}) custom-call(bf16[24,1024,72]{2,1,0:T(8,128)(2,1)} %get-tuple-element.39.q_ref.k_ref.v_ref, bf16[24,1024,72]{2,1,0:T(8,128)(2,1)} %get-tuple-element.39.q_ref.k_ref.v_ref, ...), custom_call_target="tpu_custom_call" | custom-call | tf_op jit(solution)/shard_map/pallas_call | solution.py:191
  432.8 11.8 %shard_map.243 = (bf16[1024,1728]{1,0:T(8,128)(2,1)}, bf16[1024,1152]{1,0:T(8,128)(2,1)}, f32[8,1152]{1,0:T(8,128)}, f32[1,1728]{1,0:T(1,128)}) custom-call(bf16[8,1024,72]{2,1,0:T(8,128)(2,1)} %get-tuple-element.49.gq_ref, bf16[8,1024,72]{2,1,0:T(8,128)(2,1)} %get-tuple-element.50.gk_ref, bf16[8,1024,72]{2,1,0:T(8,128)(2,1)} %get-tuple-element.51.gv_ref, ...), custom_call_target="tpu_custom_call" | custom-call | tf_op jit(solution)/shard_map/pallas_call | solution.py:400
  453.3 9.5 %convolution_convert_fusion.2 = bf16[1152,1728]{0,1:T(8,128)(2,1)} fusion(bf16[1024,1152]{1,0:T(8,128)(2,1)} %get-tuple-element.54, bf16[1024,1728]{1,0:T(8,128)(2,1)} %get-tuple-element.55), kind=kOutput, calls=%fused_computation.4 | convolution fusion | flops 4078854144 | bytes 9879552 | tf_op jit(solution)/shard_map/dot_general | solution.py:21
  544.3 42.0 %collective-permute-done.33 = bf16[144,1152]{1,0:T(8,128)(2,1)S(1)} collective-permute-done((bf16[144,1152]{1,0:T(8,128)(2,1)S(1)}, bf16[144,1152]{1,0:T(8,128)(2,1)S(1)}, u32[]{:S(2)}, u32[]{:S(2)}) %collective-permute-start.33) | collective-permute-done | bytes 331808 | tf_op jit(solution)/shard_map/ppermute | solution.py:447
  627.5 19.4 %collective-permute-done.41 = bf16[2,72,2304]{2,1,0:T(8,128)(2,1)S(1)} collective-permute-done((bf16[2,72,2304]{2,1,0:T(8,128)(2,1)S(1)}, bf16[2,72,2304]{2,1,0:T(8,128)(2,1)S(1)}, u32[]{:S(2)}, u32[]{:S(2)}) %collective-permute-start.41) | collective-permute-done | bytes 663584 | tf_op jit(solution)/shard_map/ppermute | solution.py:447
  650.4 19.0 %collective-permute-done.42 = bf16[2,36,2304]{2,1,0:T(8,128)(2,1)S(1)} collective-permute-done((bf16[2,36,2304]{2,1,0:T(8,128)(2,1)S(1)}, bf16[2,36,2304]{2,1,0:T(8,128)(2,1)S(1)}, u32[]{:S(2)}, u32[]{:S(2)}) %collective-permute-start.42) | collective-permute-done | bytes 331808 | tf_op jit(solution)/shard_map/ppermute | solution.py:447
  670.2 21.3 %collective-permute-done.50 = bf16[144,1152]{1,0:T(8,128)(2,1)S(1)} collective-permute-done((bf16[144,1152]{1,0:T(8,128)(2,1)S(1)}, bf16[144,1152]{1,0:T(8,128)(2,1)S(1)}, u32[]{:S(2)}, u32[]{:S(2)}) %collective-permute-start.50) | collective-permute-done | bytes 331808 | tf_op jit(solution)/shard_map/ppermute | solution.py:447
  712.5 20.2 %collective-permute-done.21 = bf16[2,72,1728]{2,1,0:T(8,128)(2,1)S(1)} collective-permute-done((bf16[2,72,1728]{2,1,0:T(8,128)(2,1)S(1)}, bf16[2,72,1728]{2,1,0:T(8,128)(2,1)S(1)}, u32[]{:S(2)}, u32[]{:S(2)}) %collective-permute-start.21) | collective-permute-done | bytes 497696 | tf_op jit(solution)/shard_map/ppermute | solution.py:447
  739.4 17.1 %collective-permute-done.22 = bf16[2,36,1728]{2,1,0:T(8,128)(2,1)S(1)} collective-permute-done((bf16[2,36,1728]{2,1,0:T(8,128)(2,1)S(1)}, bf16[2,36,1728]{2,1,0:T(8,128)(2,1)S(1)}, u32[]{:S(2)}, u32[]{:S(2)}) %collective-permute-start.22) | collective-permute-done | bytes 248864 | tf_op jit(solution)/shard_map/ppermute | solution.py:447
  771.7 11.4 %collective-permute-done.25 = bf16[72,3456]{1,0:T(8,128)(2,1)S(1)} collective-permute-done((bf16[72,3456]{1,0:T(8,128)(2,1)S(1)}, bf16[72,3456]{1,0:T(8,128)(2,1)S(1)}, u32[]{:S(2)}, u32[]{:S(2)}) %collective-permute-start.25) | collective-permute-done | bytes 497696 | tf_op jit(solution)/shard_map/ppermute | solution.py:447
  795.3 23.8 %collective-permute-done.46 = bf16[144,4608]{1,0:T(8,128)(2,1)S(1)} collective-permute-done((bf16[144,4608]{1,0:T(8,128)(2,1)S(1)}, bf16[144,4608]{1,0:T(8,128)(2,1)S(1)}, u32[]{:S(2)}, u32[]{:S(2)}) %collective-permute-start.46) | collective-permute-done | bytes 1327136 | tf_op jit(solution)/shard_map/ppermute | solution.py:447
  822.6 16.0 %collective-permute-done.26 = bf16[144,3456]{1,0:T(8,128)(2,1)S(1)} collective-permute-done((bf16[144,3456]{1,0:T(8,128)(2,1)S(1)}, bf16[144,3456]{1,0:T(8,128)(2,1)S(1)}, u32[]{:S(2)}, u32[]{:S(2)}) %collective-permute-start.26) | collective-permute-done | bytes 995360 | tf_op jit(solution)/shard_map/ppermute | solution.py:447
  (438 shorter events, 365.0 us)
Async XLA Ops:
  4.8 50.4 %collective-permute-start.2 = (f32[54,128]{1,0:T(8,128)S(1)}, f32[54,128]{1,0:T(8,128)S(1)}, u32[]{:S(2)}, u32[]{:S(2)}) collective-permute-start(f32[54,128]{1,0:T(8,128)S(1)} %dynamic-slice_bitcast_fusion.9), channel_id=1, source_target_pairs={{0,1},{1,0},{2,3},{3,2},{4,5},{5,4},{6,7},{7,6},{8,9},{9,8},{10,11... | collective-permute-start | bytes 82952 | tf_op jit(solution)/shard_map/ppermute | solution.py:439
  5.7 73.3 %collective-permute-start.9 = (bf16[256,1152]{1,0:T(8,128)(2,1)}, bf16[256,1152]{1,0:T(8,128)(2,1)}, u32[]{:S(2)}, u32[]{:S(2)}) collective-permute-start(bf16[256,1152]{1,0:T(8,128)(2,1)} %dynamic-slice_bitcast_fusion.4), channel_id=1, source_target_pairs={{0,1},{1,0},{2,3},{3,2},{4,5},{5,4},{6,7},{7,6},{8,9},{9,8},{10,11... | collective-permute-start | bytes 1769480 | tf_op jit(solution)/shard_map/ppermute | solution.py:439
  7.1 74.4 %collective-permute-start = (bf16[256,1152]{1,0:T(8,128)(2,1)}, bf16[256,1152]{1,0:T(8,128)(2,1)}, u32[]{:S(2)}, u32[]{:S(2)}) collective-permute-start(bf16[256,1152]{1,0:T(8,128)(2,1)} %dynamic-slice_bitcast_fusion.5), channel_id=1, source_target_pairs={{0,1},{1,0},{2,3},{3,2},{4,5},{5,4},{6,7},{7,6},{8,9},{9,8},{10,11... | collective-permute-start | bytes 1769480 | tf_op jit(solution)/shard_map/ppermute | solution.py:439
  7.1 78.3 %collective-permute-start.7 = (bf16[288,1152]{1,0:T(8,128)(2,1)}, bf16[288,1152]{1,0:T(8,128)(2,1)}, u32[]{:S(2)}, u32[]{:S(2)}) collective-permute-start(bf16[288,1152]{1,0:T(8,128)(2,1)} %param.19), channel_id=1, source_target_pairs={{0,2},{1,3},{2,0},{3,1},{4,6},{5,7},{6,4},{7,5},{8,10},{9,11},{10,... | collective-permute-start | bytes 1990664 | tf_op jit(solution)/shard_map/ppermute | solution.py:443
  27.1 62.6 %collective-permute-start.4 = (bf16[288,1728]{1,0:T(8,128)(2,1)}, bf16[288,1728]{1,0:T(8,128)(2,1)}, u32[]{:S(2)}, u32[]{:S(2)}) collective-permute-start(bf16[288,1728]{1,0:T(8,128)(2,1)} %copy.62), channel_id=1, source_target_pairs={{0,2},{1,3},{2,0},{3,1},{4,6},{5,7},{6,4},{7,5},{8,10},{9,11},{10,... | collective-permute-start | bytes 2985992 | tf_op jit(solution)/shard_map/ppermute | solution.py:443
  79.0 88.2 %collective-permute-start.13 = (bf16[1152,1152]{1,0:T(8,128)(2,1)}, bf16[1152,1152]{1,0:T(8,128)(2,1)}, u32[]{:S(2)}, u32[]{:S(2)}) collective-permute-start(bf16[1152,1152]{1,0:T(8,128)(2,1)} %param.23), channel_id=1, source_target_pairs={{0,1},{1,0},{2,3},{3,2},{4,5},{5,4},{6,7},{7,6},{8,9},{9,8},{10,11... | collective-permute-start | bytes 7962632 | tf_op jit(solution)/shard_map/ppermute | solution.py:439
  81.5 54.0 %collective-permute-start.10 = (bf16[512,1152]{1,0:T(8,128)(2,1)}, bf16[512,1152]{1,0:T(8,128)(2,1)}, u32[]{:S(2)}, u32[]{:S(2)}) collective-permute-start(bf16[512,1152]{1,0:T(8,128)(2,1)} %pad_maximum_fusion.13), channel_id=1, source_target_pairs={{0,2},{1,3},{2,0},{3,1},{4,6},{5,7},{6,4},{7,5},{8,10},{9,11},{10,... | collective-permute-start | bytes 3538952 | tf_op jit(solution)/shard_map/ppermute | solution.py:443
  85.6 73.8 %collective-permute-start.1 = (bf16[512,1152]{1,0:T(8,128)(2,1)}, bf16[512,1152]{1,0:T(8,128)(2,1)}, u32[]{:S(2)}, u32[]{:S(2)}) collective-permute-start(bf16[512,1152]{1,0:T(8,128)(2,1)} %pad_maximum_fusion.12.x_ref), channel_id=1, source_target_pairs={{0,2},{1,3},{2,0},{3,1},{4,6},{5,7},{6,4},{7,5},{8,10},{9,11},{10,... | collective-permute-start | bytes 3538952 | tf_op jit(solution)/shard_map/ppermute | solution.py:443
  89.7 74.1 %collective-permute-start.8 = (bf16[2,288,1152]{2,1,0:T(8,128)(2,1)}, bf16[2,288,1152]{2,1,0:T(8,128)(2,1)}, u32[]{:S(2)}, u32[]{:S(2)}) collective-permute-start(bf16[2,288,1152]{2,1,0:T(8,128)(2,1)} %pad_maximum_fusion.9), channel_id=1, source_target_pairs={{0,1},{1,0},{2,3},{3,2},{4,5},{5,4},{6,7},{7,6},{8,9},{9,8},{10,11... | collective-permute-start | bytes 3981320 | tf_op jit(solution)/shard_map/ppermute | solution.py:439
  110.2 62.8 %collective-permute-start.5 = (bf16[2,288,1728]{2,1,0:T(8,128)(2,1)}, bf16[2,288,1728]{2,1,0:T(8,128)(2,1)}, u32[]{:S(2)}, u32[]{:S(2)}) collective-permute-start(bf16[2,288,1728]{2,1,0:T(8,128)(2,1)} %copy.65), channel_id=1, source_target_pairs={{0,1},{1,0},{2,3},{3,2},{4,5},{5,4},{6,7},{7,6},{8,9},{9,8},{10,11... | collective-permute-start | bytes 5971976 | tf_op jit(solution)/shard_map/ppermute | solution.py:439
  135.5 94.2 %collective-permute-start.12 = (bf16[2,288,2304]{2,1,0:T(8,128)(2,1)}, bf16[2,288,2304]{2,1,0:T(8,128)(2,1)}, u32[]{:S(2)}, u32[]{:S(2)}) collective-permute-start(bf16[2,288,2304]{2,1,0:T(8,128)(2,1)} %pad_maximum_fusion.5), channel_id=1, source_target_pairs={{0,1},{1,0},{2,3},{3,2},{4,5},{5,4},{6,7},{7,6},{8,9},{9,8},{10,11... | collective-permute-start | bytes 7962632 | tf_op jit(solution)/shard_map/ppermute | solution.py:439
  313.6 75.7 %collective-permute-start.16 = (bf16[1024,1152]{1,0:T(8,128)(2,1)S(1)}, bf16[1024,1152]{1,0:T(8,128)(2,1)S(1)}, u32[]{:S(2)}, u32[]{:S(2)}) collective-permute-start(bf16[1024,1152]{1,0:T(8,128)(2,1)S(1)} %copy-done.26), channel_id=1, source_target_pairs={{0,2},{1,3},{2,0},{3,1},{4,6},{5,7},{6,4},{7,5},{8,10},{9,11},{10,... | collective-permute-start | bytes 7077896 | tf_op jit(solution)/shard_map/ppermute | solution.py:443
  327.7 185.7 %collective-permute-start.47 = (bf16[1152,1152]{1,0:T(8,128)(2,1)}, bf16[1152,1152]{1,0:T(8,128)(2,1)}, u32[]{:S(2)}, u32[]{:S(2)}) collective-permute-start(bf16[1152,1152]{1,0:T(8,128)(2,1)} %constant_dynamic-slice_fusion.5), channel_id=1, source_target_pairs={{0,1},{1,0},{2,3},{3,2},{4,5},{5,4},{6,7},{7,6},{8,9},{9,8},{10,11... | collective-permute-start | bytes 7962632 | tf_op jit(solution)/shard_map/ppermute | solution.py:439
  353.4 167.9 %collective-permute-start.39 = (bf16[2,1,288,2304]{3,2,1,0:T(8,128)(2,1)}, bf16[2,1,288,2304]{3,2,1,0:T(8,128)(2,1)}, u32[]{:S(2)}, u32[]{:S(2)}) collective-permute-start(bf16[2,1,288,2304]{3,2,1,0:T(8,128)(2,1)} %constant_dynamic-slice_fusion.8), channel_id=1, source_target_pairs={{0,1},{1,0},{2,3},{3,2},{4,5},{5,4},{6,7},{7,6},{8,9},{9,8},{10,11... | collective-permute-start | bytes 7962632 | tf_op jit(solution)/shard_map/ppermute | solution.py:439
  451.8 85.3 %collective-permute-start.32 = (bf16[288,1152]{1,0:T(8,128)(2,1)}, bf16[288,1152]{1,0:T(8,128)(2,1)}, u32[]{:S(2)}, u32[]{:S(2)}) collective-permute-start(bf16[288,1152]{1,0:T(8,128)(2,1)} %constant_dynamic-slice_fusion.12), channel_id=1, source_target_pairs={{0,1},{1,0},{2,3},{3,2},{4,5},{5,4},{6,7},{7,6},{8,9},{9,8},{10,11... | collective-permute-start | bytes 1990664 | tf_op jit(solution)/shard_map/ppermute | solution.py:439
  451.8 152.2 %collective-permute-start.17 = (bf16[512,1152]{1,0:T(8,128)(2,1)}, bf16[512,1152]{1,0:T(8,128)(2,1)}, u32[]{:S(2)}, u32[]{:S(2)}) collective-permute-start(bf16[512,1152]{1,0:T(8,128)(2,1)} %get-tuple-element.90), channel_id=1, source_target_pairs={{0,2},{1,3},{2,0},{3,1},{4,6},{5,7},{6,4},{7,5},{8,10},{9,11},{10,... | collective-permute-start | bytes 3538952 | tf_op jit(solution)/shard_map/ppermute | solution.py:443
  507.8 116.4 %collective-permute-start.19 = (bf16[2,1,288,1728]{3,2,1,0:T(8,128)(2,1)}, bf16[2,1,288,1728]{3,2,1,0:T(8,128)(2,1)}, u32[]{:S(2)}, u32[]{:S(2)}) collective-permute-start(bf16[2,1,288,1728]{3,2,1,0:T(8,128)(2,1)} %constant_dynamic-slice_fusion.16), channel_id=1, source_target_pairs={{0,1},{1,0},{2,3},{3,2},{4,5},{5,4},{6,7},{7,6},{8,9},{9,8},{10,11... | collective-permute-start | bytes 5971976 | tf_op jit(solution)/shard_map/ppermute | solution.py:439
  519.8 96.2 %collective-permute-start.48 = (bf16[576,1152]{1,0:T(8,128)(2,1)}, bf16[576,1152]{1,0:T(8,128)(2,1)}, u32[]{:S(2)}, u32[]{:S(2)}) collective-permute-start(bf16[576,1152]{1,0:T(8,128)(2,1)} %constant_dynamic-slice_fusion.4), channel_id=1, source_target_pairs={{0,4},{4,0},{8,12},{12,8},{16,20},{20,16},{24,28},{28,24},{1,5},{5... | collective-permute-start | bytes 3981320 | tf_op jit(solution)/shard_map/ppermute | solution.py:447
  535.3 84.5 %collective-permute-start.40 = (bf16[2,144,2304]{2,1,0:T(8,128)(2,1)}, bf16[2,144,2304]{2,1,0:T(8,128)(2,1)}, u32[]{:S(2)}, u32[]{:S(2)}) collective-permute-start(bf16[2,144,2304]{2,1,0:T(8,128)(2,1)} %dynamic-slice_bitcast_fusion), channel_id=1, source_target_pairs={{0,4},{4,0},{8,12},{12,8},{16,20},{20,16},{24,28},{28,24},{1,5},{5... | collective-permute-start | bytes 3981320 | tf_op jit(solution)/shard_map/ppermute | solution.py:447
  542.2 44.0 %collective-permute-start.33 = (bf16[144,1152]{1,0:T(8,128)(2,1)S(1)}, bf16[144,1152]{1,0:T(8,128)(2,1)S(1)}, u32[]{:S(2)}, u32[]{:S(2)}) collective-permute-start(bf16[144,1152]{1,0:T(8,128)(2,1)S(1)} %constant_dynamic-slice_fusion.11), channel_id=1, source_target_pairs={{0,4},{4,0},{8,12},{12,8},{16,20},{20,16},{24,28},{28,24},{1,5},{5... | collective-permute-start | bytes 995336 | tf_op jit(solution)/shard_map/ppermute | solution.py:447
  627.0 76.8 %collective-permute-start.20 = (bf16[2,144,1728]{2,1,0:T(8,128)(2,1)S(1)}, bf16[2,144,1728]{2,1,0:T(8,128)(2,1)S(1)}, u32[]{:S(2)}, u32[]{:S(2)}) collective-permute-start(bf16[2,144,1728]{2,1,0:T(8,128)(2,1)S(1)} %dynamic-slice_bitcast_fusion.1), channel_id=1, source_target_pairs={{0,4},{4,0},{8,12},{12,8},{16,20},{20,16},{24,28},{28,24},{1,5},{5... | collective-permute-start | bytes 2985992 | tf_op jit(solution)/shard_map/ppermute | solution.py:447
  712.5 50.6 %collective-permute-start.45 = (bf16[72,4608]{1,0:T(8,128)(2,1)}, bf16[72,4608]{1,0:T(8,128)(2,1)S(1)}, u32[]{:S(2)}, u32[]{:S(2)}) collective-permute-start(bf16[72,4608]{1,0:T(8,128)(2,1)} %pad_maximum_fusion.18), channel_id=1, source_target_pairs={{0,8},{4,12},{8,0},{12,4},{16,24},{20,28},{24,16},{28,20},{1,9},{5... | collective-permute-start | bytes 1990664 | tf_op jit(solution)/shard_map/ppermute | solution.py:447
  771.0 48.1 %collective-permute-start.46 = (bf16[144,4608]{1,0:T(8,128)(2,1)S(1)}, bf16[144,4608]{1,0:T(8,128)(2,1)S(1)}, u32[]{:S(2)}, u32[]{:S(2)}) collective-permute-start(bf16[144,4608]{1,0:T(8,128)(2,1)S(1)} %pad_maximum_fusion.10), channel_id=1, source_target_pairs={{0,4},{4,0},{8,12},{12,8},{16,20},{20,16},{24,28},{28,24},{1,5},{5... | collective-permute-start | bytes 3981320 | tf_op jit(solution)/shard_map/ppermute | solution.py:447
  783.4 55.2 %collective-permute-start.26 = (bf16[144,3456]{1,0:T(8,128)(2,1)S(1)}, bf16[144,3456]{1,0:T(8,128)(2,1)S(1)}, u32[]{:S(2)}, u32[]{:S(2)}) collective-permute-start(bf16[144,3456]{1,0:T(8,128)(2,1)S(1)} %pad_maximum_fusion.17), channel_id=1, source_target_pairs={{0,4},{4,0},{8,12},{12,8},{16,20},{20,16},{24,28},{28,24},{1,5},{5... | collective-permute-start | bytes 2985992 | tf_op jit(solution)/shard_map/ppermute | solution.py:447
  (90 other events, 1244.8 us)

commit v2 on v1

v2 whole, which is shorter than its diff:
```python
import functools
import math

import jax
import jax.numpy as jnp
from jax import lax
from jax.experimental import pallas as pl
from jax.experimental.pallas import tpu as pltpu
from jax.sharding import PartitionSpec as P

GRID = 32
F32 = jnp.float32
LOW = jnp.bfloat16
TILE = 256
LANES = 128
MIB = 2**20
FEED_CHUNK = 1152
SHARES = 1
COST = 5e9


def dot(left, right, left_dim, right_dim):
    return lax.dot_general(
        left, right, (((left_dim,), (right_dim,)), ((), ())), preferred_element_type=F32
    )


def call(kernel, grid, in_specs, out_specs, out_shape, scratch=(), mib=56, us=5.0):
    return pl.pallas_call(
        kernel,
        grid_spec=pltpu.PrefetchScalarGridSpec(
            num_scalar_prefetch=1,
            grid=grid,
            in_specs=in_specs,
            out_specs=out_specs,
            scratch_shapes=list(scratch),
        ),
        out_shape=out_shape,
        cost_estimate=pl.CostEstimate(
            flops=int(us * COST), bytes_accessed=1024, transcendentals=0
        ),
        compiler_params=pltpu.CompilerParams(vmem_limit_bytes=mib * MIB),
    )


def shape(dims, kind=F32):
    return jax.ShapeDtypeStruct(dims, kind)


def whole(dims):
    return pl.BlockSpec(dims, lambda *_: (0,) * len(dims))


def tiles(width, index=lambda i, place: i):
    return pl.BlockSpec((TILE, width), lambda i, place: (index(i, place), 0))


BLOCK, CHIP, CORE = 0, 1, 2


def norm_rows(values):
    centered = values - jnp.mean(values, axis=-1, keepdims=True)
    variance = jnp.mean(centered * centered, axis=-1, keepdims=True)
    inverse = lax.rsqrt(variance + 1e-06)
    return centered * inverse, inverse


def norm_back(grad_normed, normed, inverse):
    first = jnp.mean(grad_normed, axis=-1, keepdims=True)
    second = jnp.mean(grad_normed * normed, axis=-1, keepdims=True)
    return inverse * (grad_normed - first - normed * second)


def column_sum(values):
    return jnp.sum(values.astype(F32), axis=0, keepdims=True)


def gather_rows(block, pieces, out_ref):
    rows = pieces[0].shape[0]
    for r, piece in enumerate(pieces):
        start = pl.multiple_of((block ^ r) * rows, 32)
        out_ref[pl.ds(start, rows), :] = piece[...]


def pack_kernel(parts, place_ref, w_ref, mine_ref, other_ref):
    half = w_ref.shape[1] // (2 * parts)
    for chip in range(2):

        @pl.when(place_ref[CHIP] == chip)
        def _(chip=chip):
            for part in range(parts):
                for out_ref, side in ((mine_ref, chip), (other_ref, 1 - chip)):
                    start = (2 * part + side) * half
                    out_ref[:, part * half : (part + 1) * half] = w_ref[:, start : start + half]


def pack_input(place, weight):
    rows, columns = weight.shape
    out = (rows, columns // 2)
    return call(
        functools.partial(pack_kernel, 3),
        (1,),
        [whole(weight.shape)],
        [whole(out)] * 2,
        [shape(out, LOW)] * 2,
        us=3.0,
    )(place, weight)


def pack_feed_kernel(place_ref, out_ref, own_ref, mine_ref):
    mine_ref[...] = jnp.where(pl.program_id(0) == 0, out_ref[...], own_ref[...])


def pack_feed(place, out_weight, expand_weight):
    rows, width = out_weight.shape
    return call(
        pack_feed_kernel,
        (3,),
        [
            whole(out_weight.shape),
            pl.BlockSpec(
                (rows, width), lambda i, place: (0, jnp.maximum(i - 1, 0) ^ place[BLOCK])
            ),
        ],
        pl.BlockSpec((rows, width), lambda i, place: (0, i)),
        shape((rows, 3 * width), LOW),
        us=3.0,
    )(place, out_weight, expand_weight)


def spread_kernel(side, place_ref, upper_ref, lower_ref, o_ref):
    row = lax.broadcasted_iota(jnp.int32, (side, LANES), 0)
    lane = lax.broadcasted_iota(jnp.int32, (side, LANES), 1) % side
    for line in range(upper_ref.shape[1]):
        upper = jnp.broadcast_to(upper_ref[0, line : line + 1], (side, LANES))
        lower = jnp.broadcast_to(lower_ref[0, line : line + 1], (side, LANES))
        upper = pltpu.roll(upper, 0, 1, stride=1, stride_axis=0)
        lower = pltpu.roll(lower, LANES - side, 1, stride=1, stride_axis=0)
        o_ref[0, line * side : (line + 1) * side] = jnp.where(lane >= row, upper, lower)


def spread_table(place, upper, lower, side):
    heads, count, _ = upper.shape
    block = pl.BlockSpec((1, count, LANES), lambda i, place: (i, 0, 0))
    return call(
        functools.partial(spread_kernel, side),
        (heads,),
        [block, block],
        pl.BlockSpec((1, count * side, LANES), lambda i, place: (i, 0, 0)),
        shape((heads, count * side, LANES)),
        us=6.0,
    )(place, upper, lower)


def fold_kernel(side, place_ref, g_ref, upper_ref, lower_ref):
    count = upper_ref.shape[1]
    lane = lax.broadcasted_iota(jnp.int32, (count, LANES), 1) % side
    for head in range(g_ref.shape[0]):
        upper = jnp.zeros((count, LANES), F32)
        every = jnp.zeros((count, LANES), F32)
        for row in range(side):
            line = g_ref[head, pl.ds(row, count, stride=side), :]
            if row:
                line = pltpu.roll(line, LANES - row, 1)
            every = every + line
            upper = upper + jnp.where(lane + row < side, line, 0.0)
        upper_ref[head] = upper
        lower_ref[head] = pltpu.roll(every - upper, side, 1)


def fold_table(place, grads, side):
    heads, rows, _ = grads.shape
    out = (heads, rows // side, LANES)
    return call(
        functools.partial(fold_kernel, side),
        (1,),
        [whole(grads.shape)],
        [whole(out)] * 2,
        [shape(out)] * 2,
        us=3.0,
    )(place, grads)


def project_kernel(
    parts,
    head_dim,
    place_ref,
    x0_ref,
    x1_ref,
    x2_ref,
    x3_ref,
    mod_ref,
    w0_ref,
    w1_ref,
    w2_ref,
    w3_ref,
    b_ref,
    x_ref,
    h_ref,
    o_ref,
    w_ref,
):
    step = pl.program_id(0)

    @pl.when(step == 0)
    def _():
        gather_rows(place_ref[BLOCK], (w0_ref, w1_ref, w2_ref, w3_ref), w_ref)

    piece = step ^ (2 * place_ref[CHIP])
    for r, ref in enumerate((x0_ref, x1_ref, x2_ref, x3_ref)):

        @pl.when(piece == r)
        def _(ref=ref):
            x_ref[...] = ref[...]

    normed, _ = norm_rows(x_ref[...].astype(F32))
    hidden = (normed * (1.0 + mod_ref[1:2]) + mod_ref[0:1]).astype(LOW)
    h_ref[...] = hidden
    low = (dot(hidden, w_ref[...], 1, 0) + b_ref[...]).astype(LOW)
    for part in range(parts):
        o_ref[part] = low[:, part * head_dim : (part + 1) * head_dim]


def project(place, pieces, mod, weights, bias, head_dim):
    width = pieces[0].shape[1]
    count = 4 * TILE
    columns = weights[0].shape[1]
    parts = columns // head_dim
    return call(
        functools.partial(project_kernel, parts, head_dim),
        (4,),
        [whole((TILE, width))] * 4
        + [whole(mod.shape)]
        + [whole(weights[0].shape)] * 4
        + [whole((1, columns))],
        [
            tiles(width),
            tiles(width),
            pl.BlockSpec((parts, TILE, head_dim), lambda i, place: (0, i, 0)),
        ],
        [
            shape((count, width), LOW),
            shape((count, width), LOW),
            shape((parts, count, head_dim), LOW),
        ],
        [pltpu.VMEM((width, columns), LOW)],
        us=12.0,
    )(place, *pieces, mod, *weights, bias)


def table_starts(core, tile, keys):
    last = keys // LANES - 1
    per = TILE // LANES
    starts = []
    for piece in range(per):
        row = []
        for key_tile in range(keys // TILE):
            apart = (key_tile ^ core) - (tile ^ core)
            row.append((last - piece + apart * per) * LANES)
        starts.append(row)
    return starts


def bias_tile(table_ref, head, starts):
    return jnp.concatenate(
        [
            jnp.concatenate([table_ref[head, start : start + TILE, :] for start in row], axis=0)
            for row in starts
        ],
        axis=1,
    )


def on_core(place_ref, body):
    for core in range(2):
        pl.when(place_ref[CORE] == core)(functools.partial(body, core))


def attend_kernel(first_tile, place_ref, *refs):
    on_core(place_ref, lambda core: attend_body(first_tile, core, *refs))


def attend_body(first_tile, core, q_ref, k_ref, v_ref, table_ref, o_ref, lse_ref):
    heads, count, head_dim = q_ref.shape
    scale = head_dim ** (-0.5)
    for tile in range(count // TILE):
        outs, logs = [], []
        starts = table_starts(core, first_tile + tile, k_ref.shape[1])
        span = slice(tile * TILE, (tile + 1) * TILE)
        for head in range(heads):
            scores = dot(k_ref[head], q_ref[head, span, :], 1, 1) * scale
            scores = scores + bias_tile(table_ref, head, starts)
            largest = jnp.max(scores, axis=0, keepdims=True)
            exponent = jnp.exp(scores - largest)
            total = jnp.sum(exponent, axis=0, keepdims=True)
            out = dot(v_ref[head], exponent.astype(LOW), 0, 0)
            outs.append(out / total)
            logs.append(largest + jnp.log(total))
        o_ref[:, span] = jnp.concatenate(outs, axis=0).astype(LOW)
        lse_ref[0, :, span] = jnp.concatenate(logs, axis=0)


def attend(place, parts, table, heads, pair, half):
    _, count, head_dim = parts.shape
    groups = heads // pair
    part_count = count // 2

    def head_block(first):
        return pl.BlockSpec(
            (pair, count, head_dim), lambda i, place, first=first: (first * groups + i, 0, 0)
        )

    return call(
        functools.partial(attend_kernel, half * (part_count // TILE)),
        (groups,),
        [
            pl.BlockSpec((pair, part_count, head_dim), lambda i, place: (i, half, 0)),
            head_block(1),
            head_block(2),
            pl.BlockSpec((pair,) + table.shape[1:], lambda i, place: (i, 0, 0)),
        ],
        [
            pl.BlockSpec((pair * head_dim, part_count), lambda i, place: (i, 0)),
            pl.BlockSpec((1, pair, part_count), lambda i, place: (i, 0, 0)),
        ],
        [shape((heads * head_dim, part_count), LOW), shape((groups, pair, part_count))],
        us=14.0,
    )(place, parts, parts, parts, table)


def attend_back_kernel(place_ref, *refs):
    on_core(place_ref, lambda core: attend_back_body(core, *refs))


def attend_back_body(
    core,
    q_ref,
    k_ref,
    v_ref,
    go0_ref,
    go1_ref,
    o0_ref,
    o1_ref,
    lse0_ref,
    lse1_ref,
    table_ref,
    gq_ref,
    gk_ref,
    gv_ref,
    gt_ref,
):
    heads, count, head_dim = q_ref.shape
    keys = k_ref.shape[1]
    scale = head_dim ** (-0.5)
    half_tiles = count // TILE // 2
    gt_ref[...] = jnp.zeros_like(gt_ref)
    for head in range(heads):
        key = k_ref[head]
        value = v_ref[head]
        grad_key = jnp.zeros((keys, head_dim), F32)
        grad_value = jnp.zeros((keys, head_dim), F32)
        for tile in range(count // TILE):
            go_ref, o_ref, lse_ref = (
                (go0_ref, o0_ref, lse0_ref) if tile < half_tiles else (go1_ref, o1_ref, lse1_ref)
            )
            inner = slice((tile % half_tiles) * TILE, (tile % half_tiles + 1) * TILE)
            span = slice(tile * TILE, (tile + 1) * TILE)
            starts = table_starts(core, tile, keys)
            query = q_ref[head, span, :]
            grad_out = go_ref[head, inner, :]
            scores = dot(key, query, 1, 1) * scale + bias_tile(table_ref, head, starts)
            probs = jnp.exp(scores - lse_ref[0, head : head + 1, inner])
            grad_probs = dot(value, grad_out, 1, 1)
            out = o_ref[head * head_dim : (head + 1) * head_dim, inner].astype(F32)
            row_dot = jnp.sum(out * grad_out.astype(F32).T, axis=0, keepdims=True)
            grad_scores = probs * (grad_probs - row_dot)
            for piece, row in enumerate(starts):
                for key_tile, start in enumerate(row):
                    gt_ref[head, start : start + TILE, :] += grad_scores[
                        key_tile * TILE : (key_tile + 1) * TILE,
                        piece * LANES : (piece + 1) * LANES,
                    ]
            low = grad_scores.astype(LOW)
            grad_value = grad_value + dot(probs.astype(LOW), grad_out, 1, 0)
            grad_key = grad_key + dot(low, query, 1, 0)
            gq_ref[head, span, :] = (dot(key, low, 0, 0) * scale).T.astype(LOW)
        gk_ref[head] = (grad_key * scale).astype(LOW)
        gv_ref[head] = grad_value.astype(LOW)


def attend_back(place, parts, grad_outs, attended, logs, table, heads, pair, share, at):
    _, count, head_dim = parts.shape
    groups = heads // pair
    steps = share // pair
    half = count // 2

    def head_block(first, rows=count):
        return pl.BlockSpec(
            (pair, rows, head_dim),
            lambda i, place: (first * groups + at * steps + i, 0, 0),
        )

    out_block = pl.BlockSpec((pair, count, head_dim), lambda i, place: (i, 0, 0))
    attended_block = pl.BlockSpec(
        (pair * head_dim, half), lambda i, place: (at * steps + i, 0)
    )
    log_block = pl.BlockSpec((1, pair, half), lambda i, place: (at * steps + i, 0, 0))
    table_dims = (pair,) + table.shape[1:]
    return call(
        attend_back_kernel,
        (steps,),
        [head_block(0), head_block(1), head_block(2)]
        + [head_block(0, half)] * 2
        + [attended_block] * 2
        + [log_block] * 2
        + [pl.BlockSpec(table_dims, lambda i, place: (at * steps + i, 0, 0))],
        [out_block] * 3 + [pl.BlockSpec(table_dims, lambda i, place: (i, 0, 0))],
        [shape((share, count, head_dim), LOW)] * 3 + [shape((share,) + table.shape[1:])],
        us=14.0,
    )(place, parts, parts, parts, *grad_outs, *attended, *logs, table)


def middle_kernel(
    first_tile,
    place_ref,
    own_ref,
    got_ref,
    w0_ref,
    w1_ref,
    w2_ref,
    w3_ref,
    ob_ref,
    x_ref,
    c0_ref,
    c1_ref,
    c2_ref,
    c3_ref,
    mod_ref,
    br_ref,
    mid_ref,
    h_ref,
    gb_ref,
    cot_ref,
    sum_ref,
    w_ref,
):
    step = pl.program_id(0)

    @pl.when(step == 0)
    def _():
        rows = w0_ref.shape[0]
        core = place_ref[CORE]
        for r, piece in enumerate((w0_ref, w1_ref, w2_ref, w3_ref)):
            start = pl.multiple_of(((core ^ (r % 2)) + 2 * (r // 2)) * rows, 32)
            w_ref[pl.ds(start, rows), :] = piece[...]
        sum_ref[...] = jnp.zeros_like(sum_ref)

    piece = (step + first_tile) ^ (2 * place_ref[CHIP])
    for r, ref in enumerate((c0_ref, c1_ref, c2_ref, c3_ref)):

        @pl.when(piece == r)
        def _(ref=ref):
            cot_ref[...] = ref[...]

    joined = jnp.concatenate([own_ref[...], got_ref[...]], axis=0)
    branch = dot(joined, w_ref[...], 0, 0) + ob_ref[...]
    middle = x_ref[...].astype(F32) + mod_ref[2:3] * branch
    normed, _ = norm_rows(middle)
    br_ref[...] = branch.astype(LOW)
    mid_ref[...] = middle
    h_ref[...] = (normed * (1.0 + mod_ref[4:5]) + mod_ref[3:4]).astype(LOW)
    grad = (mod_ref[5:6] * cot_ref[...].astype(F32)).astype(LOW)
    gb_ref[...] = grad
    sum_ref[...] += column_sum(grad)


def middle_part(place, own, got, weights, bias, tokens, cotangents, mod, half):
    width = tokens.shape[1]
    rows, count = own.shape
    first = half * (count // TILE)
    low, full = shape((count, width), LOW), shape((count, width))
    side = pl.BlockSpec((rows, TILE), lambda i, place: (0, i))
    return call(
        functools.partial(middle_kernel, first),
        (count // TILE,),
        [side, side]
        + [whole((width // 4, width))] * 4
        + [whole((1, width)), tiles(width, lambda i, place: i + first)]
        + [whole((TILE, width))] * 4
        + [whole(mod.shape)],
        [tiles(width)] * 5 + [whole((1, width))],
        [low, full, low, low, low, shape((1, width))],
        [pltpu.VMEM((width, width), LOW)],
        us=7.0,
    )(place, own, got, *weights, bias, tokens, *cotangents, mod)


def feed_kernel(
    place_ref,
    h_ref,
    g_ref,
    e0_ref,
    e1_ref,
    e2_ref,
    e3_ref,
    s0_ref,
    s1_ref,
    be_ref,
    act_ref,
    ge_ref,
    sum_ref,
    b2_ref,
    gh_ref,
    we_ref,
    b2_acc,
    gh_acc,
):
    step = pl.program_id(0)
    steps = pl.num_programs(0)
    gather_rows(place_ref[BLOCK], (e0_ref, e1_ref, e2_ref, e3_ref), we_ref)
    expand = we_ref[...]
    hidden, grad = h_ref[...], g_ref[...]
    shrink = jnp.where(step < steps // 2, s0_ref[...], s1_ref[...])
    inner = dot(hidden, expand, 1, 0) + be_ref[...]
    slope = math.sqrt(2.0 / math.pi)
    square = inner * inner
    bent = jnp.tanh(slope * (inner + 0.044715 * inner * square))
    act = (0.5 * inner * (1.0 + bent)).astype(LOW)
    act_ref[...] = act
    back = 0.5 * (1.0 + bent) + 0.5 * inner * (1.0 - bent * bent) * (
        slope * (1.0 + 3 * 0.044715 * square)
    )
    grad_inner = (dot(grad, shrink, 1, 1) * back).astype(LOW)
    ge_ref[...] = grad_inner
    sum_ref[...] = column_sum(grad_inner)

    @pl.when(step == 0)
    def _():
        b2_acc[...] = dot(act, shrink, 1, 0)
        gh_acc[...] = dot(grad_inner, expand, 1, 1)

    @pl.when(step > 0)
    def _():
        b2_acc[...] += dot(act, shrink, 1, 0)
        gh_acc[...] += dot(grad_inner, expand, 1, 1)

    @pl.when(step == steps - 1)
    def _():
        b2_ref[...] = b2_acc[...].astype(LOW)
        gh_ref[...] = gh_acc[...].astype(LOW)


def feed(place, hidden, grad, expands, shrinks, bias, chunk):
    count, width = hidden.shape
    rows = expands[0].shape[0]
    inner = 2 * shrinks[0].shape[0]
    steps = inner // chunk
    half = steps // 2
    skip = width // chunk
    straight = pl.BlockSpec((rows, chunk), lambda i, place: (0, i + skip))
    swapped = pl.BlockSpec((rows, chunk), lambda i, place: (0, (i + half) % steps + skip))
    columns = pl.BlockSpec((count, chunk), lambda i, place: (0, i))
    return call(
        feed_kernel,
        (steps,),
        [
            whole(hidden.shape),
            whole(grad.shape),
            straight,
            swapped,
            straight,
            swapped,
            pl.BlockSpec((chunk, width), lambda i, place: (jnp.minimum(i, half - 1), 0)),
            pl.BlockSpec((chunk, width), lambda i, place: (jnp.maximum(i - half, 0), 0)),
            pl.BlockSpec((1, chunk), lambda i, place: (0, i)),
        ],
        [
            columns,
            columns,
            pl.BlockSpec((1, chunk), lambda i, place: (0, i)),
            whole((count, width)),
            whole((count, width)),
        ],
        [
            shape((count, inner), LOW),
            shape((count, inner), LOW),
            shape((1, inner)),
            shape((count, width), LOW),
            shape((count, width), LOW),
        ],
        [pltpu.VMEM((width, chunk), LOW)] + [pltpu.VMEM((count, width), F32)] * 2,
        us=22.0,
    )(place, hidden, grad, *expands, *shrinks, bias)


def shrink_grad_kernel(place_ref, a0_ref, a1_ref, g0_ref, g1_ref, o_ref):
    total = dot(a0_ref[...], g0_ref[...], 0, 0) + dot(a1_ref[...], g1_ref[...], 0, 0)
    o_ref[...] = total.astype(LOW)


def shrink_grad(place, acts, grads, half, chunk=384):
    count, inner = acts[0].shape
    width = grads[0].shape[1]
    steps = inner // 2 // chunk
    columns = pl.BlockSpec((count, chunk), lambda i, place: (0, i + half * steps))
    return call(
        shrink_grad_kernel,
        (steps,),
        [columns] * 2 + [whole((count, width))] * 2,
        pl.BlockSpec((chunk, width), lambda i, place: (i, 0)),
        shape((inner // 2, width), LOW),
        us=5.0,
    )(place, *acts, *grads)


def expand_grad_kernel(place_ref, h0_ref, h1_ref, g0_ref, g1_ref, *refs):
    keeps, sends, acc_ref = refs[:2], refs[2:4], refs[4]
    acc_ref[...] = dot(h0_ref[...], g0_ref[...], 0, 0) + dot(h1_ref[...], g1_ref[...], 0, 0)
    rows = keeps[0].shape[0]
    for r in range(4):
        start = pl.multiple_of((place_ref[BLOCK] ^ r) * rows, 32)
        out_ref = (sends if r % 2 else keeps)[r // 2]
        out_ref[...] = acc_ref[pl.ds(start, rows), :].astype(LOW)


def expand_grad(place, hiddens, grads, chunk=384):
    count, width = hiddens[0].shape
    inner = grads[0].shape[1]
    steps = inner // chunk
    half = steps // 2
    rows = width // 4
    straight = pl.BlockSpec((rows, chunk), lambda i, place: (0, i))
    swapped = pl.BlockSpec((rows, chunk), lambda i, place: (0, (i + half) % steps))
    return call(
        expand_grad_kernel,
        (steps,),
        [whole((count, width))] * 2 + [pl.BlockSpec((count, chunk), lambda i, place: (0, i))] * 2,
        [straight] * 2 + [swapped] * 2,
        [shape((rows, inner), LOW)] * 4,
        [pltpu.VMEM((width, chunk), F32)],
        us=10.0,
    )(place, *hiddens, *grads)


def input_grad_kernel(place_ref, h_ref, gq_ref, gk_ref, gv_ref, *refs):
    step = pl.program_id(0)
    chunk = h_ref.shape[1]
    heads, _, head_dim = gq_ref.shape
    columns = 3 * heads * head_dim
    keep_ref, send_ref, joined_ref, acc_ref = refs[-4:]

    @pl.when(step == 0)
    def _():
        for side, ref in enumerate((gq_ref, gk_ref, gv_ref)):
            for head in range(heads):
                start = (side * heads + head) * head_dim
                joined_ref[:, start : start + head_dim] = ref[head]

    total = dot(h_ref[...], joined_ref[...], 0, 0)
    acc_ref[pl.ds(pl.multiple_of(step * chunk, chunk), chunk), :] = total

    @pl.when(step == pl.num_programs(0) - 1)
    def _():
        rows = keep_ref.shape[0]
        block = place_ref[BLOCK]
        for r in range(4):
            start = pl.multiple_of((block ^ r) * rows, 32)
            out_ref = send_ref if r % 2 else keep_ref
            at = (r // 2) * columns
            out_ref[:, at : at + columns] = acc_ref[pl.ds(start, rows), :].astype(LOW)

    if len(refs) > 4:
        a0_ref, a1_ref, g0_ref, g1_ref = refs[:4]

        @pl.when(step == 0)
        def _():
            out = dot(a0_ref[...], g0_ref[...], 1, 0) + dot(a1_ref[...], g1_ref[...], 1, 0)
            rows = keep_ref.shape[0]
            first, second = out[:rows].astype(LOW), out[rows:].astype(LOW)
            own = place_ref[CORE] == 0
            keep_ref[:, 2 * columns :] = jnp.where(own, first, second)
            send_ref[:, 2 * columns :] = jnp.where(own, second, first)


def input_grad(place, hidden, grads, extra=(), chunk=384):
    heads, count, head_dim = grads[0].shape
    width = hidden.shape[1]
    columns = 3 * heads * head_dim
    more = [*extra[0], *extra[1]] if extra else []
    out = (width // 4, 2 * columns + (width if extra else 0))
    return call(
        input_grad_kernel,
        (width // chunk,),
        [pl.BlockSpec((count, chunk), lambda i, place: (0, i))]
        + [whole((heads, count, head_dim))] * 3
        + [whole(one.shape) for one in more],
        [whole(out)] * 2,
        [shape(out, LOW)] * 2,
        [pltpu.VMEM((count, columns), LOW), pltpu.VMEM((width, columns), F32)],
        us=9.0 if extra else 6.0,
    )(place, hidden, *grads, *more)


def branch_back_kernel(
    head_dim,
    place_ref,
    own_ref,
    got_ref,
    mid_ref,
    cot_ref,
    br_ref,
    w0_ref,
    w1_ref,
    mod_ref,
    gm_ref,
    gb_ref,
    ga_ref,
    sum_ref,
    w_ref,
):
    @pl.when(pl.program_id(0) == 0)
    def _():
        rows = w0_ref.shape[0]
        core = place_ref[CORE]
        w_ref[pl.ds(pl.multiple_of(core * rows, 32), rows), :] = w0_ref[...]
        w_ref[pl.ds(pl.multiple_of((1 - core) * rows, 32), rows), :] = w1_ref[...]
        sum_ref[...] = jnp.zeros_like(sum_ref)

    grad_hidden = own_ref[...].astype(F32) + got_ref[...].astype(F32)
    normed, inverse = norm_rows(mid_ref[...])
    grad_middle = cot_ref[...].astype(F32) + norm_back(
        grad_hidden * (1.0 + mod_ref[4:5]), normed, inverse
    )
    gm_ref[...] = grad_middle
    grad_branch = (mod_ref[2:3] * grad_middle).astype(LOW)
    gb_ref[...] = grad_branch
    grad_att = dot(grad_branch, w_ref[...], 1, 1).astype(LOW)
    for part in range(ga_ref.shape[0]):
        ga_ref[part] = grad_att[:, part * head_dim : (part + 1) * head_dim]
    sum_ref[0:1] += column_sum(grad_hidden)
    sum_ref[1:2] += column_sum(grad_hidden * normed)
    sum_ref[2:3] += column_sum(grad_middle * br_ref[...].astype(F32))
    sum_ref[3:4] += column_sum(grad_branch)


def branch_back(place, own, got, middle, cotangent, branch, weights, mod, head_dim):
    count, width = own.shape
    rows = width // 2
    parts = rows // head_dim
    return call(
        functools.partial(branch_back_kernel, head_dim),
        (count // TILE,),
        [tiles(width)] * 5 + [whole((width // 4, width))] * 2 + [whole(mod.shape)],
        [
            tiles(width),
            tiles(width),
            pl.BlockSpec((parts, TILE, head_dim), lambda i, place: (0, i, 0)),
            whole((8, width)),
        ],
        [
            shape((count, width)),
            shape((count, width), LOW),
            shape((parts, count, head_dim), LOW),
            shape((8, width)),
        ],
        [pltpu.VMEM((rows, width), LOW)],
        us=7.0,
    )(place, own, got, middle, cotangent, branch, *weights, mod)


def project_back_kernel(groups, place_ref, *refs):
    part_refs = refs[: 3 * groups]
    w_refs = refs[3 * groups : 3 * groups + 4]
    x_ref, gh_ref, sum_ref, bias_ref, w_ref = refs[3 * groups + 4 :]

    @pl.when(pl.program_id(0) == 0)
    def _():
        gather_rows(place_ref[BLOCK], w_refs, w_ref)
        sum_ref[...] = jnp.zeros_like(sum_ref)
        bias_ref[...] = jnp.zeros_like(bias_ref)

    pieces = [ref[part] for ref in part_refs for part in range(ref.shape[0])]
    joined = jnp.concatenate(pieces, axis=1)
    grad_hidden = dot(joined, w_ref[...], 1, 1)
    gh_ref[...] = grad_hidden.astype(LOW)
    normed, _ = norm_rows(x_ref[...].astype(F32))
    sum_ref[0:1] += column_sum(grad_hidden)
    sum_ref[1:2] += column_sum(grad_hidden * normed)
    bias_ref[...] += column_sum(joined)


def project_back(place, parts, weights, tokens, far):
    width = tokens.shape[1]
    count = tokens.shape[0] // 2
    columns = weights[0].shape[1]
    pair, _, head_dim = parts[0].shape
    steps = count // TILE

    def index(i, place):
        return (place[CHIP] ^ far) * steps + i

    return call(
        functools.partial(project_back_kernel, len(parts) // 3),
        (steps,),
        [pl.BlockSpec((pair, TILE, head_dim), lambda i, place: (0, index(i, place), 0))]
        * len(parts)
        + [whole(weights[0].shape)] * 4
        + [tiles(width, index)],
        [tiles(width), whole((8, width)), whole((1, columns))],
        [
            shape((count, width), LOW),
            shape((8, width)),
            shape((1, columns)),
        ],
        [pltpu.VMEM((width, columns), LOW)],
        us=7.0,
    )(place, *parts, *weights, tokens)


def input_back_kernel(place_ref, own_ref, got_ref, x_ref, gm0_ref, gm1_ref, mod_ref, o_ref):
    grad_hidden = own_ref[...].astype(F32) + got_ref[...].astype(F32)
    normed, inverse = norm_rows(x_ref[...].astype(F32))
    grad_middle = jnp.where(place_ref[CHIP] == 0, gm0_ref[...], gm1_ref[...])
    grad = grad_middle + norm_back(grad_hidden * (1.0 + mod_ref[1:2]), normed, inverse)
    o_ref[0] = grad.astype(LOW)


def input_back(place, own, got, tokens, grad_middles, mod):
    count, width = own.shape
    steps = count // TILE
    return call(
        input_back_kernel,
        (steps,),
        [tiles(width)] * 2
        + [tiles(width, lambda i, place: place[CHIP] * steps + i)]
        + [tiles(width)] * 2
        + [whole(mod.shape)],
        pl.BlockSpec((1, TILE, width), lambda i, place: (i, 0, 0)),
        shape((steps, TILE, width), LOW),
        us=4.0,
    )(place, own, got, tokens, *grad_middles, mod)


def result_kernel(
    place_ref,
    b0_ref,
    b1_ref,
    got_ref,
    mid0_ref,
    mid1_ref,
    cot0_ref,
    cot1_ref,
    bias_ref,
    mod_ref,
    o_ref,
    sum_ref,
):
    @pl.when(pl.program_id(0) == 0)
    def _():
        sum_ref[...] = jnp.zeros_like(sum_ref)

    def own(one, two):
        return jnp.where(place_ref[CHIP] == 0, one[...].astype(F32), two[...].astype(F32))

    branch = own(b0_ref, b1_ref) + got_ref[...].astype(F32) + bias_ref[...]
    o_ref[0] = (own(mid0_ref, mid1_ref) + mod_ref[5:6] * branch).astype(LOW)
    sum_ref[0:1] += column_sum(own(cot0_ref, cot1_ref) * branch)


def result_part(place, branches, got, middles, cotangents, bias, mod):
    count, width = got.shape
    steps = count // TILE
    return call(
        result_kernel,
        (steps,),
        [tiles(width)] * 7 + [whole((1, width)), whole(mod.shape)],
        [pl.BlockSpec((1, TILE, width), lambda i, place: (i, 0, 0)), whole((8, width))],
        [shape((steps, TILE, width), LOW), shape((8, width))],
        us=4.0,
    )(place, *branches, got, *middles, *cotangents, bias, mod)


def finish_expand_kernel(place_ref, own_ref, far_ref, o_ref):
    near = (pl.program_id(0) ^ place_ref[BLOCK]) < 2
    o_ref[...] = jnp.where(near, own_ref[...].astype(F32), far_ref[...].astype(F32))


def finish_expand(place, own, far):
    rows, columns = own.shape
    width = columns // 2
    block = pl.BlockSpec((rows, width), lambda i, place: (0, (i ^ place[BLOCK]) % 2))
    return call(
        finish_expand_kernel,
        (4,),
        [block, block],
        pl.BlockSpec((rows, width), lambda i, place: (0, i)),
        shape((rows, 2 * columns)),
        us=3.0,
    )(place, own, far)


def finish_input_kernel(place_ref, *refs):
    grads, o_ref = refs[:-1], refs[-1]
    shares = len(grads)
    part_width = o_ref.shape[1] // (6 * shares)
    for chip in range(2):

        @pl.when(place_ref[CHIP] == chip)
        def _(chip=chip):
            for share, g_ref in enumerate(grads):
                for side in range(2):
                    for part in range(3):
                        start = (side * 3 + part) * part_width
                        to = ((part * 2 + (side ^ chip)) * shares + share) * part_width
                        o_ref[:, to : to + part_width] = g_ref[:, start : start + part_width].astype(F32)


def finish_input(place, grads, columns):
    rows = grads[0].shape[0]
    out = (rows, columns)
    return call(
        finish_input_kernel,
        (1,),
        [whole(grad.shape) for grad in grads],
        whole(out),
        shape(out),
        us=3.0,
    )(place, *grads)


def swap_block(value, bits):
    return lax.ppermute(value, "blk", [(i, i ^ bits) for i in range(4)])


def swap_core(value):
    return swap_block(value, 1)


def swap_chip(value):
    return swap_block(value, 2)


def ordered(mine, other, place, axis=0):
    first = jnp.where(place == 0, mine, other)
    second = jnp.where(place == 0, other, mine)
    return jnp.concatenate([first, second], axis=axis)


def add_low(one, two):
    return (one.astype(F32) + two.astype(F32)).astype(LOW)


def stages():
    count = lax.axis_size("grp")
    bits = [1 << i for i in range(count.bit_length() - 1)]
    return [bits[:1]] + [bits[i : i + 2] for i in range(1, len(bits), 2)]


def stage_place(stage):
    at = 0
    for bit in stage:
        own = lax.axis_index("blk") % 2 if bit == 0 else (lax.axis_index("grp") // bit) % 2
        at = 2 * at + own
    return at


def swap_stage(values, stage):
    groups, size = lax.axis_size("grp"), lax.axis_size("blk")
    got = [values[0]]
    for mask in range(1, 1 << len(stage)):
        chosen = [bit for i, bit in enumerate(stage) if mask >> (len(stage) - 1 - i) & 1]
        core_flip = int(0 in chosen)
        group_flip = sum(chosen)
        if group_flip and core_flip:
            pairs = [
                (g * size + i, (g ^ group_flip) * size + (i ^ 1))
                for g in range(groups)
                for i in range(size)
            ]
            got.append(lax.ppermute(values[mask], ("grp", "blk"), pairs))
        elif group_flip:
            pairs = [(g, g ^ group_flip) for g in range(groups)]
            got.append(lax.ppermute(values[mask], "grp", pairs))
        else:
            got.append(swap_core(values[mask]))
    return got


def scatter_stage(value, stage, axis):
    place = stage_place(stage)
    size = value.shape[axis] >> len(stage)
    cut = [
        lax.dynamic_slice_in_dim(value, (place ^ mask) * size, size, axis)
        for mask in range(1 << len(stage))
    ]
    return sum(one.astype(F32) for one in swap_stage(cut, stage)).astype(LOW)


def gather_stage(value, stage, axis=0):
    place = stage_place(stage)
    count = 1 << len(stage)
    got = swap_stage([value] * count, stage)
    parts = []
    for at in range(count):
        part = got[count - 1]
        for mask in range(count - 1):
            part = jnp.where(place == at ^ mask, got[mask], part)
        parts.append(part)
    return jnp.concatenate(parts, axis=axis)


def total_stage(value, stage):
    return sum(swap_stage([value] * (1 << len(stage)), stage))


class Far:
    def __init__(self, share):
        self.value = swap_chip(share)
        self.left = stages()

    @staticmethod
    def share_of(value):
        rows = value.shape[0] // lax.axis_size("grp")
        at = 0
        for stage in stages():
            at = (at << len(stage)) + stage_place(stage)
        return lax.dynamic_slice_in_dim(value, at * rows, rows, 0)

    def gather(self):
        if self.left:
            self.value = gather_stage(self.value, self.left.pop())


def after(value, *others):
    return lax.optimization_barrier((value, *others))[0]


class Sum:
    def __init__(self, keep, send, columns):
        self.value = add_low(keep, swap_core(send))
        self.columns = columns
        self.down = stages()
        self.up = []

    def step(self):
        if self.down:
            stage = self.down.pop(0)
            self.value = scatter_stage(self.value, stage, 0)
            self.up.append(stage)
            if not self.down:
                self.far = swap_chip(self.value[:, self.columns : 2 * self.columns])
        elif self.up:
            if self.far is not None:
                self.value = lax.dynamic_update_slice_in_dim(
                    self.value, self.far, self.columns, 1
                )
                self.far = None
            self.value = gather_stage(self.value, self.up.pop())
        return self.value

    def finish(self):
        while self.down or self.up:
            self.step()
        return self.value


def table_lines(table, side):
    span = 2 * side - 1
    per = LANES // side
    heads = table.shape[1]
    count = 2 * side - per
    flipped = table.T.reshape(heads, span, span)[:, ::-1]
    lines = [flipped[:, per - 1 - k : per - 1 - k + count] for k in range(per)]
    upper = jnp.concatenate([line[:, :, side - 1 :] for line in lines], axis=2)
    lower = jnp.concatenate(
        [jnp.pad(line[:, :, : side - 1], ((0, 0), (0, 0), (1, 0))) for line in lines], axis=2
    )
    return upper, lower


def table_from_lines(upper, lower, side):
    span = 2 * side - 1
    per = LANES // side
    heads, count, _ = upper.shape
    total = 0.0
    for k in range(per):
        line = jnp.concatenate(
            [lower[:, :, k * side + 1 : (k + 1) * side], upper[:, :, k * side : (k + 1) * side]],
            axis=2,
        )
        before = per - 1 - k
        total = total + jnp.pad(line, ((0, 0), (before, span - count - before), (0, 0)))
    return total[:, ::-1].reshape(heads, span * span)


def embedding(step_values, width):
    half_width = width // 2
    frequency = jnp.exp(-math.log(10000.0) * jnp.arange(half_width, dtype=F32) / half_width)
    angles = step_values.astype(F32)[:, None] * frequency[None, :]
    return jnp.concatenate([jnp.cos(angles), jnp.sin(angles)], axis=-1)


def pick(value, place, axis=0):
    return lax.dynamic_index_in_dim(value, place, axis, keepdims=False)


def shards(
    images,
    cotangent,
    timestep,
    input_weight,
    input_bias,
    output_weight,
    output_bias,
    expand_weight,
    expand_bias,
    shrink_weight,
    shrink_bias,
    modulate_weight,
    modulate_bias,
    position_table,
):
    width = images.shape[2]
    heads_all = position_table.shape[1]
    head_dim = width // heads_all
    heads = heads_all // 2
    pair = 2
    own_rows = modulate_weight.shape[0]
    block = lax.axis_index("blk").astype(jnp.int32)
    chip, core = block // 2, block % 2
    place = jnp.stack([block, chip, core])

    condition = jax.nn.silu(embedding(timestep, width)).astype(LOW)
    condition_own = lax.dynamic_slice_in_dim(condition, block * own_rows, own_rows, 1)
    partial = jnp.dot(condition_own, modulate_weight, preferred_element_type=F32)
    partial = partial.reshape(2, -1, LANES)
    partial_mine, partial_other = pick(partial, core), pick(partial, 1 - core)
    summed = (partial_mine + swap_block(partial_other, 1)) + (
        swap_block(partial_mine, 2) + swap_block(partial_other, 3)
    )
    mod = (summed.reshape(-1) + modulate_bias).reshape(6, width)

    out_share, expand_share = Far.share_of(output_weight), Far.share_of(expand_weight)
    far = Far(
        jnp.concatenate(
            [out_share]
            + [
                lax.dynamic_slice_in_dim(expand_share, (block ^ bits) * width, width, 1)
                for bits in (2, 3)
            ],
            axis=1,
        )
    )

    in_mine, in_other = pack_input(place, after(input_weight, partial_mine))
    in_far = swap_chip(in_other)

    def mine_and_other(value):
        return pick(value, core), pick(value, 1 - core)

    token_mine, token_other = mine_and_other(after(images, partial_mine))
    token_pieces = (
        token_mine,
        swap_block(token_other, 1),
        swap_block(token_mine, 2),
        swap_block(token_other, 3),
    )
    in_mine_got = swap_core(after(in_mine, token_pieces[1], summed))
    feed_mine = pack_feed(place, after(output_weight, in_mine), expand_weight)
    feed_mine_got = swap_core(after(feed_mine, in_mine_got))
    far.gather()
    weights_in = (in_mine, in_mine_got, in_far, swap_core(after(in_far, feed_mine_got)))

    def own_half(vector):
        size = vector.shape[0] // 2
        return lax.dynamic_slice_in_dim(vector, chip * size, size, 0)

    bias_in = jnp.concatenate(
        [
            own_half(input_bias[:width]),
            jnp.zeros((width // 2,), F32),
            own_half(input_bias[width:]),
        ]
    )[None]
    expand_bias_blocks = expand_bias.reshape(4, -1)
    bias_expand = jnp.concatenate(
        [pick(expand_bias_blocks, block), pick(expand_bias_blocks, block ^ 1)]
    )[None]
    upper, lower = table_lines(
        lax.dynamic_slice_in_dim(position_table, chip * heads, heads, 1), GRID
    )
    table = spread_table(place, upper, lower, GRID)

    tokens, hidden_one, parts = project(
        place,
        token_pieces,
        after(mod, feed_mine_got, far.value, table),
        weights_in,
        bias_in,
        head_dim,
    )
    far.gather()
    cot_mine, cot_other = mine_and_other(after(cotangent, token_pieces[2], token_pieces[3]))
    cot_pieces = (
        cot_mine,
        swap_block(cot_other, 1),
        swap_block(cot_mine, 2),
        swap_block(cot_other, 3),
    )
    attended, logs = [None, None], [None, None]
    attended[0], logs[0] = attend(
        place, after(parts, cot_pieces[1]), table, heads, pair, 0
    )
    far.gather()
    shrink_got = swap_core(after(shrink_weight, cot_pieces[1]))
    weights_shrink = (shrink_weight, shrink_got)
    attended_got = [swap_chip(attended[0]), None]
    attended[1], logs[1] = attend(
        place, after(parts, shrink_got, far.value, attended[0]), table, heads, pair, 1
    )
    attended_got[1] = swap_chip(attended[1])
    weights_feed = (feed_mine, feed_mine_got, far.value, swap_core(far.value))

    def forward_half(half, attended_half):
        one = middle_part(
            place,
            attended_half,
            attended_got[half],
            weights_feed,
            output_bias[None],
            tokens,
            cot_pieces,
            mod,
            half,
        )
        two = feed(
            place, one[2], one[3], weights_feed, weights_shrink, bias_expand, FEED_CHUNK
        )
        return one + two

    forward = [forward_half(0, attended[0])]
    grad_hidden_two_got = [swap_chip(forward[0][-1])]
    forward.append(forward_half(1, after(attended[1], forward[0][-1])))
    grad_hidden_two_got.append(swap_chip(forward[1][-1]))
    (
        branch_one,
        middle,
        hidden_two,
        grad_branch_two,
        cots,
        shrink_sums,
        activated,
        grad_expanded,
        expand_sums,
        branch_two,
        grad_hidden_two,
    ) = zip(*forward)

    shrink_send = shrink_grad(
        place, (after(activated[0], grad_hidden_two_got[0]), activated[1]), grad_branch_two, 1
    )
    shrink_keep = shrink_grad(place, activated, grad_branch_two, 0)
    shrink_own = add_low(shrink_keep, swap_core(shrink_send))
    expand_keep0, expand_keep1, expand_send0, expand_send1 = expand_grad(
        place, (after(hidden_two[0], shrink_keep), hidden_two[1]), grad_expanded
    )
    expand_own = add_low(expand_keep0, swap_core(expand_send0))
    expand_far = add_low(expand_keep1, swap_core(expand_send1))
    total_shrink, total_own, total_far = lax.psum((shrink_own, expand_own, expand_far), "grp")

    def branch_half(half, *others):
        return branch_back(
            place,
            grad_hidden_two[half],
            grad_hidden_two_got[half],
            after(middle[half], *others),
            cots[half],
            branch_one[half],
            weights_feed[:2],
            mod,
            head_dim,
        )

    grad_middle, grad_branch_one, grad_attended, sums_two = zip(
        branch_half(0, shrink_own), branch_half(1, expand_own, expand_far)
    )
    branch_two_send = jnp.where(chip == 0, branch_two[1], branch_two[0])

    def attend_share(at, *others):
        return attend_back(
            place,
            after(parts, *others),
            grad_attended,
            attended,
            logs,
            table,
            heads,
            pair,
            heads // SHARES,
            at,
        )

    share_columns = width * 3 // (2 * SHARES)
    share = attend_share(0)
    branch_two_got = swap_chip(after(branch_two_send, share[0]))
    keep, send = input_grad(
        place, hidden_one, share[:3], (attended, grad_branch_one), 384
    )
    input_total = Sum(keep, send, share_columns)
    grad_parts, table_grads = share[:3], share[3:]
    grad_hidden_far, sums_far, bias_far = project_back(
        place, grad_parts, weights_in, after(tokens, input_total.value), 1
    )
    input_total.step()
    grad_hidden_got = swap_chip(grad_hidden_far)
    grad_hidden_own, sums_own, bias_own = project_back(
        place, grad_parts, weights_in, after(tokens, grad_hidden_far), 0
    )
    result_half, gate_sums = result_part(
        place,
        branch_two,
        branch_two_got,
        middle,
        cots,
        shrink_bias[None],
        after(mod, grad_hidden_own),
    )
    grad_tokens = input_back(
        place, grad_hidden_own, grad_hidden_got, tokens, grad_middle, mod
    )

    def to_blocks(value):
        return ordered(value[0][None], swap_core(value[1])[None], core)

    result = to_blocks(result_half)
    grad_images = to_blocks(grad_tokens)
    total_shrink = total_shrink.astype(F32)
    total_expand = finish_expand(place, total_own, swap_chip(total_far))
    totals = [input_total.finish()]
    total_input = finish_input(place, totals, 3 * width)
    total_output = totals[0][:, 2 * share_columns :].astype(F32)

    half_width = width // 2
    folded = [fold_table(place, grads, GRID) for grads in table_grads]
    table_vector = table_from_lines(
        jnp.concatenate([one for one, _ in folded]),
        jnp.concatenate([two for _, two in folded]),
        GRID,
    )
    projected_bias = (bias_far + bias_own)[0]
    expand_sum = (expand_sums[0] + expand_sums[1]).reshape(2, -1)
    split_vector = jnp.concatenate(
        [
            table_vector.reshape(-1),
            projected_bias[:half_width],
            projected_bias[2 * half_width :],
            ordered(expand_sum[0], expand_sum[1], core),
        ]
    )
    sums_two = sums_two[0] + sums_two[1]
    both_vector = jnp.concatenate([sums_two[3], (shrink_sums[0] + shrink_sums[1])[0]])
    split_rows = -(-split_vector.shape[0] // LANES)
    split_vector_padded = jnp.pad(split_vector, (0, split_rows * LANES - split_vector.shape[0]))
    small = jnp.concatenate([split_vector_padded, both_vector]).reshape(-1, LANES)
    ends = stages()
    ends[0] = ends[0] + [0]
    for stage in ends:
        small = total_stage(small, stage)
    small_own = small[:split_rows]
    small_two = ordered(small_own[None], swap_chip(small_own)[None], chip).reshape(2, -1)
    table_size = table_vector.size
    table_total = small_two[:, :table_size].reshape(heads_all, -1).T
    at = table_size
    bias_query = small_two[:, at : at + half_width]
    bias_value = small_two[:, at + half_width : at + 2 * half_width]
    at = at + 2 * half_width
    bias_expand_total = small_two[:, at : at + expand_sum.size].reshape(-1)
    bias_input_total = jnp.stack([bias_query, bias_value]).reshape(-1)
    both = small[split_rows:].reshape(2, width)

    def own_part(vector):
        size = vector.shape[0] // 4
        return lax.dynamic_slice_in_dim(vector, block * size, size, 0)

    sums_one = sums_far + sums_own
    split_sums = jnp.stack([sums_one[0], sums_one[1], gate_sums[0]]).reshape(-1, LANES)
    split_sums = (split_sums + swap_chip(split_sums)).reshape(3, width)
    image_row = jnp.concatenate(
        [
            split_sums[0],
            split_sums[1],
            sums_two[2],
            sums_two[0],
            sums_two[1],
            split_sums[2],
            pick(condition, core).astype(F32),
        ]
    ).astype(LOW)
    rows = image_row.reshape(1, -1, LANES)
    for stage in ends:
        rows = gather_stage(rows, stage if 0 in stage else stage[::-1])
    rows = rows.reshape(rows.shape[0], -1)
    grads_all, conditions = rows[:, : 6 * width], rows[:, 6 * width :]
    conditions_own = lax.dynamic_slice_in_dim(conditions, block * own_rows, own_rows, 1)
    modulate_grad = dot(conditions_own, grads_all, 0, 0)
    modulate_bias_grad = own_part(jnp.sum(grads_all.astype(F32), axis=0))

    return (
        result,
        grad_images,
        total_input,
        own_part(bias_input_total),
        total_output,
        own_part(both[0]),
        total_expand,
        own_part(bias_expand_total),
        total_shrink,
        own_part(both[1]),
        modulate_grad,
        modulate_bias_grad,
        table_total,
    )


def solution(mesh):
    return jax.shard_map(
        shards,
        mesh=mesh,
        in_specs=(
            P("grp", "blk", None),
            P("grp", "blk", None),
            P("grp"),
            P("blk", None),
            P(),
            P("blk", None),
            P(),
            P("blk", None),
            P(),
            P("blk", None),
            P(),
            P("blk", None),
            P(),
            P(),
        ),
        out_specs=(
            P("grp", "blk", None),
            P("grp", "blk", None),
            P("blk", None),
            P("blk"),
            P("blk", None),
            P("blk"),
            P("blk", None),
            P("blk"),
            P("blk", None),
            P("blk"),
            P("blk", None),
            P("blk"),
            P(),
        ),
        check_vma=False,
    )
```

time: 853 us -> 592 us (0.69)
  waiting for transfers between devices: 377 us -> 181 us
  Pallas kernels: 145 us -> 263 us
  local copies, waits for them, and re-layouts: 132 us -> 32.5 us
  matrix products: 51 us -> 7.5 us
  other arithmetic: 75.6 us -> 32.9 us
  between operations: 2.74 us -> 15.2 us
  starting transfers between devices: 58.2 us -> 48.7 us
    ppermute x59 -> x56, waiting for transfers between devices: 377 us -> 181 us  [the longest x20 157 us: swap_stage(): got.append(lax.ppermute(values[mask], 'grp', pairs))]
    pallas_call x7 -> x22, Pallas kernels: 133 us -> 247 us  [the longest x2 45.2 us: feed(): call(feed_kernel, (steps,), [whole(hidden.shape), whole(grad.shape), stra...]
    dot_general x5 -> x1, matrix products: 33.2 us -> 4.55 us  [dot(): lax.dot_general(left, right, (((left_dim,), (right_dim,)), ((), ())), pre...]
    select_n x32 -> x2, other arithmetic: 24.6 us -> 1.3 us  [ordered(): first = jnp.where(place == 0, mine, other)]
    reshape x12 -> x5, local copies, waits for them, and re-layouts: 22.4 us -> 0.41 us  [the longest x1 0.29 us: table_lines(): flipped = table.T.reshape(heads, span, span)[:, ::-1]]
    concatenate x28 -> x3, other arithmetic: 22.3 us -> 2.5 us  [ordered(): return jnp.concatenate([first, second], axis=axis)]
    unnamed x118 -> x81, local copies, waits for them, and re-layouts: 23.3 us -> 8.11 us
    dot_general x2 -> x0, matrix products: 14.9 us -> none  [the longest x1 9.43 us: gather_table(): lax.dot_general(flat, table_picks(grid_side), (((1,), (1,)), ((), ())), p...]
  transfers between devices with their start and end apart: 59 -> 57, of which waited for: 32 -> 24; matrix products, arithmetic and copies ran while one was open for 28% -> 10% of each run, Pallas kernels for 11% -> 44%
where the time goes in v2:
time: 592 us; the launch traced here: 582 us
  Pallas kernels  263 us (44%)
  waiting for transfers between devices  181 us (31%)
  starting transfers between devices  48.7 us (8%)
  other arithmetic  32.9 us (6%)
  local copies, waits for them, and re-layouts  32.5 us (5%)
  between operations  15.2 us (3%)
  matrix products  7.5 us (1%)
    ppermute x20, waiting for transfers between devices, swap_stage(): got.append(lax.ppermute(values[mask], 'grp', pairs))  157 us
    pallas_call x2, Pallas kernels, feed(): call(feed_kernel, (steps,), [whole(hidden.shape), whole(grad.shape), stra...  45.2 us
    pallas_call x2, Pallas kernels, attend(): call(functools.partial(attend_kernel, half * (part_count // TILE)), (grou...  31 us
    pallas_call x1, Pallas kernels, attend_back(): call(attend_back_kernel, (steps,), [head_block(0), head_block(1), head_bl...  27.2 us
    ppermute x20, starting transfers between devices, swap_stage(): got.append(lax.ppermute(values[mask], 'grp', pairs))  26 us
    ppermute x34, waiting for transfers between devices, swap_block(): return lax.ppermute(value, 'blk', [(i, i ^ bits) for i in range(4)])  23.3 us
    ppermute x34, starting transfers between devices, swap_block(): return lax.ppermute(value, 'blk', [(i, i ^ bits) for i in range(4)])  21.5 us
    pallas_call x1, Pallas kernels, input_grad(): call(input_grad_kernel, (width // chunk,), [pl.BlockSpec((count, chunk),...  17.9 us
  transfers between devices with their start and end apart: 57, of which 24 were waited for; matrix products, arithmetic and copies ran while one was open for 10% of the time, Pallas kernels for 44%

profile of v2, /device:TPU:16, one launch (start us, length us, event | category | flops | bytes accessed | tf_op | source)
XLA Modules:
  0.0 581.5 jit_solution(5662228804839225022)
XLA Ops:
  64.7 8.5 %shard_map.239.refs_3_.refs_9_ = f32[8,1920,128]{2,1,0:T(8,128)} custom-call(s32[3]{0:T(128)} %pad_add_fusion.place_ref, f32[8,60,128]{2,1,0:T(8,128)} %get-tuple-element.251.upper_ref, f32[8,60,128]{2,1,0:T(8,128)} %get-tuple-element.250.lower_ref), custom_call_target="tpu_custom_call" | custom-call | flops 30000001024 | bytes 1024 | tf_op jit(solution)/shard_map/pallas_call | solution.py:145
  93.0 13.2 %shard_map.240 = (bf16[1024,1152]{1,0:T(8,128)(2,1)}, bf16[1024,1152]{1,0:T(8,128)(2,1)}, bf16[24,1024,72]{2,1,0:T(8,128)(2,1)}) custom-call(s32[3]{0:T(128)} %pad_add_fusion.place_ref, bf16[256,1152]{1,0:T(8,128)(2,1)} %get-tuple-element.207.x0_ref, bf16[256,1152]{1,0:T(8,128)(2,1)} %collective-permute-done.x1_ref, bf16[256,1152]{1,0:T(8,128)(2,1)} %copy-done.37, ...), custom_call_target="tpu_custom_call" | custom-call | flops 60000002048 | bytes 1024 | tf_op jit(solution)/shard_map/pallas_call | solution.py:229
  106.2 15.5 %shard_map.241 = (bf16[576,512]{1,0:T(8,128)(2,1)}, f32[4,2,512]{2,1,0:T(2,128)}) custom-call(s32[3]{0:T(128)} %pad_add_fusion.place_ref, bf16[24,1024,72]{2,1,0:T(8,128)(2,1)} %get-tuple-element.110.refs_0_.refs_1_.refs_2_, bf16[24,1024,72]{2,1,0:T(8,128)(2,1)} %get-tuple-element.110.refs_0_.refs_1_.refs_2_, ...), custom_call_target="tpu_custom_call" | custom-call | flops 70000001024 | bytes 1024 | tf_op jit(solution)/shard_map/pallas_call | solution.py:313
  122.9 15.5 %shard_map.244 = (bf16[576,512]{1,0:T(8,128)(2,1)}, f32[4,2,512]{2,1,0:T(2,128)}) custom-call(s32[3]{0:T(128)} %pad_add_fusion.place_ref, bf16[24,1024,72]{2,1,0:T(8,128)(2,1)} %get-tuple-element.110.refs_0_.refs_1_.refs_2_, bf16[24,1024,72]{2,1,0:T(8,128)(2,1)} %get-tuple-element.110.refs_0_.refs_1_.refs_2_, ...), custom_call_target="tpu_custom_call" | custom-call | flops 70000001024 | bytes 1024 | tf_op jit(solution)/shard_map/pallas_call | solution.py:313
  140.2 8.7 %shard_map.242 = (bf16[512,1152]{1,0:T(8,128)(2,1)}, f32[512,1152]{1,0:T(8,128)}, bf16[512,1152]{1,0:T(8,128)(2,1)}, bf16[512,1152]{1,0:T(8,128)(2,1)}, bf16[512,1152]{1,0:T(8,128)(2,1)}, /*index=5*/f32[1,1152]{1,0:T(1,128)}) custom-call(s32[3]{0:T(128)} %pad_add_fusion.place_ref, bf16[576,512]{1,0:T(8,128)(2,1)} %get-tuple-element.104.own_ref.refs_5_.refs_0_, ...), custom_call_target="tpu_custom_call" | custom-call | flops 35000000512 | bytes 1024 | tf_op jit(solution)/shard_map/pallas_call | solution.py:483
  148.9 22.7 %shard_map.243 = (bf16[512,2304]{1,0:T(8,128)(2,1)}, bf16[512,2304]{1,0:T(8,128)(2,1)}, f32[1,2304]{1,0:T(1,128)}, bf16[512,1152]{1,0:T(8,128)(2,1)}, bf16[512,1152]{1,0:T(8,128)(2,1)}) custom-call(s32[3]{0:T(128)} %pad_add_fusion.place_ref, bf16[512,1152]{1,0:T(8,128)(2,1)} %get-tuple-element.127.h_ref.h0_ref, ...), custom_call_target="tpu_custom_call" | custom-call | flops 109999996928 | bytes 1024 | tf_op jit(solution)/shard_map/pallas_call | solution.py:563
  172.8 8.7 %shard_map.245 = (bf16[512,1152]{1,0:T(8,128)(2,1)}, f32[512,1152]{1,0:T(8,128)}, bf16[512,1152]{1,0:T(8,128)(2,1)}, bf16[512,1152]{1,0:T(8,128)(2,1)}, bf16[512,1152]{1,0:T(8,128)(2,1)}, /*index=5*/f32[1,1152]{1,0:T(1,128)}) custom-call(s32[3]{0:T(128)} %pad_add_fusion.place_ref, bf16[576,512]{1,0:T(8,128)(2,1)} %get-tuple-element.113.own_ref.refs_6_.refs_1_, ...), custom_call_target="tpu_custom_call" | custom-call | flops 35000000512 | bytes 1024 | tf_op jit(solution)/shard_map/pallas_call | solution.py:483
  181.6 22.5 %shard_map.246 = (bf16[512,2304]{1,0:T(8,128)(2,1)}, bf16[512,2304]{1,0:T(8,128)(2,1)}, f32[1,2304]{1,0:T(1,128)}, bf16[512,1152]{1,0:T(8,128)(2,1)}, bf16[512,1152]{1,0:T(8,128)(2,1)}) custom-call(s32[3]{0:T(128)} %pad_add_fusion.place_ref, bf16[512,1152]{1,0:T(8,128)(2,1)} %get-tuple-element.114.h_ref.h1_ref, ...), custom_call_target="tpu_custom_call" | custom-call | flops 109999996928 | bytes 1024 | tf_op jit(solution)/shard_map/pallas_call | solution.py:563
  212.3 12.9 %shard_map.250 = (bf16[288,2304]{1,0:T(8,128)(2,1)}, bf16[288,2304]{1,0:T(8,128)(2,1)}, bf16[288,2304]{1,0:T(8,128)(2,1)}, bf16[288,2304]{1,0:T(8,128)(2,1)}) custom-call(s32[3]{0:T(128)} %pad_add_fusion.place_ref, bf16[512,1152]{1,0:T(8,128)(2,1)} %get-tuple-element.127.h_ref.h0_ref, bf16[512,1152]{1,0:T(8,128)(2,1)} %get-tuple-element.114.h_ref.h1_ref, ...), custom_call_target="tpu_custom_call" | custom-call | flops 49999998976 | bytes 1024 | tf_op jit(solution)/shard_map/pallas_call | solution.py:634
  228.2 7.9 %shard_map.248 = bf16[1152,1152]{1,0:T(8,128)(2,1)} custom-call(s32[3]{0:T(128)} %pad_add_fusion.place_ref, bf16[512,2304]{1,0:T(8,128)(2,1)} %get-tuple-element.120.a0_ref, bf16[512,2304]{1,0:T(8,128)(2,1)} %get-tuple-element.119.a1_ref, bf16[512,1152]{1,0:T(8,128)(2,1)} %get-tuple-element.107.g_ref.g0_ref, bf16[512,1152]{1,0:T(8,128)(2,1)} %get-tuple-element.115.g_ref.g1_ref), custom_call_target="tpu_custom_call" | custom-call | flops 24999999488 | bytes 1024 | tf_op jit(solution)/shard_map/pallas_call | solution.py:606
  240.2 8.2 %shard_map.251 = (f32[512,1152]{1,0:T(8,128)}, bf16[512,1152]{1,0:T(8,128)(2,1)}, bf16[8,512,72]{2,1,0:T(8,128)(2,1)}, f32[8,1152]{1,0:T(8,128)}) custom-call(s32[3]{0:T(128)} %pad_add_fusion.place_ref, bf16[512,1152]{1,0:T(8,128)(2,1)} %get-tuple-element.125.own_ref, bf16[512,1152]{1,0:T(8,128)(2,1)} %copy-done.33, ...), custom_call_target="tpu_custom_call" | custom-call | flops 35000000512 | bytes 1024 | tf_op jit(solution)/shard_map/pallas_call | solution.py:750
  250.6 8.2 %shard_map.249 = (f32[512,1152]{1,0:T(8,128)}, bf16[512,1152]{1,0:T(8,128)(2,1)}, bf16[8,512,72]{2,1,0:T(8,128)(2,1)}, f32[8,1152]{1,0:T(8,128)}) custom-call(s32[3]{0:T(128)} %pad_add_fusion.place_ref, bf16[512,1152]{1,0:T(8,128)(2,1)} %get-tuple-element.112.own_ref, bf16[512,1152]{1,0:T(8,128)(2,1)} %collective-permute-done.22.got_ref, ...), custom_call_target="tpu_custom_call" | custom-call | flops 35000000512 | bytes 1024 | tf_op jit(solution)/shard_map/pallas_call | solution.py:750
  258.8 27.2 %shard_map.252 = (bf16[8,1024,72]{2,1,0:T(8,128)(2,1)}, bf16[8,1024,72]{2,1,0:T(8,128)(2,1)}, bf16[8,1024,72]{2,1,0:T(8,128)(2,1)}, f32[8,1920,128]{2,1,0:T(8,128)}) custom-call(s32[3]{0:T(128)} %pad_add_fusion.place_ref, bf16[24,1024,72]{2,1,0:T(8,128)(2,1)} %get-tuple-element.110.refs_0_.refs_1_.refs_2_, ...), custom_call_target="tpu_custom_call" | custom-call | flops 70000001024 | bytes 1024 | tf_op jit(solution)/shard_map/pallas_call | solution.py:409
  287.2 17.9 %shard_map.253 = (bf16[288,4608]{1,0:T(8,128)(2,1)}, bf16[288,4608]{1,0:T(8,128)(2,1)}) custom-call(s32[3]{0:T(128)} %pad_add_fusion.place_ref, bf16[1024,1152]{1,0:T(8,128)(2,1)} %get-tuple-element.144.h_ref, bf16[8,1024,72]{2,1,0:T(8,128)(2,1)} %get-tuple-element.140.gq_ref.refs_0_, bf16[8,1024,72]{2,1,0:T(8,128)(2,1)} %get-tuple-element.142.gk_ref.refs_1_, ...), custom_call_target="tpu_custom_call" | custom-call | flops 44999999488 | bytes 1024 | tf_op jit(solution)/shard_map/pallas_call | solution.py:691
  305.3 10.3 %shard_map.259 = (f32[8,60,128]{2,1,0:T(8,128)}, f32[8,60,128]{2,1,0:T(8,128)}) custom-call(s32[3]{0:T(128)} %pad_add_fusion.place_ref, f32[8,1920,128]{2,1,0:T(8,128)} %get-tuple-element.157.g_ref), custom_call_target="tpu_custom_call" | custom-call | flops 15000000512 | bytes 1024 | tf_op jit(solution)/shard_map/pallas_call | solution.py:174
  323.3 8.3 %shard_map.254 = (bf16[512,1152]{1,0:T(8,128)(2,1)}, f32[8,1152]{1,0:T(8,128)}, f32[1,1728]{1,0:T(1,128)}) custom-call(s32[3]{0:T(128)} %pad_add_fusion.place_ref, bf16[8,1024,72]{2,1,0:T(8,128)(2,1)} %get-tuple-element.140.gq_ref.refs_0_, bf16[8,1024,72]{2,1,0:T(8,128)(2,1)} %get-tuple-element.142.gk_ref.refs_1_, ...), custom_call_target="tpu_custom_call" | custom-call | flops 35000000512 | bytes 1024 | tf_op jit(solution)/shard_map/pallas_call | solution.py:802
  332.6 8.0 %shard_map.255 = (bf16[512,1152]{1,0:T(8,128)(2,1)}, f32[8,1152]{1,0:T(8,128)}, f32[1,1728]{1,0:T(1,128)}) custom-call(s32[3]{0:T(128)} %pad_add_fusion.place_ref, bf16[8,1024,72]{2,1,0:T(8,128)(2,1)} %get-tuple-element.140.gq_ref.refs_0_, bf16[8,1024,72]{2,1,0:T(8,128)(2,1)} %get-tuple-element.142.gk_ref.refs_1_, ...), custom_call_target="tpu_custom_call" | custom-call | flops 35000000512 | bytes 1024 | tf_op jit(solution)/shard_map/pallas_call | solution.py:802
  397.0 11.9 %collective-permute-done.44 = f32[294,128]{1,0:T(8,128)S(1)} collective-permute-done((f32[294,128]{1,0:T(8,128)S(1)}, f32[294,128]{1,0:T(8,128)S(1)}, u32[]{:S(2)}, u32[]{:S(2)}) %collective-permute-start.44) | collective-permute-done | bytes 150560 | tf_op jit(solution)/shard_map/ppermute | solution.py:983
  414.8 13.5 %collective-permute-done.32 = bf16[144,4608]{1,0:T(8,128)(2,1)S(1)} collective-permute-done((bf16[144,4608]{1,0:T(8,128)(2,1)S(1)}, bf16[144,4608]{1,0:T(8,128)(2,1)S(1)}, u32[]{:S(2)}, u32[]{:S(2)}) %collective-permute-start.32) | collective-permute-done | bytes 1327136 | tf_op jit(solution)/shard_map/ppermute | solution.py:983
  436.5 35.1 %collective-permute-done.35 = bf16[36,4608]{1,0:T(8,128)(2,1)S(1)} collective-permute-done((bf16[36,4608]{1,0:T(8,128)(2,1)S(1)}, bf16[36,4608]{1,0:T(8,128)(2,1)S(1)}, u32[]{:S(2)}, u32[]{:S(2)}) %collective-permute-start.35) | collective-permute-done | bytes 331808 | tf_op jit(solution)/shard_map/ppermute | solution.py:983
  471.7 9.7 %collective-permute-done.33 = bf16[36,4608]{1,0:T(8,128)(2,1)S(1)} collective-permute-done((bf16[36,4608]{1,0:T(8,128)(2,1)S(1)}, bf16[36,4608]{1,0:T(8,128)(2,1)S(1)}, u32[]{:S(2)}, u32[]{:S(2)}) %collective-permute-start.33) | collective-permute-done | bytes 331808 | tf_op jit(solution)/shard_map/ppermute | solution.py:983
  496.7 12.0 %collective-permute-done.37 = bf16[36,4608]{1,0:T(8,128)(2,1)S(1)} collective-permute-done((bf16[36,4608]{1,0:T(8,128)(2,1)S(1)}, bf16[36,4608]{1,0:T(8,128)(2,1)S(1)}, u32[]{:S(2)}, u32[]{:S(2)}) %collective-permute-start.37) | collective-permute-done | bytes 331808 | tf_op jit(solution)/shard_map/ppermute | solution.py:983
  508.7 11.2 %collective-permute-done.38 = bf16[36,4608]{1,0:T(8,128)(2,1)S(1)} collective-permute-done((bf16[36,4608]{1,0:T(8,128)(2,1)S(1)}, bf16[36,4608]{1,0:T(8,128)(2,1)S(1)}, u32[]{:S(2)}, u32[]{:S(2)}) %collective-permute-start.38) | collective-permute-done | bytes 331808 | tf_op jit(solution)/shard_map/ppermute | solution.py:983
  539.1 19.7 %collective-permute-done.40 = bf16[144,4608]{1,0:T(8,128)(2,1)S(1)} collective-permute-done((bf16[144,4608]{1,0:T(8,128)(2,1)}, bf16[144,4608]{1,0:T(8,128)(2,1)S(1)}, u32[]{:S(2)}, u32[]{:S(2)}) %collective-permute-start.40) | collective-permute-done | bytes 1327136 | tf_op jit(solution)/shard_map/ppermute | solution.py:983
  (311 shorter events, 229.1 us)
Async XLA Ops:
  7.2 526.5 %all-reduce.12.cloned.1.call-start = ((), (), s32[]{:S(2)}) async-start(), calls=%async_computation | async-start | bytes 10616832 | tf_op jit(solution)/shard_map/psum | solution.py:1269
  33.8 27.7 %collective-permute-start.2 = (bf16[256,1152]{1,0:T(8,128)(2,1)}, bf16[256,1152]{1,0:T(8,128)(2,1)S(1)}, u32[]{:S(2)}, u32[]{:S(2)}) collective-permute-start(bf16[256,1152]{1,0:T(8,128)(2,1)} %get-tuple-element.206), channel_id=1, source_target_pairs={{0,3},{1,2},{2,1},{3,0},{4,7},{5,6},{6,5},{7,4},{8,11},{9,10},{10,... | collective-permute-start | bytes 1769480 | tf_op jit(solution)/shard_map/ppermute | solution.py:932
  34.7 26.9 %collective-permute-start.1 = (bf16[256,1152]{1,0:T(8,128)(2,1)}, bf16[256,1152]{1,0:T(8,128)(2,1)S(1)}, u32[]{:S(2)}, u32[]{:S(2)}) collective-permute-start(bf16[256,1152]{1,0:T(8,128)(2,1)} %get-tuple-element.207.x0_ref), channel_id=1, source_target_pairs={{0,2},{1,3},{2,0},{3,1},{4,6},{5,7},{6,4},{7,5},{8,10},{9,11},{10,... | collective-permute-start | bytes 1769480 | tf_op jit(solution)/shard_map/ppermute | solution.py:932
  41.5 42.2 %collective-permute-start.12 = (bf16[288,1728]{1,0:T(8,128)(2,1)}, bf16[288,1728]{1,0:T(8,128)(2,1)}, u32[]{:S(2)}, u32[]{:S(2)}) collective-permute-start(bf16[288,1728]{1,0:T(8,128)(2,1)} %get-tuple-element.99), channel_id=1, source_target_pairs={{0,2},{1,3},{2,0},{3,1},{4,6},{5,7},{6,4},{7,5},{8,10},{9,11},{10,... | collective-permute-start | bytes 2985992 | tf_op jit(solution)/shard_map/ppermute | solution.py:932
  57.1 27.2 %collective-permute-start.16 = (bf16[144,3456]{1,0:T(8,128)(2,1)S(1)}, bf16[144,3456]{1,0:T(8,128)(2,1)S(1)}, u32[]{:S(2)}, u32[]{:S(2)}) collective-permute-start(bf16[144,3456]{1,0:T(8,128)(2,1)S(1)} %pad_maximum_fusion.5), channel_id=1, source_target_pairs={{0,4},{4,0},{8,12},{12,8},{16,20},{20,16},{24,28},{28,24},{1,5},{5... | collective-permute-start | bytes 2985992 | tf_op jit(solution)/shard_map/ppermute | solution.py:983
  77.2 62.2 %collective-permute-start.19 = (bf16[256,1152]{1,0:T(8,128)(2,1)}, bf16[256,1152]{1,0:T(8,128)(2,1)}, u32[]{:S(2)}, u32[]{:S(2)}) collective-permute-start(bf16[256,1152]{1,0:T(8,128)(2,1)} %get-tuple-element.205), channel_id=1, source_target_pairs={{0,3},{1,2},{2,1},{3,0},{4,7},{5,6},{6,5},{7,4},{8,11},{9,10},{10,... | collective-permute-start | bytes 1769480 | tf_op jit(solution)/shard_map/ppermute | solution.py:932
  77.7 61.6 %collective-permute-start.18 = (bf16[256,1152]{1,0:T(8,128)(2,1)}, bf16[256,1152]{1,0:T(8,128)(2,1)}, u32[]{:S(2)}, u32[]{:S(2)}) collective-permute-start(bf16[256,1152]{1,0:T(8,128)(2,1)} %get-tuple-element.204.c0_ref), channel_id=1, source_target_pairs={{0,2},{1,3},{2,0},{3,1},{4,6},{5,7},{6,4},{7,5},{8,10},{9,11},{10,... | collective-permute-start | bytes 1769480 | tf_op jit(solution)/shard_map/ppermute | solution.py:932
  83.7 39.2 %collective-permute-start.20 = (bf16[1152,1152]{1,0:T(8,128)(2,1)}, bf16[1152,1152]{1,0:T(8,128)(2,1)S(1)}, u32[]{:S(2)}, u32[]{:S(2)}) collective-permute-start(bf16[1152,1152]{1,0:T(8,128)(2,1)} %s0_ref.3), channel_id=1, source_target_pairs={{0,1},{1,0},{2,3},{3,2},{4,5},{5,4},{6,7},{7,6},{8,9},{9,8},{10,11... | collective-permute-start | bytes 7962632 | tf_op jit(solution)/shard_map/ppermute | solution.py:932
  86.2 53.2 %collective-permute-start.17 = (bf16[288,3456]{1,0:T(8,128)(2,1)}, bf16[288,3456]{1,0:T(8,128)(2,1)}, u32[]{:S(2)}, u32[]{:S(2)}) collective-permute-start(bf16[288,3456]{1,0:T(8,128)(2,1)} %pad_maximum_fusion.1.w2_ref.e2_ref), channel_id=1, source_target_pairs={{0,1},{1,0},{2,3},{3,2},{4,5},{5,4},{6,7},{7,6},{8,9},{9,8},{10,11... | collective-permute-start | bytes 5971976 | tf_op jit(solution)/shard_map/ppermute | solution.py:932
  138.5 34.4 %collective-permute-start.21 = (bf16[576,512]{1,0:T(8,128)(2,1)}, bf16[576,512]{1,0:T(8,128)(2,1)}, u32[]{:S(2)}, u32[]{:S(2)}) collective-permute-start(bf16[576,512]{1,0:T(8,128)(2,1)} %get-tuple-element.113.own_ref.refs_6_.refs_1_), channel_id=1, source_target_pairs={{0,2},{1,3},{2,0},{3,1},{4,6},{5,7},{6,4},{7,5},{8,10},{9,11},{10,... | collective-permute-start | bytes 1769480 | tf_op jit(solution)/shard_map/ppermute | solution.py:932
  171.5 56.7 %collective-permute-start.22 = (bf16[512,1152]{1,0:T(8,128)(2,1)}, bf16[512,1152]{1,0:T(8,128)(2,1)}, u32[]{:S(2)}, u32[]{:S(2)}) collective-permute-start(bf16[512,1152]{1,0:T(8,128)(2,1)} %get-tuple-element.112.own_ref), channel_id=1, source_target_pairs={{0,2},{1,3},{2,0},{3,1},{4,6},{5,7},{6,4},{7,5},{8,10},{9,11},{10,... | collective-permute-start | bytes 3538952 | tf_op jit(solution)/shard_map/ppermute | solution.py:932
  204.1 35.1 %collective-permute-start.24 = (bf16[512,1152]{1,0:T(8,128)(2,1)}, bf16[512,1152]{1,0:T(8,128)(2,1)S(1)}, u32[]{:S(2)}, u32[]{:S(2)}) collective-permute-start(bf16[512,1152]{1,0:T(8,128)(2,1)} %get-tuple-element.125.own_ref), channel_id=1, source_target_pairs={{0,2},{1,3},{2,0},{3,1},{4,6},{5,7},{6,4},{7,5},{8,10},{9,11},{10,... | collective-permute-start | bytes 3538952 | tf_op jit(solution)/shard_map/ppermute | solution.py:932
  286.0 55.7 %collective-permute-start.27 = (bf16[512,1152]{1,0:T(8,128)(2,1)}, bf16[512,1152]{1,0:T(8,128)(2,1)}, u32[]{:S(2)}, u32[]{:S(2)}) collective-permute-start(bf16[512,1152]{1,0:T(8,128)(2,1)} %broadcast_select_fusion.2), channel_id=1, source_target_pairs={{0,2},{1,3},{2,0},{3,1},{4,6},{5,7},{6,4},{7,5},{8,10},{9,11},{10,... | collective-permute-start | bytes 3538952 | tf_op jit(solution)/shard_map/ppermute | solution.py:932
  331.6 152.6 %collective-permute-start.30 = (bf16[512,1152]{1,0:T(8,128)(2,1)}, bf16[512,1152]{1,0:T(8,128)(2,1)}, u32[]{:S(2)}, u32[]{:S(2)}) collective-permute-start(bf16[512,1152]{1,0:T(8,128)(2,1)} %get-tuple-element.150), channel_id=1, source_target_pairs={{0,2},{1,3},{2,0},{3,1},{4,6},{5,7},{6,4},{7,5},{8,10},{9,11},{10,... | collective-permute-start | bytes 3538952 | tf_op jit(solution)/shard_map/ppermute | solution.py:932
  375.5 154.6 %collective-permute-start.29 = (bf16[256,1152]{1,0:T(8,128)(2,1)}, bf16[256,1152]{1,0:T(8,128)(2,1)}, u32[]{:S(2)}, u32[]{:S(2)}) collective-permute-start(bf16[256,1152]{1,0:T(8,128)(2,1)} %slice_bitcast_fusion.1), channel_id=1, source_target_pairs={{0,1},{1,0},{2,3},{3,2},{4,5},{5,4},{6,7},{7,6},{8,9},{9,8},{10,11... | collective-permute-start | bytes 1769480 | tf_op jit(solution)/shard_map/ppermute | solution.py:932
  382.5 26.3 %collective-permute-start.44 = (f32[294,128]{1,0:T(8,128)S(1)}, f32[294,128]{1,0:T(8,128)S(1)}, u32[]{:S(2)}, u32[]{:S(2)}) collective-permute-start(f32[294,128]{1,0:T(8,128)S(1)} %add_add_fusion.1), channel_id=1, source_target_pairs={{0,16},{4,20},{8,24},{12,28},{16,0},{20,4},{24,8},{28,12},{1,17},{... | collective-permute-start | bytes 451592 | tf_op jit(solution)/shard_map/ppermute | solution.py:983
  396.4 31.9 %collective-permute-start.32 = (bf16[144,4608]{1,0:T(8,128)(2,1)S(1)}, bf16[144,4608]{1,0:T(8,128)(2,1)S(1)}, u32[]{:S(2)}, u32[]{:S(2)}) collective-permute-start(bf16[144,4608]{1,0:T(8,128)(2,1)S(1)} %copy-done.6), channel_id=1, source_target_pairs={{0,4},{4,0},{8,12},{12,8},{16,20},{20,16},{24,28},{28,24},{1,5},{5... | collective-permute-start | bytes 3981320 | tf_op jit(solution)/shard_map/ppermute | solution.py:983
  430.0 41.7 %collective-permute-start.35 = (bf16[36,4608]{1,0:T(8,128)(2,1)S(1)}, bf16[36,4608]{1,0:T(8,128)(2,1)S(1)}, u32[]{:S(2)}, u32[]{:S(2)}) collective-permute-start(bf16[36,4608]{1,0:T(8,128)(2,1)S(1)} %get-tuple-element.202), channel_id=1, source_target_pairs={{0,24},{4,28},{8,16},{12,20},{16,8},{20,12},{24,0},{28,4},{1,25},{... | collective-permute-start | bytes 995336 | tf_op jit(solution)/shard_map/ppermute | solution.py:983
  430.6 41.1 %collective-permute-start.34 = (bf16[36,4608]{1,0:T(8,128)(2,1)S(1)}, bf16[36,4608]{1,0:T(8,128)(2,1)S(1)}, u32[]{:S(2)}, u32[]{:S(2)}) collective-permute-start(bf16[36,4608]{1,0:T(8,128)(2,1)S(1)} %get-tuple-element.203), channel_id=1, source_target_pairs={{0,8},{4,12},{8,0},{12,4},{16,24},{20,28},{24,16},{28,20},{1,9},{5... | collective-permute-start | bytes 995336 | tf_op jit(solution)/shard_map/ppermute | solution.py:983
  432.0 49.3 %collective-permute-start.33 = (bf16[36,4608]{1,0:T(8,128)(2,1)S(1)}, bf16[36,4608]{1,0:T(8,128)(2,1)S(1)}, u32[]{:S(2)}, u32[]{:S(2)}) collective-permute-start(bf16[36,4608]{1,0:T(8,128)(2,1)S(1)} %get-tuple-element.201), channel_id=1, source_target_pairs={{0,16},{4,20},{8,24},{12,28},{16,0},{20,4},{24,8},{28,12},{1,17},{... | collective-permute-start | bytes 995336 | tf_op jit(solution)/shard_map/ppermute | solution.py:983
  495.0 32.3 %collective-permute-start.39 = (bf16[36,4608]{1,0:T(8,128)(2,1)S(1)}, bf16[36,4608]{1,0:T(8,128)(2,1)S(1)}, u32[]{:S(2)}, u32[]{:S(2)}) collective-permute-start(bf16[36,4608]{1,0:T(8,128)(2,1)S(1)} %dynamic_update_slice.3), channel_id=1, source_target_pairs={{0,24},{4,28},{8,16},{12,20},{16,8},{20,12},{24,0},{28,4},{1,25},{... | collective-permute-start | bytes 995336 | tf_op jit(solution)/shard_map/ppermute | solution.py:983
  496.6 35.8 %collective-permute-start.31 = (bf16[256,1152]{1,0:T(8,128)(2,1)S(1)}, bf16[256,1152]{1,0:T(8,128)(2,1)S(1)}, u32[]{:S(2)}, u32[]{:S(2)}) collective-permute-start(bf16[256,1152]{1,0:T(8,128)(2,1)S(1)} %slice_bitcast_fusion), channel_id=1, source_target_pairs={{0,1},{1,0},{2,3},{3,2},{4,5},{5,4},{6,7},{7,6},{8,9},{9,8},{10,11... | collective-permute-start | bytes 1769480 | tf_op jit(solution)/shard_map/ppermute | solution.py:932
  528.8 30.0 %collective-permute-start.40 = (bf16[144,4608]{1,0:T(8,128)(2,1)}, bf16[144,4608]{1,0:T(8,128)(2,1)S(1)}, u32[]{:S(2)}, u32[]{:S(2)}) collective-permute-start(bf16[144,4608]{1,0:T(8,128)(2,1)} %pad_maximum_fusion.2), channel_id=1, source_target_pairs={{0,4},{4,0},{8,12},{12,8},{16,20},{20,16},{24,28},{28,24},{1,5},{5... | collective-permute-start | bytes 3981320 | tf_op jit(solution)/shard_map/ppermute | solution.py:983
  533.7 33.3 %collective-permute-start.48 = (bf16[288,2304]{1,0:T(8,128)(2,1)}, bf16[288,2304]{1,0:T(8,128)(2,1)S(1)}, u32[]{:S(2)}, u32[]{:S(2)}) collective-permute-start(bf16[288,2304]{1,0:T(8,128)(2,1)} %get-tuple-element.181), channel_id=1, source_target_pairs={{0,2},{1,3},{2,0},{3,1},{4,6},{5,7},{6,4},{7,5},{8,10},{9,11},{10,... | collective-permute-start | bytes 3981320 | tf_op jit(solution)/shard_map/ppermute | solution.py:932
  (72 other events, 772.8 us)
Sparse Core Ops, SparseCore 0:
  250.7 226.7 all-reduce.11

commit v3 on v2

--- a/solution.py
+++ b/solution.py
@@ -1019,6 +1019,10 @@
         self.left = stages()
 
     @staticmethod
+    def steps():
+        return [[bit] for stage in stages() for bit in stage]
+
+    @staticmethod
     def share_of(value):
         rows = value.shape[0] // lax.axis_size("grp")
         at = 0
@@ -1042,7 +1046,8 @@
         self.down = stages()
         self.up = []
 
-    def step(self):
+    def step(self, *others):
+        self.value = after(self.value, *others) if others else self.value
         if self.down:
             stage = self.down.pop(0)
             self.value = scatter_stage(self.value, stage, 0)
@@ -1194,12 +1199,11 @@
     tokens, hidden_one, parts = project(
         place,
         token_pieces,
-        after(mod, feed_mine_got, far.value, table),
+        after(mod, feed_mine_got, table),
         weights_in,
         bias_in,
         head_dim,
     )
-    far.gather()
     cot_mine, cot_other = mine_and_other(after(cotangent, token_pieces[2], token_pieces[3]))
     cot_pieces = (
         cot_mine,
@@ -1209,7 +1213,7 @@
     )
     attended, logs = [None, None], [None, None]
     attended[0], logs[0] = attend(
-        place, after(parts, cot_pieces[1]), table, heads, pair, 0
+        place, after(parts, cot_pieces[1], far.value), table, heads, pair, 0
     )
     far.gather()
     shrink_got = swap_core(after(shrink_weight, cot_pieces[1]))
@@ -1312,6 +1316,7 @@
         place, grad_parts, weights_in, after(tokens, input_total.value), 1
     )
     input_total.step()
+    first_cut = input_total.value
     grad_hidden_got = swap_chip(grad_hidden_far)
     grad_hidden_own, sums_own, bias_own = project_back(
         place, grad_parts, weights_in, after(tokens, grad_hidden_far), 0
@@ -1323,8 +1328,12 @@
         middle,
         cots,
         shrink_bias[None],
-        after(mod, grad_hidden_own),
-    )
+        after(mod, grad_hidden_own, first_cut),
+    )
+    input_total.step()
+    input_total.step()
+    far_got = swap_chip(total_far)
+    input_total.step(total_far)
     grad_tokens = input_back(
         place, grad_hidden_own, grad_hidden_got, tokens, grad_middle, mod
     )
@@ -1335,7 +1344,7 @@
     result = to_blocks(result_half)
     grad_images = to_blocks(grad_tokens)
     total_shrink = total_shrink.astype(F32)
-    total_expand = finish_expand(place, total_own, swap_chip(total_far))
+    total_expand = finish_expand(place, total_own, far_got)
     totals = [input_total.finish()]
     total_input = finish_input(place, totals, 3 * width)
     total_output = totals[0][:, 2 * share_columns :].astype(F32)
@@ -1362,8 +1371,8 @@
     split_rows = -(-split_vector.shape[0] // LANES)
     split_vector_padded = jnp.pad(split_vector, (0, split_rows * LANES - split_vector.shape[0]))
     small = jnp.concatenate([split_vector_padded, both_vector]).reshape(-1, LANES)
-    ends = stages()
-    ends[0] = ends[0] + [0]
+    small = after(small, first_cut)
+    ends = [[0]] + Far.steps()
     for stage in ends:
         small = total_stage(small, stage)
     small_own = small[:split_rows]
@@ -1398,7 +1407,7 @@
     ).astype(LOW)
     rows = image_row.reshape(1, -1, LANES)
     for stage in ends:
-        rows = gather_stage(rows, stage if 0 in stage else stage[::-1])
+        rows = gather_stage(rows, stage)
     rows = rows.reshape(rows.shape[0], -1)
     grads_all, conditions = rows[:, : 6 * width], rows[:, 6 * width :]
     conditions_own = lax.dynamic_slice_in_dim(conditions, block * own_rows, own_rows, 1)

time: 592 us -> 590 us (level)
    ppermute x20 -> x18, waiting for transfers between devices: 157 us -> 165 us  [swap_stage(): got.append(lax.ppermute(values[mask], 'grp', pairs))]
    ppermute x20 -> x18, starting transfers between devices: 26 us -> 27.5 us  [swap_stage(): got.append(lax.ppermute(values[mask], 'grp', pairs))]
  transfers between devices with their start and end apart: 57 -> 53, of which waited for: 24 -> 18; matrix products, arithmetic and copies ran while one was open for 10% -> 10% of each run, Pallas kernels for 44% -> 44%
where the time goes in v3:
time: 590 us; the launch traced here: 581 us
  Pallas kernels  264 us (45%)
  waiting for transfers between devices  184 us (31%)
  starting transfers between devices  48.8 us (8%)
  other arithmetic  32.4 us (5%)
  local copies, waits for them, and re-layouts  29.4 us (5%)
  between operations  15.2 us (3%)
  matrix products  7.51 us (1%)
    ppermute x18, waiting for transfers between devices, swap_stage(): got.append(lax.ppermute(values[mask], 'grp', pairs))  165 us
    pallas_call x2, Pallas kernels, feed(): call(feed_kernel, (steps,), [whole(hidden.shape), whole(grad.shape), stra...  45.2 us
    pallas_call x2, Pallas kernels, attend(): call(functools.partial(attend_kernel, half * (part_count // TILE)), (grou...  31 us
    ppermute x18, starting transfers between devices, swap_stage(): got.append(lax.ppermute(values[mask], 'grp', pairs))  27.5 us
    pallas_call x1, Pallas kernels, attend_back(): call(attend_back_kernel, (steps,), [head_block(0), head_block(1), head_bl...  27.2 us
    ppermute x34, starting transfers between devices, swap_block(): return lax.ppermute(value, 'blk', [(i, i ^ bits) for i in range(4)])  21.3 us
    ppermute x34, waiting for transfers between devices, swap_block(): return lax.ppermute(value, 'blk', [(i, i ^ bits) for i in range(4)])  18.7 us
    pallas_call x1, Pallas kernels, input_grad(): call(input_grad_kernel, (width // chunk,), [pl.BlockSpec((count, chunk),...  17.9 us
  transfers between devices with their start and end apart: 53, of which 18 were waited for; matrix products, arithmetic and copies ran while one was open for 10% of the time, Pallas kernels for 44%

profile of v3, /device:TPU:16, one launch (start us, length us, event | category | flops | bytes accessed | tf_op | source)
XLA Modules:
  0.0 580.9 jit_solution(6044621985045562433)
XLA Ops:
  64.6 8.5 %shard_map.239.refs_3_.refs_9_ = f32[8,1920,128]{2,1,0:T(8,128)} custom-call(s32[3]{0:T(128)} %pad_add_fusion.place_ref, f32[8,60,128]{2,1,0:T(8,128)} %get-tuple-element.256.upper_ref, f32[8,60,128]{2,1,0:T(8,128)} %get-tuple-element.255.lower_ref), custom_call_target="tpu_custom_call" | custom-call | flops 30000001024 | bytes 1024 | tf_op jit(solution)/shard_map/pallas_call | solution.py:145
  92.9 13.3 %shard_map.240 = (bf16[1024,1152]{1,0:T(8,128)(2,1)}, bf16[1024,1152]{1,0:T(8,128)(2,1)}, bf16[24,1024,72]{2,1,0:T(8,128)(2,1)}) custom-call(s32[3]{0:T(128)} %pad_add_fusion.place_ref, bf16[256,1152]{1,0:T(8,128)(2,1)} %get-tuple-element.211.x0_ref, bf16[256,1152]{1,0:T(8,128)(2,1)} %collective-permute-done.x1_ref, bf16[256,1152]{1,0:T(8,128)(2,1)} %copy-done.35, ...), custom_call_target="tpu_custom_call" | custom-call | flops 60000002048 | bytes 1024 | tf_op jit(solution)/shard_map/pallas_call | solution.py:229
  106.2 15.5 %shard_map.241 = (bf16[576,512]{1,0:T(8,128)(2,1)}, f32[4,2,512]{2,1,0:T(2,128)}) custom-call(s32[3]{0:T(128)} %pad_add_fusion.place_ref, bf16[24,1024,72]{2,1,0:T(8,128)(2,1)} %get-tuple-element.112.refs_0_.refs_1_.refs_2_, bf16[24,1024,72]{2,1,0:T(8,128)(2,1)} %get-tuple-element.112.refs_0_.refs_1_.refs_2_, ...), custom_call_target="tpu_custom_call" | custom-call | flops 70000001024 | bytes 1024 | tf_op jit(solution)/shard_map/pallas_call | solution.py:313
  122.9 15.5 %shard_map.244 = (bf16[576,512]{1,0:T(8,128)(2,1)}, f32[4,2,512]{2,1,0:T(2,128)}) custom-call(s32[3]{0:T(128)} %pad_add_fusion.place_ref, bf16[24,1024,72]{2,1,0:T(8,128)(2,1)} %get-tuple-element.112.refs_0_.refs_1_.refs_2_, bf16[24,1024,72]{2,1,0:T(8,128)(2,1)} %get-tuple-element.112.refs_0_.refs_1_.refs_2_, ...), custom_call_target="tpu_custom_call" | custom-call | flops 70000001024 | bytes 1024 | tf_op jit(solution)/shard_map/pallas_call | solution.py:313
  140.1 8.7 %shard_map.242 = (bf16[512,1152]{1,0:T(8,128)(2,1)}, f32[512,1152]{1,0:T(8,128)}, bf16[512,1152]{1,0:T(8,128)(2,1)}, bf16[512,1152]{1,0:T(8,128)(2,1)}, bf16[512,1152]{1,0:T(8,128)(2,1)}, /*index=5*/f32[1,1152]{1,0:T(1,128)}) custom-call(s32[3]{0:T(128)} %pad_add_fusion.place_ref, bf16[576,512]{1,0:T(8,128)(2,1)} %get-tuple-element.106.own_ref.refs_5_.refs_0_, ...), custom_call_target="tpu_custom_call" | custom-call | flops 35000000512 | bytes 1024 | tf_op jit(solution)/shard_map/pallas_call | solution.py:483
  148.8 22.7 %shard_map.243 = (bf16[512,2304]{1,0:T(8,128)(2,1)}, bf16[512,2304]{1,0:T(8,128)(2,1)}, f32[1,2304]{1,0:T(1,128)}, bf16[512,1152]{1,0:T(8,128)(2,1)}, bf16[512,1152]{1,0:T(8,128)(2,1)}) custom-call(s32[3]{0:T(128)} %pad_add_fusion.place_ref, bf16[512,1152]{1,0:T(8,128)(2,1)} %get-tuple-element.129.h_ref.h0_ref, ...), custom_call_target="tpu_custom_call" | custom-call | flops 109999996928 | bytes 1024 | tf_op jit(solution)/shard_map/pallas_call | solution.py:563
  172.8 8.7 %shard_map.245 = (bf16[512,1152]{1,0:T(8,128)(2,1)}, f32[512,1152]{1,0:T(8,128)}, bf16[512,1152]{1,0:T(8,128)(2,1)}, bf16[512,1152]{1,0:T(8,128)(2,1)}, bf16[512,1152]{1,0:T(8,128)(2,1)}, /*index=5*/f32[1,1152]{1,0:T(1,128)}) custom-call(s32[3]{0:T(128)} %pad_add_fusion.place_ref, bf16[576,512]{1,0:T(8,128)(2,1)} %get-tuple-element.115.own_ref.refs_6_.refs_1_, ...), custom_call_target="tpu_custom_call" | custom-call | flops 35000000512 | bytes 1024 | tf_op jit(solution)/shard_map/pallas_call | solution.py:483
  181.5 22.5 %shard_map.246 = (bf16[512,2304]{1,0:T(8,128)(2,1)}, bf16[512,2304]{1,0:T(8,128)(2,1)}, f32[1,2304]{1,0:T(1,128)}, bf16[512,1152]{1,0:T(8,128)(2,1)}, bf16[512,1152]{1,0:T(8,128)(2,1)}) custom-call(s32[3]{0:T(128)} %pad_add_fusion.place_ref, bf16[512,1152]{1,0:T(8,128)(2,1)} %get-tuple-element.116.h_ref.h1_ref, ...), custom_call_target="tpu_custom_call" | custom-call | flops 109999996928 | bytes 1024 | tf_op jit(solution)/shard_map/pallas_call | solution.py:563
  212.3 13.0 %shard_map.250 = (bf16[288,2304]{1,0:T(8,128)(2,1)}, bf16[288,2304]{1,0:T(8,128)(2,1)}, bf16[288,2304]{1,0:T(8,128)(2,1)}, bf16[288,2304]{1,0:T(8,128)(2,1)}) custom-call(s32[3]{0:T(128)} %pad_add_fusion.place_ref, bf16[512,1152]{1,0:T(8,128)(2,1)} %get-tuple-element.129.h_ref.h0_ref, bf16[512,1152]{1,0:T(8,128)(2,1)} %get-tuple-element.116.h_ref.h1_ref, ...), custom_call_target="tpu_custom_call" | custom-call | flops 49999998976 | bytes 1024 | tf_op jit(solution)/shard_map/pallas_call | solution.py:634
  228.3 7.9 %shard_map.248 = bf16[1152,1152]{1,0:T(8,128)(2,1)} custom-call(s32[3]{0:T(128)} %pad_add_fusion.place_ref, bf16[512,2304]{1,0:T(8,128)(2,1)} %get-tuple-element.122.a0_ref, bf16[512,2304]{1,0:T(8,128)(2,1)} %get-tuple-element.121.a1_ref, bf16[512,1152]{1,0:T(8,128)(2,1)} %get-tuple-element.109.g_ref.g0_ref, bf16[512,1152]{1,0:T(8,128)(2,1)} %get-tuple-element.117.g_ref.g1_ref), custom_call_target="tpu_custom_call" | custom-call | flops 24999999488 | bytes 1024 | tf_op jit(solution)/shard_map/pallas_call | solution.py:606
  240.2 8.2 %shard_map.251 = (f32[512,1152]{1,0:T(8,128)}, bf16[512,1152]{1,0:T(8,128)(2,1)}, bf16[8,512,72]{2,1,0:T(8,128)(2,1)}, f32[8,1152]{1,0:T(8,128)}) custom-call(s32[3]{0:T(128)} %pad_add_fusion.place_ref, bf16[512,1152]{1,0:T(8,128)(2,1)} %get-tuple-element.127.own_ref, bf16[512,1152]{1,0:T(8,128)(2,1)} %copy-done.31, ...), custom_call_target="tpu_custom_call" | custom-call | flops 35000000512 | bytes 1024 | tf_op jit(solution)/shard_map/pallas_call | solution.py:750
  250.7 8.2 %shard_map.249 = (f32[512,1152]{1,0:T(8,128)}, bf16[512,1152]{1,0:T(8,128)(2,1)}, bf16[8,512,72]{2,1,0:T(8,128)(2,1)}, f32[8,1152]{1,0:T(8,128)}) custom-call(s32[3]{0:T(128)} %pad_add_fusion.place_ref, bf16[512,1152]{1,0:T(8,128)(2,1)} %get-tuple-element.114.own_ref, bf16[512,1152]{1,0:T(8,128)(2,1)} %collective-permute-done.22.got_ref, ...), custom_call_target="tpu_custom_call" | custom-call | flops 35000000512 | bytes 1024 | tf_op jit(solution)/shard_map/pallas_call | solution.py:750
  258.8 27.2 %shard_map.252 = (bf16[8,1024,72]{2,1,0:T(8,128)(2,1)}, bf16[8,1024,72]{2,1,0:T(8,128)(2,1)}, bf16[8,1024,72]{2,1,0:T(8,128)(2,1)}, f32[8,1920,128]{2,1,0:T(8,128)}) custom-call(s32[3]{0:T(128)} %pad_add_fusion.place_ref, bf16[24,1024,72]{2,1,0:T(8,128)(2,1)} %get-tuple-element.112.refs_0_.refs_1_.refs_2_, ...), custom_call_target="tpu_custom_call" | custom-call | flops 70000001024 | bytes 1024 | tf_op jit(solution)/shard_map/pallas_call | solution.py:409
  287.2 17.9 %shard_map.253 = (bf16[288,4608]{1,0:T(8,128)(2,1)}, bf16[288,4608]{1,0:T(8,128)(2,1)}) custom-call(s32[3]{0:T(128)} %pad_add_fusion.place_ref, bf16[1024,1152]{1,0:T(8,128)(2,1)} %get-tuple-element.146.h_ref, bf16[8,1024,72]{2,1,0:T(8,128)(2,1)} %get-tuple-element.142.gq_ref.refs_0_, bf16[8,1024,72]{2,1,0:T(8,128)(2,1)} %get-tuple-element.144.gk_ref.refs_1_, ...), custom_call_target="tpu_custom_call" | custom-call | flops 44999999488 | bytes 1024 | tf_op jit(solution)/shard_map/pallas_call | solution.py:691
  305.4 10.3 %shard_map.259 = (f32[8,60,128]{2,1,0:T(8,128)}, f32[8,60,128]{2,1,0:T(8,128)}) custom-call(s32[3]{0:T(128)} %pad_add_fusion.place_ref, f32[8,1920,128]{2,1,0:T(8,128)} %get-tuple-element.160.g_ref), custom_call_target="tpu_custom_call" | custom-call | flops 15000000512 | bytes 1024 | tf_op jit(solution)/shard_map/pallas_call | solution.py:174
  323.3 8.3 %shard_map.254 = (bf16[512,1152]{1,0:T(8,128)(2,1)}, f32[8,1152]{1,0:T(8,128)}, f32[1,1728]{1,0:T(1,128)}) custom-call(s32[3]{0:T(128)} %pad_add_fusion.place_ref, bf16[8,1024,72]{2,1,0:T(8,128)(2,1)} %get-tuple-element.142.gq_ref.refs_0_, bf16[8,1024,72]{2,1,0:T(8,128)(2,1)} %get-tuple-element.144.gk_ref.refs_1_, ...), custom_call_target="tpu_custom_call" | custom-call | flops 35000000512 | bytes 1024 | tf_op jit(solution)/shard_map/pallas_call | solution.py:802
  335.3 8.3 %shard_map.255 = (bf16[512,1152]{1,0:T(8,128)(2,1)}, f32[8,1152]{1,0:T(8,128)}, f32[1,1728]{1,0:T(1,128)}) custom-call(s32[3]{0:T(128)} %pad_add_fusion.place_ref, bf16[8,1024,72]{2,1,0:T(8,128)(2,1)} %get-tuple-element.142.gq_ref.refs_0_, bf16[8,1024,72]{2,1,0:T(8,128)(2,1)} %get-tuple-element.144.gk_ref.refs_1_, ...), custom_call_target="tpu_custom_call" | custom-call | flops 35000000512 | bytes 1024 | tf_op jit(solution)/shard_map/pallas_call | solution.py:802
  345.3 29.4 %collective-permute-done.29 = bf16[144,4608]{1,0:T(8,128)(2,1)} collective-permute-done((bf16[144,4608]{1,0:T(8,128)(2,1)}, bf16[144,4608]{1,0:T(8,128)(2,1)}, u32[]{:S(2)}, u32[]{:S(2)}) %collective-permute-start.29) | collective-permute-done | bytes 1327136 | tf_op jit(solution)/shard_map/ppermute | solution.py:983
  416.1 16.6 %collective-permute-done.51 = bf16[8,63,128]{2,1,0:T(8,128)(2,1)S(1)} collective-permute-done((bf16[8,63,128]{2,1,0:T(8,128)(2,1)S(1)}, bf16[8,63,128]{2,1,0:T(8,128)(2,1)S(1)}, u32[]{:S(2)}, u32[]{:S(2)}) %collective-permute-start.51) | collective-permute-done | bytes 129056 | tf_op jit(solution)/shard_map/ppermute | solution.py:983
  439.8 27.6 %collective-permute-done.35 = bf16[36,4608]{1,0:T(8,128)(2,1)S(1)} collective-permute-done((bf16[36,4608]{1,0:T(8,128)(2,1)S(1)}, bf16[36,4608]{1,0:T(8,128)(2,1)S(1)}, u32[]{:S(2)}, u32[]{:S(2)}) %collective-permute-start.35) | collective-permute-done | bytes 331808 | tf_op jit(solution)/shard_map/ppermute | solution.py:983
  467.4 14.6 %collective-permute-done.33 = bf16[36,4608]{1,0:T(8,128)(2,1)S(1)} collective-permute-done((bf16[36,4608]{1,0:T(8,128)(2,1)S(1)}, bf16[36,4608]{1,0:T(8,128)(2,1)S(1)}, u32[]{:S(2)}, u32[]{:S(2)}) %collective-permute-start.33) | collective-permute-done | bytes 331808 | tf_op jit(solution)/shard_map/ppermute | solution.py:983
  507.2 10.4 %collective-permute-done.38 = bf16[36,4608]{1,0:T(8,128)(2,1)S(1)} collective-permute-done((bf16[36,4608]{1,0:T(8,128)(2,1)S(1)}, bf16[36,4608]{1,0:T(8,128)(2,1)S(1)}, u32[]{:S(2)}, u32[]{:S(2)}) %collective-permute-start.38) | collective-permute-done | bytes 331808 | tf_op jit(solution)/shard_map/ppermute | solution.py:983
  517.6 9.5 %collective-permute-done.39 = bf16[36,4608]{1,0:T(8,128)(2,1)S(1)} collective-permute-done((bf16[36,4608]{1,0:T(8,128)(2,1)S(1)}, bf16[36,4608]{1,0:T(8,128)(2,1)S(1)}, u32[]{:S(2)}, u32[]{:S(2)}) %collective-permute-start.39) | collective-permute-done | bytes 331808 | tf_op jit(solution)/shard_map/ppermute | solution.py:983
  537.0 21.7 %collective-permute-done.40 = bf16[144,4608]{1,0:T(8,128)(2,1)S(1)} collective-permute-done((bf16[144,4608]{1,0:T(8,128)(2,1)S(1)}, bf16[144,4608]{1,0:T(8,128)(2,1)S(1)}, u32[]{:S(2)}, u32[]{:S(2)}) %collective-permute-start.40) | collective-permute-done | bytes 1327136 | tf_op jit(solution)/shard_map/ppermute | solution.py:983
  (304 shorter events, 211.2 us)
Async XLA Ops:
  7.2 520.4 %all-reduce.12.cloned.1.call-start = ((), (), s32[]{:S(2)}) async-start(), calls=%async_computation | async-start | bytes 10616832 | tf_op jit(solution)/shard_map/psum | solution.py:1273
  33.7 27.7 %collective-permute-start.2 = (bf16[256,1152]{1,0:T(8,128)(2,1)}, bf16[256,1152]{1,0:T(8,128)(2,1)S(1)}, u32[]{:S(2)}, u32[]{:S(2)}) collective-permute-start(bf16[256,1152]{1,0:T(8,128)(2,1)} %get-tuple-element.210), channel_id=1, source_target_pairs={{0,3},{1,2},{2,1},{3,0},{4,7},{5,6},{6,5},{7,4},{8,11},{9,10},{10,... | collective-permute-start | bytes 1769480 | tf_op jit(solution)/shard_map/ppermute | solution.py:932
  34.5 26.9 %collective-permute-start.1 = (bf16[256,1152]{1,0:T(8,128)(2,1)}, bf16[256,1152]{1,0:T(8,128)(2,1)S(1)}, u32[]{:S(2)}, u32[]{:S(2)}) collective-permute-start(bf16[256,1152]{1,0:T(8,128)(2,1)} %get-tuple-element.211.x0_ref), channel_id=1, source_target_pairs={{0,2},{1,3},{2,0},{3,1},{4,6},{5,7},{6,4},{7,5},{8,10},{9,11},{10,... | collective-permute-start | bytes 1769480 | tf_op jit(solution)/shard_map/ppermute | solution.py:932
  41.4 42.2 %collective-permute-start.8 = (bf16[288,1728]{1,0:T(8,128)(2,1)}, bf16[288,1728]{1,0:T(8,128)(2,1)}, u32[]{:S(2)}, u32[]{:S(2)}) collective-permute-start(bf16[288,1728]{1,0:T(8,128)(2,1)} %get-tuple-element.101), channel_id=1, source_target_pairs={{0,2},{1,3},{2,0},{3,1},{4,6},{5,7},{6,4},{7,5},{8,10},{9,11},{10,... | collective-permute-start | bytes 2985992 | tf_op jit(solution)/shard_map/ppermute | solution.py:932
  57.0 27.2 %collective-permute-start.16 = (bf16[144,3456]{1,0:T(8,128)(2,1)S(1)}, bf16[144,3456]{1,0:T(8,128)(2,1)S(1)}, u32[]{:S(2)}, u32[]{:S(2)}) collective-permute-start(bf16[144,3456]{1,0:T(8,128)(2,1)S(1)} %pad_maximum_fusion.5), channel_id=1, source_target_pairs={{0,4},{4,0},{8,12},{12,8},{16,20},{20,16},{24,28},{28,24},{1,5},{5... | collective-permute-start | bytes 2985992 | tf_op jit(solution)/shard_map/ppermute | solution.py:983
  77.0 62.3 %collective-permute-start.19 = (bf16[256,1152]{1,0:T(8,128)(2,1)}, bf16[256,1152]{1,0:T(8,128)(2,1)}, u32[]{:S(2)}, u32[]{:S(2)}) collective-permute-start(bf16[256,1152]{1,0:T(8,128)(2,1)} %get-tuple-element.209), channel_id=1, source_target_pairs={{0,3},{1,2},{2,1},{3,0},{4,7},{5,6},{6,5},{7,4},{8,11},{9,10},{10,... | collective-permute-start | bytes 1769480 | tf_op jit(solution)/shard_map/ppermute | solution.py:932
  77.6 61.7 %collective-permute-start.18 = (bf16[256,1152]{1,0:T(8,128)(2,1)}, bf16[256,1152]{1,0:T(8,128)(2,1)}, u32[]{:S(2)}, u32[]{:S(2)}) collective-permute-start(bf16[256,1152]{1,0:T(8,128)(2,1)} %get-tuple-element.208.c0_ref), channel_id=1, source_target_pairs={{0,2},{1,3},{2,0},{3,1},{4,6},{5,7},{6,4},{7,5},{8,10},{9,11},{10,... | collective-permute-start | bytes 1769480 | tf_op jit(solution)/shard_map/ppermute | solution.py:932
  83.6 39.3 %collective-permute-start.20 = (bf16[1152,1152]{1,0:T(8,128)(2,1)}, bf16[1152,1152]{1,0:T(8,128)(2,1)S(1)}, u32[]{:S(2)}, u32[]{:S(2)}) collective-permute-start(bf16[1152,1152]{1,0:T(8,128)(2,1)} %s0_ref.3), channel_id=1, source_target_pairs={{0,1},{1,0},{2,3},{3,2},{4,5},{5,4},{6,7},{7,6},{8,9},{9,8},{10,11... | collective-permute-start | bytes 7962632 | tf_op jit(solution)/shard_map/ppermute | solution.py:932
  86.1 53.3 %collective-permute-start.17 = (bf16[288,3456]{1,0:T(8,128)(2,1)}, bf16[288,3456]{1,0:T(8,128)(2,1)}, u32[]{:S(2)}, u32[]{:S(2)}) collective-permute-start(bf16[288,3456]{1,0:T(8,128)(2,1)} %pad_maximum_fusion.1.w2_ref.e2_ref), channel_id=1, source_target_pairs={{0,1},{1,0},{2,3},{3,2},{4,5},{5,4},{6,7},{7,6},{8,9},{9,8},{10,11... | collective-permute-start | bytes 5971976 | tf_op jit(solution)/shard_map/ppermute | solution.py:932
  138.4 34.4 %collective-permute-start.21 = (bf16[576,512]{1,0:T(8,128)(2,1)}, bf16[576,512]{1,0:T(8,128)(2,1)}, u32[]{:S(2)}, u32[]{:S(2)}) collective-permute-start(bf16[576,512]{1,0:T(8,128)(2,1)} %get-tuple-element.115.own_ref.refs_6_.refs_1_), channel_id=1, source_target_pairs={{0,2},{1,3},{2,0},{3,1},{4,6},{5,7},{6,4},{7,5},{8,10},{9,11},{10,... | collective-permute-start | bytes 1769480 | tf_op jit(solution)/shard_map/ppermute | solution.py:932
  171.5 56.8 %collective-permute-start.22 = (bf16[512,1152]{1,0:T(8,128)(2,1)}, bf16[512,1152]{1,0:T(8,128)(2,1)}, u32[]{:S(2)}, u32[]{:S(2)}) collective-permute-start(bf16[512,1152]{1,0:T(8,128)(2,1)} %get-tuple-element.114.own_ref), channel_id=1, source_target_pairs={{0,2},{1,3},{2,0},{3,1},{4,6},{5,7},{6,4},{7,5},{8,10},{9,11},{10,... | collective-permute-start | bytes 3538952 | tf_op jit(solution)/shard_map/ppermute | solution.py:932
  204.1 35.1 %collective-permute-start.24 = (bf16[512,1152]{1,0:T(8,128)(2,1)}, bf16[512,1152]{1,0:T(8,128)(2,1)S(1)}, u32[]{:S(2)}, u32[]{:S(2)}) collective-permute-start(bf16[512,1152]{1,0:T(8,128)(2,1)} %get-tuple-element.127.own_ref), channel_id=1, source_target_pairs={{0,2},{1,3},{2,0},{3,1},{4,6},{5,7},{6,4},{7,5},{8,10},{9,11},{10,... | collective-permute-start | bytes 3538952 | tf_op jit(solution)/shard_map/ppermute | solution.py:932
  286.0 91.4 %collective-permute-start.27 = (bf16[512,1152]{1,0:T(8,128)(2,1)}, bf16[512,1152]{1,0:T(8,128)(2,1)}, u32[]{:S(2)}, u32[]{:S(2)}) collective-permute-start(bf16[512,1152]{1,0:T(8,128)(2,1)} %broadcast_select_fusion.2), channel_id=1, source_target_pairs={{0,2},{1,3},{2,0},{3,1},{4,6},{5,7},{6,4},{7,5},{8,10},{9,11},{10,... | collective-permute-start | bytes 3538952 | tf_op jit(solution)/shard_map/ppermute | solution.py:932
  331.6 57.5 %collective-permute-start.31 = (bf16[512,1152]{1,0:T(8,128)(2,1)}, bf16[512,1152]{1,0:T(8,128)(2,1)}, u32[]{:S(2)}, u32[]{:S(2)}) collective-permute-start(bf16[512,1152]{1,0:T(8,128)(2,1)} %get-tuple-element.152), channel_id=1, source_target_pairs={{0,2},{1,3},{2,0},{3,1},{4,6},{5,7},{6,4},{7,5},{8,10},{9,11},{10,... | collective-permute-start | bytes 3538952 | tf_op jit(solution)/shard_map/ppermute | solution.py:932
  333.8 40.9 %collective-permute-start.29 = (bf16[144,4608]{1,0:T(8,128)(2,1)}, bf16[144,4608]{1,0:T(8,128)(2,1)}, u32[]{:S(2)}, u32[]{:S(2)}) collective-permute-start(bf16[144,4608]{1,0:T(8,128)(2,1)} %constant_dynamic-slice_fusion.4), channel_id=1, source_target_pairs={{0,4},{4,0},{8,12},{12,8},{16,20},{20,16},{24,28},{28,24},{1,5},{5... | collective-permute-start | bytes 3981320 | tf_op jit(solution)/shard_map/ppermute | solution.py:983
  397.9 86.0 %collective-permute-start.32 = (bf16[256,1152]{1,0:T(8,128)(2,1)S(1)}, bf16[256,1152]{1,0:T(8,128)(2,1)S(1)}, u32[]{:S(2)}, u32[]{:S(2)}) collective-permute-start(bf16[256,1152]{1,0:T(8,128)(2,1)S(1)} %slice_bitcast_fusion), channel_id=1, source_target_pairs={{0,1},{1,0},{2,3},{3,2},{4,5},{5,4},{6,7},{7,6},{8,9},{9,8},{10,11... | collective-permute-start | bytes 1769480 | tf_op jit(solution)/shard_map/ppermute | solution.py:932
  412.5 54.9 %collective-permute-start.35 = (bf16[36,4608]{1,0:T(8,128)(2,1)S(1)}, bf16[36,4608]{1,0:T(8,128)(2,1)S(1)}, u32[]{:S(2)}, u32[]{:S(2)}) collective-permute-start(bf16[36,4608]{1,0:T(8,128)(2,1)S(1)} %get-tuple-element.206), channel_id=1, source_target_pairs={{0,24},{4,28},{8,16},{12,20},{16,8},{20,12},{24,0},{28,4},{1,25},{... | collective-permute-start | bytes 995336 | tf_op jit(solution)/shard_map/ppermute | solution.py:983
  412.9 54.5 %collective-permute-start.34 = (bf16[36,4608]{1,0:T(8,128)(2,1)S(1)}, bf16[36,4608]{1,0:T(8,128)(2,1)S(1)}, u32[]{:S(2)}, u32[]{:S(2)}) collective-permute-start(bf16[36,4608]{1,0:T(8,128)(2,1)S(1)} %get-tuple-element.207), channel_id=1, source_target_pairs={{0,8},{4,12},{8,0},{12,4},{16,24},{20,28},{24,16},{28,20},{1,9},{5... | collective-permute-start | bytes 995336 | tf_op jit(solution)/shard_map/ppermute | solution.py:983
  414.1 67.9 %collective-permute-start.33 = (bf16[36,4608]{1,0:T(8,128)(2,1)S(1)}, bf16[36,4608]{1,0:T(8,128)(2,1)S(1)}, u32[]{:S(2)}, u32[]{:S(2)}) collective-permute-start(bf16[36,4608]{1,0:T(8,128)(2,1)S(1)} %get-tuple-element.205), channel_id=1, source_target_pairs={{0,16},{4,20},{8,24},{12,28},{16,0},{20,4},{24,8},{28,12},{1,17},{... | collective-permute-start | bytes 995336 | tf_op jit(solution)/shard_map/ppermute | solution.py:983
  439.7 53.9 %collective-permute-start.30 = (bf16[256,1152]{1,0:T(8,128)(2,1)S(1)}, bf16[256,1152]{1,0:T(8,128)(2,1)S(1)}, u32[]{:S(2)}, u32[]{:S(2)}) collective-permute-start(bf16[256,1152]{1,0:T(8,128)(2,1)S(1)} %slice_bitcast_fusion.1), channel_id=1, source_target_pairs={{0,1},{1,0},{2,3},{3,2},{4,5},{5,4},{6,7},{7,6},{8,9},{9,8},{10,11... | collective-permute-start | bytes 1769480 | tf_op jit(solution)/shard_map/ppermute | solution.py:932
  491.5 26.1 %collective-permute-start.38 = (bf16[36,4608]{1,0:T(8,128)(2,1)S(1)}, bf16[36,4608]{1,0:T(8,128)(2,1)S(1)}, u32[]{:S(2)}, u32[]{:S(2)}) collective-permute-start(bf16[36,4608]{1,0:T(8,128)(2,1)S(1)} %dynamic_update_slice.3), channel_id=1, source_target_pairs={{0,16},{4,20},{8,24},{12,28},{16,0},{20,4},{24,8},{28,12},{1,17},{... | collective-permute-start | bytes 995336 | tf_op jit(solution)/shard_map/ppermute | solution.py:983
  492.7 34.4 %collective-permute-start.39 = (bf16[36,4608]{1,0:T(8,128)(2,1)S(1)}, bf16[36,4608]{1,0:T(8,128)(2,1)S(1)}, u32[]{:S(2)}, u32[]{:S(2)}) collective-permute-start(bf16[36,4608]{1,0:T(8,128)(2,1)S(1)} %dynamic_update_slice.3), channel_id=1, source_target_pairs={{0,24},{4,28},{8,16},{12,20},{16,8},{20,12},{24,0},{28,4},{1,25},{... | collective-permute-start | bytes 995336 | tf_op jit(solution)/shard_map/ppermute | solution.py:983
  527.6 31.1 %collective-permute-start.40 = (bf16[144,4608]{1,0:T(8,128)(2,1)S(1)}, bf16[144,4608]{1,0:T(8,128)(2,1)S(1)}, u32[]{:S(2)}, u32[]{:S(2)}) collective-permute-start(bf16[144,4608]{1,0:T(8,128)(2,1)S(1)} %pad_maximum_fusion.2), channel_id=1, source_target_pairs={{0,4},{4,0},{8,12},{12,8},{16,20},{20,16},{24,28},{28,24},{1,5},{5... | collective-permute-start | bytes 3981320 | tf_op jit(solution)/shard_map/ppermute | solution.py:983
  532.0 34.5 %collective-permute-start.46 = (bf16[288,2304]{1,0:T(8,128)(2,1)}, bf16[288,2304]{1,0:T(8,128)(2,1)S(1)}, u32[]{:S(2)}, u32[]{:S(2)}) collective-permute-start(bf16[288,2304]{1,0:T(8,128)(2,1)} %get-tuple-element.184), channel_id=1, source_target_pairs={{0,2},{1,3},{2,0},{3,1},{4,6},{5,7},{6,4},{7,5},{8,10},{9,11},{10,... | collective-permute-start | bytes 3981320 | tf_op jit(solution)/shard_map/ppermute | solution.py:932
  (66 other events, 738.9 us)
Sparse Core Ops, SparseCore 0:
  250.8 229.4 all-reduce.11
